TPU v7x, 32 devices: a whole 2x2x4 slice. The times are simulated.
32 devices in a mesh: batch: 16 (over z, x, core), blk: 2 (over y).
Axes of the slice: x: 2, y: 2, z: 4, core: 2. Of those that a mesh axis runs over, the one named last changes fastest.
Arguments:
- inputs: bfloat16 [32, 1024, 1024], P('batch', 'blk'), may hold values from -6 to 6
- memory: bfloat16 [32, 1024, 1024], P('batch', 'blk'), may hold values from -6 to 6
- target_ids: int32 [32, 1024], P('batch', 'blk'), may hold values from 0 to 1, as said below
- memory_ids: int32 [32, 1024], P('batch', 'blk'), may hold values from 0 to 1, as said below
- cotangent: bfloat16 [32, 1024, 1024], P('batch', 'blk'), may hold values from -6 to 6
- w_self_qkv: bfloat16 [1024, 3072], P('batch'), may hold values from -0.25 to 0.25
- w_self_out: bfloat16 [1024, 1024], P('batch'), may hold values from -2 to 2
- w_cross_q: bfloat16 [1024, 1024], P('batch'), may hold values from -0.25 to 0.25
- w_cross_kv: bfloat16 [1024, 2048], P('batch'), may hold values from -0.25 to 0.25
- w_cross_out: bfloat16 [1024, 1024], P('batch'), may hold values from -2 to 2
- w_up: bfloat16 [1024, 4096], P('batch'), may hold values from -0.1875 to 0.1875
- w_down: bfloat16 [4096, 1024], P('batch'), may hold values from -0.5 to 0.5
- b_up: bfloat16 [4096], P('batch'), may hold values from -3 to 3
- gains: bfloat16 [3, 1024], P(None, 'batch'), may hold values from 0.25 to 1.75
- shifts: bfloat16 [4, 1024], P(None, 'batch'), may hold values from -3 to 3
Outputs:
- output: bfloat16 [32, 1024, 1024], P('batch', 'blk')
- d_input: float32 [32, 1024, 1024], P('batch', 'blk')
- d_memory: float32 [32, 1024, 1024], P('batch', 'blk')
- d_w_self_qkv: float32 [1024, 3072], P('batch')
- d_w_self_out: float32 [1024, 1024], P('batch')
- d_w_cross_q: float32 [1024, 1024], P('batch')
- d_w_cross_kv: float32 [1024, 2048], P('batch')
- d_w_cross_out: float32 [1024, 1024], P('batch')
- d_w_up: float32 [1024, 4096], P('batch')
- d_w_down: float32 [4096, 1024], P('batch')
- d_b_up: float32 [4096], P('batch')
- d_gains: float32 [3, 1024], P(None, 'batch')
- d_shifts: float32 [4, 1024], P(None, 'batch')
Inputs may be any that keep to these rules, and one draw needn't show every extreme that they name: `target_ids`: two packed documents a row: ids are 0 before a cut and 1 from it on, so each document has one token or more. `memory_ids`: two packed documents a memory row, numbered as those of the target row: 0 before a cut and 1 from it on, each with one token or more.
All inputs are finite; a program needn't handle non-finite values.
Results may differ from a plain program's by a relative error of at most 0.03.
The roundings to bfloat16 on the way count: a program that leaves them out, or rounds other values in their place, can miss the bound.
Values may be sent and summed in bfloat16 or wider, within the bound.
No kernel may reach another device: no remote copies, remote signals or barrier semaphores. Data moves between devices by JAX's collectives and lax.ppermute only.
A program may use at most 312 MiB of HBM per device.

v0:
```python
import jax
import jax.numpy as jnp
from jax import lax
from jax.sharding import PartitionSpec as P

D = 1024
NH = 16
HD = 64
MB_ROWS = 1
MICRO = 2


ALPHA = 300.0**0.25
MASKED = -1e30
EPSILON = 1e-05


def shortened(array):
    return jax.tree.map(lambda a: a.astype(jnp.bfloat16) if a.dtype == jnp.float32 else a, array)


def layer_norm(summed, gain_row, shift_row):
    average = jnp.mean(summed, axis=-1, keepdims=True)
    centred = summed - average
    spread = jnp.mean(centred * centred, axis=-1, keepdims=True)
    return centred * lax.rsqrt(spread + EPSILON) * gain_row + shift_row


def split_heads(array_in):
    return array_in.reshape(array_in.shape[0], array_in.shape[1], NH, HD)


def weight_grad(left_rows, right_rows):
    return jnp.einsum("tk,tn->kn", left_rows, right_rows, preferred_element_type=jnp.float32)


def back_prod(grad_rows, matrix):
    return jnp.einsum("tn,kn->tk", grad_rows, matrix, preferred_element_type=jnp.float32)


def attention_scores(queries, key_rows, allowed):
    scores = jnp.einsum(
        "rqhd,rkhd->rhqk",
        split_heads(queries),
        split_heads(key_rows),
        preferred_element_type=jnp.float32,
    ) * HD ** (-0.5)
    return jnp.where(allowed[:, None], scores, MASKED)


def attention_forward(queries, key_rows, value_rows, allowed):
    scores = attention_scores(queries, key_rows, allowed)
    row_peak = jnp.max(scores, axis=-1, keepdims=True)
    raised = jnp.exp(scores - row_peak)
    row_total = jnp.sum(raised, axis=-1, keepdims=True)
    probabilities = (raised / row_total).astype(jnp.bfloat16)
    attended = jnp.einsum(
        "rhqk,rkhd->rqhd",
        probabilities,
        split_heads(value_rows),
        preferred_element_type=jnp.float32,
    )
    return (attended.reshape(queries.shape).astype(jnp.bfloat16), row_peak, row_total)


def attention_backward(queries, key_rows, value_rows, allowed, row_peak, row_total, d_attended):
    scores = attention_scores(queries, key_rows, allowed)
    probabilities = jnp.exp(scores - row_peak) / row_total
    d_heads = split_heads(d_attended)
    d_values = jnp.einsum(
        "rhqk,rqhd->rkhd",
        probabilities.astype(jnp.bfloat16),
        d_heads,
        preferred_element_type=jnp.float32,
    )
    d_probs = jnp.einsum(
        "rqhd,rkhd->rhqk", d_heads, split_heads(value_rows), preferred_element_type=jnp.float32
    )
    inner_sum = jnp.sum(probabilities * d_probs, axis=-1, keepdims=True)
    d_scores = (probabilities * (d_probs - inner_sum)).astype(jnp.bfloat16)
    d_queries = jnp.einsum(
        "rhqk,rkhd->rqhd", d_scores, split_heads(key_rows), preferred_element_type=jnp.float32
    ) * HD ** (-0.5)
    d_keys = jnp.einsum(
        "rhqk,rqhd->rkhd", d_scores, split_heads(queries), preferred_element_type=jnp.float32
    ) * HD ** (-0.5)
    d_pairs = jnp.concatenate(
        [d_keys.reshape(key_rows.shape), d_values.reshape(value_rows.shape)], axis=2
    )
    return (d_queries.reshape(queries.shape), d_pairs)


def add_terms(running, fresh):
    if running is None:
        return fresh
    return tuple((first_term + second_term for first_term, second_term in zip(running, fresh)))


def per_device(
    inputs,
    memory,
    target_ids,
    memory_ids,
    cotangent,
    w_self_qkv,
    w_self_out,
    w_cross_q,
    w_cross_kv,
    w_cross_out,
    w_up,
    w_down,
    b_up,
    gains,
    shifts,
):
    tokens_here = inputs.shape[1]
    length = tokens_here * lax.axis_size("blk")
    token_count = MB_ROWS * tokens_here
    query_places = lax.axis_index("blk") * tokens_here + jnp.arange(tokens_here, dtype=jnp.int32)
    key_places = jnp.arange(length, dtype=jnp.int32)
    causal = key_places[None, :] <= query_places[:, None]
    outputs, input_grads, memory_grads = ([], [], [])
    attn_total = None
    ffn_total = None
    for micro_step in range(MICRO):
        row_range = slice(micro_step * MB_ROWS, (micro_step + 1) * MB_ROWS)
        qkv_full, out_full, cross_q_full, cross_kv_full, cross_out_full, gain_low, shift_low = (
            lax.all_gather(w_self_qkv, "batch", axis=0, tiled=True),
            lax.all_gather(w_self_out, "batch", axis=0, tiled=True),
            lax.all_gather(w_cross_q, "batch", axis=0, tiled=True),
            lax.all_gather(w_cross_kv, "batch", axis=0, tiled=True),
            lax.all_gather(w_cross_out, "batch", axis=0, tiled=True),
            lax.all_gather(gains, "batch", axis=1, tiled=True),
            lax.all_gather(shifts, "batch", axis=1, tiled=True),
        )
        gain_full = gain_low.astype(jnp.float32)
        shift_full = shift_low.astype(jnp.float32)
        x_flat = inputs[row_range].reshape(token_count, D)
        memory_flat = memory[row_range].reshape(token_count, D)
        seg_rows = target_ids[row_range]
        memory_seg_rows = memory_ids[row_range]
        projected = (
            jnp.dot(x_flat, qkv_full, preferred_element_type=jnp.float32)
            .astype(jnp.bfloat16)
            .reshape(MB_ROWS, tokens_here, 3 * D)
        )
        self_queries = projected[:, :, :D]
        key_pairs, key_segs = (
            lax.all_gather(projected[:, :, D:], "blk", axis=1, tiled=True),
            lax.all_gather(seg_rows, "blk", axis=1, tiled=True),
        )
        self_allowed = (seg_rows[:, :, None] == key_segs[:, None, :]) & causal[None]
        self_mixed, self_peak, self_total = attention_forward(
            self_queries, key_pairs[:, :, :D], key_pairs[:, :, D:], self_allowed
        )
        mixed_flat = self_mixed.reshape(token_count, D)
        first_sum = ALPHA * x_flat.astype(jnp.float32) + jnp.dot(
            mixed_flat, out_full, preferred_element_type=jnp.float32
        )
        first = layer_norm(first_sum, gain_full[0], shift_full[0])
        first_low = first.astype(jnp.bfloat16)
        cross_queries = (
            jnp.dot(first_low, cross_q_full, preferred_element_type=jnp.float32)
            .astype(jnp.bfloat16)
            .reshape(MB_ROWS, tokens_here, D)
        )
        memory_local = (
            jnp.dot(memory_flat, cross_kv_full, preferred_element_type=jnp.float32)
            .astype(jnp.bfloat16)
            .reshape(MB_ROWS, tokens_here, 2 * D)
        )
        memory_pairs, memory_segs = (
            lax.all_gather(memory_local, "blk", axis=1, tiled=True),
            lax.all_gather(memory_seg_rows, "blk", axis=1, tiled=True),
        )
        cross_allowed = seg_rows[:, :, None] == memory_segs[:, None, :]
        cross_mixed, cross_peak, cross_total = attention_forward(
            cross_queries, memory_pairs[:, :, :D], memory_pairs[:, :, D:], cross_allowed
        )
        cross_flat = cross_mixed.reshape(token_count, D)
        second_sum = ALPHA * first + jnp.dot(
            cross_flat, cross_out_full, preferred_element_type=jnp.float32
        )
        second = layer_norm(second_sum, gain_full[1], shift_full[1])
        second_low = second.astype(jnp.bfloat16)
        up_full, down_full, bias_full = (
            lax.all_gather(w_up, "batch", axis=0, tiled=True),
            lax.all_gather(w_down, "batch", axis=0, tiled=True),
            lax.all_gather(b_up, "batch", axis=0, tiled=True),
        )
        hidden_pre = jnp.dot(
            second_low, up_full, preferred_element_type=jnp.float32
        ) + bias_full.astype(jnp.float32)
        hidden_low = jax.nn.gelu(hidden_pre).astype(jnp.bfloat16)
        third_sum = (
            ALPHA * second
            + jnp.dot(hidden_low, down_full, preferred_element_type=jnp.float32)
            + shift_full[3]
        )
        result, third_back = jax.vjp(layer_norm, third_sum, gain_full[2], shift_full[2])
        outputs.append(result.astype(jnp.bfloat16).reshape(MB_ROWS, tokens_here, D))
        cot_flat = cotangent[row_range].reshape(token_count, D).astype(jnp.float32)
        d_third, d_gain_three, d_shift_three = third_back(cot_flat)
        d_branch_three = d_third.astype(jnp.bfloat16)
        grad_down = weight_grad(hidden_low, d_branch_three)
        grad_bias_down = jnp.sum(d_branch_three.astype(jnp.float32), axis=0)
        d_hidden = back_prod(d_branch_three, down_full).astype(jnp.bfloat16)
        gelu_back = jax.vjp(jax.nn.gelu, hidden_pre)[1]
        d_pre = gelu_back(d_hidden.astype(jnp.float32))[0].astype(jnp.bfloat16)
        grad_up = weight_grad(second_low, d_pre)
        grad_bias_up = jnp.sum(d_pre.astype(jnp.float32), axis=0)
        d_second = ALPHA * d_third + back_prod(d_pre, up_full)
        ffn_terms = (grad_up, grad_down, grad_bias_up)
        ffn_share = (
            lax.psum_scatter(
                ffn_terms[0].astype(jnp.bfloat16), "batch", scatter_dimension=0, tiled=True
            ).astype(jnp.float32),
            lax.psum_scatter(
                ffn_terms[1].astype(jnp.bfloat16), "batch", scatter_dimension=0, tiled=True
            ).astype(jnp.float32),
            lax.psum_scatter(
                ffn_terms[2].astype(jnp.bfloat16), "batch", scatter_dimension=0, tiled=True
            ).astype(jnp.float32),
        )
        ffn_total = add_terms(ffn_total, ffn_share)
        second_back = jax.vjp(layer_norm, second_sum, gain_full[1], shift_full[1])[1]
        d_second_sum, d_gain_two, d_shift_two = second_back(d_second)
        d_branch_two = d_second_sum.astype(jnp.bfloat16)
        grad_cross_out = weight_grad(cross_flat, d_branch_two)
        d_cross = (
            back_prod(d_branch_two, cross_out_full)
            .astype(jnp.bfloat16)
            .reshape(MB_ROWS, tokens_here, D)
        )
        d_cross_queries, d_memory_all = attention_backward(
            cross_queries,
            memory_pairs[:, :, :D],
            memory_pairs[:, :, D:],
            cross_allowed,
            cross_peak,
            cross_total,
            d_cross,
        )
        d_memory_pairs = lax.psum_scatter(
            d_memory_all.astype(jnp.bfloat16), "blk", scatter_dimension=1, tiled=True
        ).reshape(token_count, 2 * D)
        grad_cross_kv = weight_grad(memory_flat, d_memory_pairs)
        memory_grads.append(
            back_prod(d_memory_pairs, cross_kv_full).reshape(MB_ROWS, tokens_here, D)
        )
        d_cross_low = d_cross_queries.astype(jnp.bfloat16).reshape(token_count, D)
        grad_cross_q = weight_grad(first_low, d_cross_low)
        d_first = ALPHA * d_second_sum + back_prod(d_cross_low, cross_q_full)
        first_back = jax.vjp(layer_norm, first_sum, gain_full[0], shift_full[0])[1]
        d_first_sum, d_gain_one, d_shift_one = first_back(d_first)
        d_branch_one = d_first_sum.astype(jnp.bfloat16)
        grad_self_out = weight_grad(mixed_flat, d_branch_one)
        d_self = (
            back_prod(d_branch_one, out_full).astype(jnp.bfloat16).reshape(MB_ROWS, tokens_here, D)
        )
        d_self_queries, d_key_all = attention_backward(
            self_queries,
            key_pairs[:, :, :D],
            key_pairs[:, :, D:],
            self_allowed,
            self_peak,
            self_total,
            d_self,
        )
        d_self_pairs = lax.psum_scatter(
            d_key_all.astype(jnp.bfloat16), "blk", scatter_dimension=1, tiled=True
        )
        d_projected = jnp.concatenate(
            [d_self_queries.astype(jnp.bfloat16), d_self_pairs], axis=2
        ).reshape(token_count, 3 * D)
        grad_self_qkv = weight_grad(x_flat, d_projected)
        input_grads.append(
            (ALPHA * d_first_sum + back_prod(d_projected, qkv_full)).reshape(
                MB_ROWS, tokens_here, D
            )
        )
        grad_gains = jnp.stack([d_gain_one, d_gain_two, d_gain_three])
        grad_shifts = jnp.stack([d_shift_one, d_shift_two, d_shift_three, grad_bias_down])
        attn_terms = (
            grad_self_qkv,
            grad_self_out,
            grad_cross_q,
            grad_cross_kv,
            grad_cross_out,
            grad_gains,
            grad_shifts,
        )
        attn_share = (
            lax.psum_scatter(
                attn_terms[0].astype(jnp.bfloat16), "batch", scatter_dimension=0, tiled=True
            ).astype(jnp.float32),
            lax.psum_scatter(
                attn_terms[1].astype(jnp.bfloat16), "batch", scatter_dimension=0, tiled=True
            ).astype(jnp.float32),
            lax.psum_scatter(
                attn_terms[2].astype(jnp.bfloat16), "batch", scatter_dimension=0, tiled=True
            ).astype(jnp.float32),
            lax.psum_scatter(
                attn_terms[3].astype(jnp.bfloat16), "batch", scatter_dimension=0, tiled=True
            ).astype(jnp.float32),
            lax.psum_scatter(
                attn_terms[4].astype(jnp.bfloat16), "batch", scatter_dimension=0, tiled=True
            ).astype(jnp.float32),
            lax.psum_scatter(
                attn_terms[5].astype(jnp.bfloat16), "batch", scatter_dimension=1, tiled=True
            ).astype(jnp.float32),
            lax.psum_scatter(
                attn_terms[6].astype(jnp.bfloat16), "batch", scatter_dimension=1, tiled=True
            ).astype(jnp.float32),
        )
        attn_total = add_terms(attn_total, attn_share)
    grad_parts = tuple(attn_total) + tuple(ffn_total)
    totals = jax.tree.map(
        lambda part: part.astype(jnp.float32), lax.psum(shortened(grad_parts), "blk")
    )
    output = jnp.concatenate(outputs, axis=0)
    d_input = jnp.concatenate(input_grads, axis=0)
    d_memory = jnp.concatenate(memory_grads, axis=0)
    return (
        output,
        d_input,
        d_memory,
        totals[0],
        totals[1],
        totals[2],
        totals[3],
        totals[4],
        totals[7],
        totals[8],
        totals[9],
        totals[5],
        totals[6],
    )


def solution(mesh):
    return jax.shard_map(
        per_device,
        mesh=mesh,
        in_specs=(
            P("batch", "blk", None),
            P("batch", "blk", None),
            P("batch", "blk"),
            P("batch", "blk"),
            P("batch", "blk", None),
            P("batch", None),
            P("batch", None),
            P("batch", None),
            P("batch", None),
            P("batch", None),
            P("batch", None),
            P("batch", None),
            P("batch"),
            P(None, "batch"),
            P(None, "batch"),
        ),
        out_specs=(
            P("batch", "blk", None),
            P("batch", "blk", None),
            P("batch", "blk", None),
            P("batch", None),
            P("batch", None),
            P("batch", None),
            P("batch", None),
            P("batch", None),
            P("batch", None),
            P("batch", None),
            P("batch"),
            P(None, "batch"),
            P(None, "batch"),
        ),
        check_vma=False,
    )
```

profile of v0, /device:TPU:0, one launch (start us, length us, event | category | flops | bytes accessed | tf_op | source)
XLA Modules:
  0.0 2725.7 jit_solution(186252383514323777)
XLA Ops:
  8.7 54.8 %all-gather.23.cloned.1.call-done = bf16[1024,2048]{1,0:T(8,128)(2,1)} async-done(((bf16[64,2048]{1,0:T(8,128)(2,1)}), bf16[1024,2048]{1,0:T(8,128)(2,1)}) %all-gather.23.cloned.1.call-update) | async-done | bytes 4194320 | tf_op jit(solution)/shard_map/all_gather | solution.py:131
  77.5 48.6 %all-gather.17.cloned.1.call-done = bf16[1024,3072]{1,0:T(8,128)(2,1)} async-done(((bf16[64,3072]{1,0:T(8,128)(2,1)}), bf16[1024,3072]{1,0:T(8,128)(2,1)}) %all-gather.17.cloned.1.call-update) | async-done | bytes 6291472 | tf_op jit(solution)/shard_map/all_gather | solution.py:128
  166.4 18.8 all-gather.4
  185.3 17.4 all-gather.2
  203.4 19.3 all-gather.3
  252.5 47.7 %all-gather.33.cloned.1.call-done = bf16[1,1024,2048]{2,1,0:T(8,128)(2,1)} async-done(((bf16[1,512,2048]{2,1,0:T(8,128)(2,1)}), bf16[1,1024,2048]{2,1,0:T(8,128)(2,1)}) %all-gather.33.cloned.1.call-update) | async-done | bytes 4194320 | tf_op jit(solution)/shard_map/all_gather | solution.py:149
  310.7 47.7 %all-gather.19.cloned.1.call-done = bf16[1,1024,2048]{2,1,0:T(8,128)(2,1)} async-done(((bf16[1,512,2048]{2,1,0:T(8,128)(2,1)}), bf16[1,1024,2048]{2,1,0:T(8,128)(2,1)}) %all-gather.19.cloned.1.call-update) | async-done | bytes 4194320 | tf_op jit(solution)/shard_map/all_gather | solution.py:149
  370.5 16.7 fusion.185
  387.2 14.3 fusion.98
  405.6 38.7 %all-gather.25.cloned.1.call-done = bf16[1024,1024]{1,0:T(8,128)(2,1)} async-done(((bf16[64,1024]{1,0:T(8,128)(2,1)}), bf16[1024,1024]{1,0:T(8,128)(2,1)}) %all-gather.25.cloned.1.call-update) | async-done | bytes 2097168 | tf_op jit(solution)/shard_map/all_gather | solution.py:130
  449.7 19.3 fusion.187
  469.0 14.6 fusion.101
  492.1 70.3 %all-gather.29.cloned.1.call-done = bf16[1024,4096]{1,0:T(8,128)(2,1)} async-done(((bf16[64,4096]{1,0:T(8,128)(2,1)}), bf16[1024,4096]{1,0:T(8,128)(2,1)}) %all-gather.29.cloned.1.call-update) | async-done | bytes 8388624 | tf_op jit(solution)/shard_map/all_gather | solution.py:187
  574.5 63.3 %all-gather.31.cloned.1.call-done = bf16[4096,1024]{1,0:T(8,128)(2,1)} async-done(((bf16[256,1024]{1,0:T(8,128)(2,1)}), bf16[4096,1024]{1,0:T(8,128)(2,1)}) %all-gather.31.cloned.1.call-update) | async-done | bytes 8388624 | tf_op jit(solution)/shard_map/all_gather | solution.py:188
  650.9 17.0 fusion.180
  667.9 14.0 fusion.104
  691.7 19.2 fusion.182
  710.8 14.0 fusion.107
  757.3 16.4 fusion.190
  773.7 16.7 fusion.191
  814.4 14.1 fusion.79
  828.5 21.5 multiply_reduce_fusion.3
  850.0 27.7 %multiply_convert_fusion.3 = bf16[16,512,1024]{2,1,0:T(8,128)(2,1)} fusion(f32[16,512,1024]{2,1,0:T(8,128)} %get-tuple-element.173, f32[16,512]{1,0:T(8,128)S(1)} %get-tuple-element.172, f32[16,512,1024]{2,1,0:T(8,128)} %get-tuple-element.166, f32[16,512]{1,0:T(8,128)S(1)} %copy-done.73), kind=kLoop, calls=%fused_computation.10 | loop fusion | flops 33554432 | bytes 83951616 | tf_op jit(solution)/shard_map/convert_element_type | solution.py:80
  902.1 14.1 fusion.85
  916.3 21.6 multiply_reduce_fusion.1
  937.8 28.2 %multiply_convert_fusion.1 = bf16[16,512,1024]{2,1,0:T(8,128)(2,1)} fusion(f32[16,512,1024]{2,1,0:T(8,128)} %get-tuple-element.175, f32[16,512]{1,0:T(8,128)S(1)} %get-tuple-element.174, f32[16,512,1024]{2,1,0:T(8,128)} %get-tuple-element.156, f32[16,512]{1,0:T(8,128)S(1)} %copy-done.75), kind=kLoop, calls=%fused_computation.6 | loop fusion | flops 33554432 | bytes 83951616 | tf_op jit(solution)/shard_map/convert_element_type | solution.py:80
  1019.1 22.6 multiply_reduce_fusion.2
  1041.7 27.6 %multiply_convert_fusion.2 = bf16[16,512,1024]{2,1,0:T(8,128)(2,1)} fusion(f32[16,512,1024]{2,1,0:T(8,128)} %get-tuple-element.180, f32[16,512]{1,0:T(8,128)S(1)} %get-tuple-element.179, f32[16,512,1024]{2,1,0:T(8,128)} %get-tuple-element.162, f32[16,512]{1,0:T(8,128)S(1)} %copy-done.69), kind=kLoop, calls=%fused_computation.8 | loop fusion | flops 33554432 | bytes 83951616 | tf_op jit(solution)/shard_map/convert_element_type | solution.py:80
  1079.4 14.9 fusion.76
  1098.4 22.7 multiply_reduce_fusion
  1121.2 28.1 %multiply_convert_fusion = bf16[16,512,1024]{2,1,0:T(8,128)(2,1)} fusion(f32[16,512,1024]{2,1,0:T(8,128)} %get-tuple-element.178, f32[16,512]{1,0:T(8,128)S(1)} %get-tuple-element.177, f32[16,512,1024]{2,1,0:T(8,128)} %get-tuple-element.152, f32[16,512]{1,0:T(8,128)S(1)} %copy-done.71), kind=kLoop, calls=%fused_computation.4 | loop fusion | flops 33554432 | bytes 83951616 | tf_op jit(solution)/shard_map/convert_element_type | solution.py:80
  1348.1 58.5 %all-reduce.2 = (bf16[4096]{0:T(1024)(128)(2,1)S(1)}, bf16[4096]{0:T(1024)(128)(2,1)S(1)}) all-reduce(bf16[4096]{0:T(1024)(128)(2,1)S(1)} %copy-done.118, bf16[4096]{0:T(1024)(128)(2,1)S(1)} %copy-done.119), channel_id=23, replica_groups=mesh['batch'=16,'blk'=2] {'batch'}, use_global_device_ids=true, to_apply=%region_64.65.clone | all-reduce | flops 8192 | bytes 32768
  1420.5 57.6 %reduce-scatter.79.cloned.1.call-done = bf16[64,4]{1,0:T(8,128)(2,1)} async-done(((bf16[1024,4]{1,0:T(8,128)(2,1)}), bf16[64,4]{1,0:T(8,128)(2,1)}) %reduce-scatter.79.cloned.1.call-update) | async-done | bytes 528
  1485.8 56.6 %reduce-scatter.57.cloned.1.call-done = bf16[64,1024]{1,0:T(8,128)(2,1)} async-done(((bf16[1024,1024]{1,0:T(8,128)(2,1)}), bf16[64,1024]{1,0:T(8,128)(2,1)}) %reduce-scatter.57.cloned.1.call-update) | async-done | bytes 131088 | tf_op jit(solution)/shard_map/reduce_scatter | solution.py:306
  1542.4 64.9 %reduce-scatter.55.cloned.1.call-done = bf16[64,1024]{1,0:T(8,128)(2,1)} async-done(((bf16[1024,1024]{1,0:T(8,128)(2,1)}), bf16[64,1024]{1,0:T(8,128)(2,1)}) %reduce-scatter.55.cloned.1.call-update) | async-done | bytes 131088 | tf_op jit(solution)/shard_map/reduce_scatter | solution.py:306
  1608.9 62.6 %reduce-scatter.51.cloned.1.call-done = bf16[64,1024]{1,0:T(8,128)(2,1)} async-done(((bf16[1024,1024]{1,0:T(8,128)(2,1)}), bf16[64,1024]{1,0:T(8,128)(2,1)}) %reduce-scatter.51.cloned.1.call-update) | async-done | bytes 131088 | tf_op jit(solution)/shard_map/reduce_scatter | solution.py:300
  1671.5 64.8 %reduce-scatter.53.cloned.1.call-done = bf16[64,1024]{1,0:T(8,128)(2,1)} async-done(((bf16[1024,1024]{1,0:T(8,128)(2,1)}), bf16[64,1024]{1,0:T(8,128)(2,1)}) %reduce-scatter.53.cloned.1.call-update) | async-done | bytes 131088 | tf_op jit(solution)/shard_map/reduce_scatter | solution.py:300
  1738.0 62.6 %reduce-scatter.49.cloned.1.call-done = bf16[64,1024]{1,0:T(8,128)(2,1)} async-done(((bf16[1024,1024]{1,0:T(8,128)(2,1)}), bf16[64,1024]{1,0:T(8,128)(2,1)}) %reduce-scatter.49.cloned.1.call-update) | async-done | bytes 131088 | tf_op jit(solution)/shard_map/reduce_scatter | solution.py:297
  1800.6 64.8 %reduce-scatter.47.cloned.1.call-done = bf16[64,1024]{1,0:T(8,128)(2,1)} async-done(((bf16[1024,1024]{1,0:T(8,128)(2,1)}), bf16[64,1024]{1,0:T(8,128)(2,1)}) %reduce-scatter.47.cloned.1.call-update) | async-done | bytes 131088 | tf_op jit(solution)/shard_map/reduce_scatter | solution.py:297
  1877.1 95.8 %reduce-scatter.65.cloned.1.call-done = bf16[256,1024]{1,0:T(8,128)(2,1)} async-done(((bf16[4096,1024]{1,0:T(8,128)(2,1)}), bf16[256,1024]{1,0:T(8,128)(2,1)}) %reduce-scatter.65.cloned.1.call-update) | async-done | bytes 524304 | tf_op jit(solution)/shard_map/reduce_scatter | solution.py:218
  1972.9 108.3 %reduce-scatter.63.cloned.1.call-done = bf16[256,1024]{1,0:T(8,128)(2,1)} async-done(((bf16[4096,1024]{1,0:T(8,128)(2,1)}), bf16[256,1024]{1,0:T(8,128)(2,1)}) %reduce-scatter.63.cloned.1.call-update) | async-done | bytes 524304 | tf_op jit(solution)/shard_map/reduce_scatter | solution.py:218
  2083.4 106.2 %reduce-scatter.61.cloned.1.call-done = bf16[64,4096]{1,0:T(8,128)(2,1)} async-done(((bf16[1024,4096]{1,0:T(8,128)(2,1)}), bf16[64,4096]{1,0:T(8,128)(2,1)}) %reduce-scatter.61.cloned.1.call-update) | async-done | bytes 524304 | tf_op jit(solution)/shard_map/reduce_scatter | solution.py:215
  2189.6 108.5 %reduce-scatter.59.cloned.1.call-done = bf16[64,4096]{1,0:T(8,128)(2,1)} async-done(((bf16[1024,4096]{1,0:T(8,128)(2,1)}), bf16[64,4096]{1,0:T(8,128)(2,1)}) %reduce-scatter.59.cloned.1.call-update) | async-done | bytes 524304 | tf_op jit(solution)/shard_map/reduce_scatter | solution.py:215
  2300.2 74.1 %reduce-scatter.71.cloned.1.call-done = bf16[64,2048]{1,0:T(8,128)(2,1)} async-done(((bf16[1024,2048]{1,0:T(8,128)(2,1)}), bf16[64,2048]{1,0:T(8,128)(2,1)}) %reduce-scatter.71.cloned.1.call-update) | async-done | bytes 262160
  2375.5 75.3 %reduce-scatter.73.cloned.1.call-done = bf16[64,2048]{1,0:T(8,128)(2,1)} async-done(((bf16[1024,2048]{1,0:T(8,128)(2,1)}), bf16[64,2048]{1,0:T(8,128)(2,1)}) %reduce-scatter.73.cloned.1.call-update) | async-done | bytes 262160
  2453.0 86.1 %reduce-scatter.67.cloned.1.call-done = bf16[64,3072]{1,0:T(8,128)(2,1)} async-done(((bf16[1024,3072]{1,0:T(8,128)(2,1)}), bf16[64,3072]{1,0:T(8,128)(2,1)}) %reduce-scatter.67.cloned.1.call-update) | async-done | bytes 393232
  2540.5 87.4 %reduce-scatter.69.cloned.1.call-done = bf16[64,3072]{1,0:T(8,128)(2,1)} async-done(((bf16[1024,3072]{1,0:T(8,128)(2,1)}), bf16[64,3072]{1,0:T(8,128)(2,1)}) %reduce-scatter.69.cloned.1.call-update) | async-done | bytes 393232
  2646.5 62.6 %all-reduce.7.cloned.1.call-done = (bf16[64,3072]{0,1:T(8,128)(2,1)}, bf16[64,2048]{0,1:T(8,128)(2,1)}, bf16[64,1024]{1,0:T(8,128)(2,1)}, bf16[64,1024]{1,0:T(8,...) async-done(((bf16[64,3072]{0,1:T(8,128)(2,1)}, bf16[64,2048]{0,1:T(8,128)(2,1)}, bf16[64,1024]{1,0:T(8,128)(2,1)}, ...) | async-done | bytes 2097168 | tf_op jit(solution)/shard_map/psum | solution.py:319
  (594 shorter events, 580.2 us)
Async XLA Ops:
  7.2 56.3 %all-gather.23.cloned.1.call-start = ((), (), s32[]{:S(2)}) async-start(), calls=%async_computation.25 | async-start | bytes 4456448 | tf_op jit(solution)/shard_map/all_gather | solution.py:131
  7.9 118.2 %all-gather.17.cloned.1.call-start = ((), (), s32[]{:S(2)}) async-start(), calls=%async_computation.22 | async-start | bytes 6684672 | tf_op jit(solution)/shard_map/all_gather | solution.py:128
  8.7 220.4 %all-gather.37.cloned.1.call-start = ((), (), s32[]{:S(2)}) async-start(), calls=%async_computation.46 | async-start | bytes 6291456 | tf_op jit(solution)/shard_map/all_gather | solution.py:173
  69.7 172.3 %all-gather.35.cloned.1.call-start = ((), (), s32[]{:S(2)}) async-start(), calls=%async_computation.45 | async-start | bytes 6291456 | tf_op jit(solution)/shard_map/all_gather | solution.py:173
  77.5 222.7 %all-gather.33.cloned.1.call-start = ((), (), s32[]{:S(2)}) async-start(), calls=%async_computation.30 | async-start | bytes 6291456 | tf_op jit(solution)/shard_map/all_gather | solution.py:149
  132.7 93.3 %copy-start.32 = (bf16[1,512,3072]{2,1,0:T(8,128)(2,1)}, bf16[1,512,3072]{2,1,0:T(8,128)(2,1)S(1)}, u32[]{:S(2)}) copy-start(bf16[1,512,3072]{2,1,0:T(8,128)(2,1)S(1)} %fusion.57) | copy-start | bytes 9437188
  134.3 224.0 %all-gather.19.cloned.1.call-start = ((), (), s32[]{:S(2)}) async-start(), calls=%async_computation.23 | async-start | bytes 6291456 | tf_op jit(solution)/shard_map/all_gather | solution.py:149
  145.3 256.6 %all-gather.21.cloned.1.call-start = ((), (), s32[]{:S(2)}) async-start(), calls=%async_computation.24 | async-start | bytes 2228224 | tf_op jit(solution)/shard_map/all_gather | solution.py:129
  146.1 298.2 %all-gather.25.cloned.1.call-start = ((), (), s32[]{:S(2)}) async-start(), calls=%async_computation.26 | async-start | bytes 2228224 | tf_op jit(solution)/shard_map/all_gather | solution.py:130
  146.8 339.9 %all-gather.27.cloned.1.call-start = ((), (), s32[]{:S(2)}) async-start(), calls=%async_computation.27 | async-start | bytes 2228224 | tf_op jit(solution)/shard_map/all_gather | solution.py:132
  147.6 414.8 %all-gather.29.cloned.1.call-start = ((), (), s32[]{:S(2)}) async-start(), calls=%async_computation.28 | async-start | bytes 8912896 | tf_op jit(solution)/shard_map/all_gather | solution.py:187
  148.2 489.6 %all-gather.31.cloned.1.call-start = ((), (), s32[]{:S(2)}) async-start(), calls=%async_computation.29 | async-start | bytes 8912896 | tf_op jit(solution)/shard_map/all_gather | solution.py:188
  148.9 1111.2 %reduce-scatter.43.cloned.1.call-start = ((), (), s32[]{:S(2)}) async-start(), calls=%async_computation.33 | async-start | bytes 6291456 | tf_op jit(solution)/shard_map/reduce_scatter | solution.py:244
  185.3 588.4 %copy-start.101 = (f32[16,1,256]{2,1,0:T(1,128)}, f32[16,1,256]{2,1,0:T(1,128)S(1)}, u32[]{:S(2)}) copy-start(f32[16,1,256]{2,1,0:T(1,128)S(1)} %convert_element_type.651) | copy-start | bytes 49156
  203.4 521.4 %copy-start.97 = (f32[1,1024]{1,0:T(1,128)}, f32[1,1024]{1,0:T(1,128)S(1)}, u32[]{:S(2)}) copy-start(f32[1,1024]{1,0:T(1,128)S(1)} %get-tuple-element.128) | copy-start | bytes 12292
  203.4 604.9 %copy-start.95 = (f32[1,1024]{1,0:T(1,128)}, f32[1,1024]{1,0:T(1,128)S(1)}, u32[]{:S(2)}) copy-start(f32[1,1024]{1,0:T(1,128)S(1)} %get-tuple-element.127) | copy-start | bytes 12292
  223.4 501.4 %copy-start.124 = (f32[1,1024]{1,0:T(1,128)}, f32[1,1024]{1,0:T(1,128)S(1)}, u32[]{:S(2)}) copy-start(f32[1,1024]{1,0:T(1,128)S(1)} %get-tuple-element.132) | copy-start | bytes 12292
  223.4 516.1 %copy-start.122 = (f32[1,1024]{1,0:T(1,128)}, f32[1,1024]{1,0:T(1,128)S(1)}, u32[]{:S(2)}) copy-start(f32[1,1024]{1,0:T(1,128)S(1)} %get-tuple-element.131) | copy-start | bytes 12292
  229.0 141.5 %copy-start.26 = (bf16[1,512,1024]{1,2,0:T(8,128)(2,1)}, bf16[1,512,1024]{1,2,0:T(8,128)(2,1)S(1)}, u32[]{:S(2)}) copy-start(bf16[1,512,1024]{1,2,0:T(8,128)(2,1)S(1)} %copy.103) | copy-start | bytes 3145732
  405.2 81.5 %copy-start = (f32[512,1024]{1,0:T(8,128)}, f32[512,1024]{1,0:T(8,128)S(1)}, u32[]{:S(2)}) copy-start(f32[512,1024]{1,0:T(8,128)S(1)} %get-tuple-element.164) | copy-start | bytes 6291460
  405.2 81.5 %copy-start.81 = (f32[512]{0:T(512)}, f32[512]{0:T(512)S(1)}, u32[]{:S(2)}) copy-start(f32[512]{0:T(512)S(1)} %broadcast_multiply_fusion.5) | copy-start | bytes 6148
  405.6 81.1 %copy-start.112 = (f32[512]{0:T(512)}, f32[512]{0:T(512)S(1)}, u32[]{:S(2)}) copy-start(f32[512]{0:T(512)S(1)} %fusion.128) | copy-start | bytes 6148
  489.8 147.9 %copy-start.76 = (f32[512]{0:T(512)}, f32[512]{0:T(512)S(1)}, u32[]{:S(2)}) copy-start(f32[512]{0:T(512)S(1)} %broadcast_multiply_fusion.4) | copy-start | bytes 6148
  492.1 145.6 %copy-start.107 = (f32[512]{0:T(512)}, f32[512]{0:T(512)S(1)}, u32[]{:S(2)}) copy-start(f32[512]{0:T(512)S(1)} %fusion.129) | copy-start | bytes 6148
  728.4 80.0 %copy-start.22 = (f32[512,1024]{1,0:T(8,128)}, f32[512,1024]{1,0:T(8,128)S(1)}, u32[]{:S(2)}) copy-start(f32[512,1024]{1,0:T(8,128)S(1)} %get-tuple-element.158) | copy-start | bytes 6291460
  900.1 89.4 %copy-start.141 = (f32[512]{0:T(512)}, f32[512]{0:T(512)S(1)}, u32[]{:S(2)}) copy-start(f32[512]{0:T(512)S(1)} %negate_multiply_fusion.1) | copy-start | bytes 6148
  989.4 284.5 %reduce-scatter.45.cloned.1.call-start = ((), (), s32[]{:S(2)}) async-start(), calls=%async_computation.34 | async-start | bytes 6291456 | tf_op jit(solution)/shard_map/reduce_scatter | solution.py:244
  1078.2 220.8 %reduce-scatter.39.cloned.1.call-start = ((), (), s32[]{:S(2)}) async-start(), calls=%async_computation.31 | async-start | bytes 6291456 | tf_op jit(solution)/shard_map/reduce_scatter | solution.py:270
  1121.1 208.2 %reduce-scatter.41.cloned.1.call-start = ((), (), s32[]{:S(2)}) async-start(), calls=%async_computation.32 | async-start | bytes 6291456 | tf_op jit(solution)/shard_map/reduce_scatter | solution.py:270
  1174.6 233.6 %reduce-scatter.77.cloned.1.call-start = ((), (), s32[]{:S(2)}) async-start(), calls=%async_computation.52 | async-start | bytes 278528
  1177.4 231.6 %reduce-scatter.75.cloned.1.call-start = ((), (), s32[]{:S(2)}) async-start(), calls=%async_computation.51 | async-start | bytes 278528
  1178.5 241.2 %reduce-scatter.81.cloned.1.call-start = ((), (), s32[]{:S(2)}) async-start(), calls=%async_computation.54 | async-start | bytes 278528
  1179.6 298.6 %reduce-scatter.79.cloned.1.call-start = ((), (), s32[]{:S(2)}) async-start(), calls=%async_computation.53 | async-start | bytes 278528
  1180.5 361.9 %reduce-scatter.57.cloned.1.call-start = ((), (), s32[]{:S(2)}) async-start(), calls=%async_computation.40 | async-start | bytes 2228224 | tf_op jit(solution)/shard_map/reduce_scatter | solution.py:306
  1183.4 423.9 %reduce-scatter.55.cloned.1.call-start = ((), (), s32[]{:S(2)}) async-start(), calls=%async_computation.39 | async-start | bytes 2228224 | tf_op jit(solution)/shard_map/reduce_scatter | solution.py:306
  1189.0 482.6 %reduce-scatter.51.cloned.1.call-start = ((), (), s32[]{:S(2)}) async-start(), calls=%async_computation.37 | async-start | bytes 2228224 | tf_op jit(solution)/shard_map/reduce_scatter | solution.py:300
  1193.4 542.9 %reduce-scatter.53.cloned.1.call-start = ((), (), s32[]{:S(2)}) async-start(), calls=%async_computation.38 | async-start | bytes 2228224 | tf_op jit(solution)/shard_map/reduce_scatter | solution.py:300
  1199.4 601.2 %reduce-scatter.49.cloned.1.call-start = ((), (), s32[]{:S(2)}) async-start(), calls=%async_computation.36 | async-start | bytes 2228224 | tf_op jit(solution)/shard_map/reduce_scatter | solution.py:297
  1205.0 660.4 %reduce-scatter.47.cloned.1.call-start = ((), (), s32[]{:S(2)}) async-start(), calls=%async_computation.35 | async-start | bytes 2228224 | tf_op jit(solution)/shard_map/reduce_scatter | solution.py:297
  1209.2 763.7 %reduce-scatter.65.cloned.1.call-start = ((), (), s32[]{:S(2)}) async-start(), calls=%async_computation.44 | async-start | bytes 8912896 | tf_op jit(solution)/shard_map/reduce_scatter | solution.py:218
  1223.7 857.5 %reduce-scatter.63.cloned.1.call-start = ((), (), s32[]{:S(2)}) async-start(), calls=%async_computation.43 | async-start | bytes 8912896 | tf_op jit(solution)/shard_map/reduce_scatter | solution.py:218
  1238.2 951.5 %reduce-scatter.61.cloned.1.call-start = ((), (), s32[]{:S(2)}) async-start(), calls=%async_computation.42 | async-start | bytes 8912896 | tf_op jit(solution)/shard_map/reduce_scatter | solution.py:215
  1249.0 1049.1 %reduce-scatter.59.cloned.1.call-start = ((), (), s32[]{:S(2)}) async-start(), calls=%async_computation.41 | async-start | bytes 8912896 | tf_op jit(solution)/shard_map/reduce_scatter | solution.py:215
  1259.8 1114.5 %reduce-scatter.71.cloned.1.call-start = ((), (), s32[]{:S(2)}) async-start(), calls=%async_computation.49 | async-start | bytes 4456448
  1273.9 1177.0 %reduce-scatter.73.cloned.1.call-start = ((), (), s32[]{:S(2)}) async-start(), calls=%async_computation.50 | async-start | bytes 4456448
  1286.4 1252.8 %reduce-scatter.67.cloned.1.call-start = ((), (), s32[]{:S(2)}) async-start(), calls=%async_computation.47 | async-start | bytes 6684672
  1315.6 1312.2 %reduce-scatter.69.cloned.1.call-start = ((), (), s32[]{:S(2)}) async-start(), calls=%async_computation.48 | async-start | bytes 6684672
  1346.3 1362.9 %all-reduce.7.cloned.1.call-start = ((), (), s32[]{:S(2)}) async-start(), calls=%async_computation.55 | async-start | bytes 5505024 | tf_op jit(solution)/shard_map/psum | solution.py:319
  (150 other events, 1383.0 us)
Sparse Core Ops, SparseCore 0:
  10.2 53.2 all-gather.22
  65.7 60.3 all-gather.16
  128.2 55.5 all-gather.36
  185.2 56.7 all-gather.34
  243.4 56.7 all-gather.32
  301.6 56.7 all-gather.18
  360.5 41.3 all-gather.20
  404.1 40.1 all-gather.24
  446.5 40.1 all-gather.26
  488.7 73.6 all-gather.28
  564.6 73.1 all-gather.30
  989.6 52.5 reduce-scatter.42
  1078.3 52.3 reduce-scatter.44
  1132.9 54.3 reduce-scatter.38
  1189.5 54.2 reduce-scatter.40
  1247.7 55.3 reduce-scatter.76
  1307.1 54.2 reduce-scatter.74
  1365.3 54.3 reduce-scatter.80
  1423.8 54.2 reduce-scatter.78
  1481.7 60.5 reduce-scatter.56
  1546.6 60.6 reduce-scatter.54
  1611.0 60.5 reduce-scatter.50
  1675.8 60.5 reduce-scatter.52
  1739.9 60.6 reduce-scatter.48
  1804.8 60.5 reduce-scatter.46
  1869.3 103.5 reduce-scatter.64
  1976.8 104.3 reduce-scatter.62
  2085.3 104.3 reduce-scatter.60
  2193.7 104.3 reduce-scatter.58
  2301.8 72.4 reduce-scatter.70
  2379.3 71.5 reduce-scatter.72
  2454.8 84.3 reduce-scatter.66
  2543.5 84.3 reduce-scatter.68
  2631.7 77.3 all-reduce.6
where the time goes:
time: 2740 us; the launch traced here: 2730 us
  waiting for transfers between devices  1630 us (59%)
  matrix products  629 us (23%)
  other arithmetic  168 us (6%)
  local copies, waits for them, and re-layouts  143 us (5%)
  blocking collectives  137 us (5%)
    unnamed x42, waiting for transfers between devices  396 us
    reduce_scatter x2, waiting for transfers between devices, per_device(): lax.psum_scatter(ffn_terms[0].astype(jnp.bfloat16), 'batch', scatter_dime...  215 us
    reduce_scatter x2, waiting for transfers between devices, per_device(): lax.psum_scatter(ffn_terms[1].astype(jnp.bfloat16), 'batch', scatter_dime...  204 us
    reduce_scatter x2, waiting for transfers between devices, per_device(): lax.psum_scatter(attn_terms[1].astype(jnp.bfloat16), 'batch', scatter_dim...  127 us
    reduce_scatter x2, waiting for transfers between devices, per_device(): lax.psum_scatter(attn_terms[2].astype(jnp.bfloat16), 'batch', scatter_dim...  127 us
    reduce_scatter x2, waiting for transfers between devices, per_device(): lax.psum_scatter(attn_terms[4].astype(jnp.bfloat16), 'batch', scatter_dim...  121 us
    convert_element_type x4, other arithmetic, attention_backward(): d_scores = (probabilities * (d_probs - inner_sum)).astype(jnp.bfloat16)  112 us
    all_gather x2, waiting for transfers between devices, per_device(): lax.all_gather(projected[:, :, D:], 'blk', axis=1, tiled=True)  95.4 us
  transfers between devices with their start and end apart: 34, of which 27 were waited for; matrix products, arithmetic and copies ran while one was open for 20% of the time, Pallas kernels for 0%

commit v1 on v0

--- a/solution.py
+++ b/solution.py
@@ -1,6 +1,10 @@
+import functools
+
 import jax
 import jax.numpy as jnp
 from jax import lax
+from jax.experimental import pallas as pl
+from jax.experimental.pallas import tpu as pltpu
 from jax.sharding import PartitionSpec as P
 
 D = 1024
@@ -8,11 +12,200 @@
 HD = 64
 MB_ROWS = 1
 MICRO = 2
-
-
 ALPHA = 300.0**0.25
 MASKED = -1e30
 EPSILON = 1e-05
+PAIR = 2 * HD
+BLOCK = 256
+MASK_STEP = -(2.0**100)
+
+
+def nt(left, right):
+    return lax.dot_general(left, right, (((1,), (1,)), ((), ())), preferred_element_type=jnp.float32)
+
+
+def nn(left, right):
+    return lax.dot_general(left, right, (((1,), (0,)), ((), ())), preferred_element_type=jnp.float32)
+
+
+def lane_of(rows):
+    return lax.broadcasted_iota(jnp.int32, (rows, PAIR), 1)
+
+
+def attention_fwd_kernel(causal, q_ref, k_ref, v_ref, fq_ref, fk_ref, out_ref, lse_ref):
+    length = q_ref.shape[0]
+    mem = k_ref.shape[0]
+    low_q = lane_of(length) < HD
+    low_k = lane_of(mem) < HD
+    q = q_ref[...] * jnp.bfloat16(HD**-0.5)
+    k = k_ref[...]
+    v = v_ref[...]
+    fq = fq_ref[...]
+    fk = fk_ref[...]
+    ones = jnp.ones_like(v)
+    queries = (jnp.where(low_q, q, fq), jnp.where(low_q, fq, q))
+    keys = (jnp.where(low_k, k, fk), jnp.where(low_k, fk, k))
+    values = (jnp.where(low_k, v, ones), jnp.where(low_k, ones, v))
+    low_blk = lane_of(BLOCK) < HD
+    for i in range(length // BLOCK):
+        seen = (i + 1) * BLOCK if causal else mem
+        rows = slice(i * BLOCK, (i + 1) * BLOCK)
+        accs, peaks = [], []
+        for h in range(2):
+            scores = nt(queries[h][rows], keys[h][:seen])
+            if causal:
+                tri = lax.broadcasted_iota(jnp.int32, (BLOCK, BLOCK), 0) >= lax.broadcasted_iota(
+                    jnp.int32, (BLOCK, BLOCK), 1
+                )
+                diag = jnp.where(tri, scores[:, seen - BLOCK :], MASK_STEP)
+                scores = diag if i == 0 else jnp.concatenate([scores[:, : seen - BLOCK], diag], axis=1)
+            peak = jnp.max(scores, axis=1, keepdims=True)
+            raised = jnp.exp(scores - peak).astype(jnp.bfloat16)
+            accs.append(nn(raised, values[h][:seen]))
+            peaks.append(peak)
+        total = pltpu.roll(jnp.where(low_blk, accs[1], accs[0]), HD, 1)
+        out_ref[rows, :] = (jnp.where(low_blk, accs[0], accs[1]) / total).astype(out_ref.dtype)
+        lse_ref[rows, :] = jnp.where(low_blk, peaks[0], peaks[1]) + jnp.log(total)
+
+
+def split3(value):
+    hi = value.astype(jnp.bfloat16)
+    rest = value - hi.astype(jnp.float32)
+    mid = rest.astype(jnp.bfloat16)
+    lo = (rest - mid.astype(jnp.float32)).astype(jnp.bfloat16)
+    return hi, mid, lo
+
+
+def placed(lane, start, pieces, other):
+    for n, piece in enumerate(pieces):
+        other = jnp.where(lane == start + n, piece, other)
+    return other
+
+
+def attention_bwd_kernel(causal, q_ref, k_ref, v_ref, fq_ref, fk_ref, out_ref, lse_ref, do_ref, dq_ref, dk_ref, dv_ref, dk_acc, dv_acc, dq_acc):
+    length = q_ref.shape[0]
+    mem = k_ref.shape[0]
+    lane_q = lane_of(length)
+    lane_k = lane_of(mem)
+    low_q = lane_q < HD
+    low_k = lane_k < HD
+    scale = jnp.bfloat16(HD**-0.5)
+    q = q_ref[...] * scale
+    k = k_ref[...]
+    v = v_ref[...]
+    do = do_ref[...]
+    fq = fq_ref[...]
+    fk = fk_ref[...]
+    zero_q = jnp.zeros_like(q)
+    zero_k = jnp.zeros_like(k)
+    one_k = jnp.ones_like(k)
+    prod = do.astype(jnp.float32) * out_ref[...].astype(jnp.float32)
+    sum_a = jnp.sum(jnp.where(low_q, prod, 0.0), axis=1, keepdims=True)
+    sum_b = jnp.sum(jnp.where(low_q, 0.0, prod), axis=1, keepdims=True)
+    inner = jnp.where(low_q, sum_b, sum_a)
+    lse = pltpu.roll(lse_ref[...], HD, 1)
+    half_q = lane_q & (HD - 1)
+    half_k = lane_k & (HD - 1)
+    fq = placed(half_q, 2, split3(-lse), fq)
+    fk = jnp.where((half_k >= 2) & (half_k < 5), one_k, fk)
+    fd = placed(half_q, 0, split3(-inner), zero_q)
+    fv = jnp.where(half_k < 3, one_k, zero_k)
+    queries = (jnp.where(low_q, q, fq), jnp.where(low_q, fq, q))
+    keys = (jnp.where(low_k, k, fk), jnp.where(low_k, fk, k))
+    grads = (jnp.where(low_q, do, fd), jnp.where(low_q, fd, do))
+    values = (jnp.where(low_k, v, fv), jnp.where(low_k, fv, v))
+    plain_q = (jnp.where(low_q, q, zero_q), jnp.where(low_q, zero_q, q))
+    plain_do = (jnp.where(low_q, do, zero_q), jnp.where(low_q, zero_q, do))
+    k_t = k.T
+    blocks = length // BLOCK
+    for i in range(blocks):
+        rows = slice(i * BLOCK, (i + 1) * BLOCK)
+        seen = (i + 1) * BLOCK if causal else mem
+        probs, d_scores = [], []
+        for h in range(2):
+            p = jnp.exp(nt(keys[h][:seen], queries[h][rows]))
+            if causal:
+                tri = lax.broadcasted_iota(jnp.int32, (BLOCK, BLOCK), 0) <= lax.broadcasted_iota(
+                    jnp.int32, (BLOCK, BLOCK), 1
+                )
+                diag = jnp.where(tri, p[seen - BLOCK :], 0.0)
+                p = diag if i == 0 else jnp.concatenate([p[: seen - BLOCK], diag], axis=0)
+            ds = (p * nt(values[h][:seen], grads[h][rows])).astype(jnp.bfloat16)
+            probs.append(p.astype(jnp.bfloat16))
+            d_scores.append(ds)
+            dq_acc[h * HD : (h + 1) * HD, rows] = nn(k_t[h * HD : (h + 1) * HD, :seen], ds)
+        dv = nn(probs[0], plain_do[0][rows]) + nn(probs[1], plain_do[1][rows])
+        dk = nn(d_scores[0], plain_q[0][rows]) + nn(d_scores[1], plain_q[1][rows])
+        if i == 0:
+            dv_acc[:seen] = dv
+            dk_acc[:seen] = dk
+        elif causal:
+            dv_acc[: seen - BLOCK] += dv[: seen - BLOCK]
+            dk_acc[: seen - BLOCK] += dk[: seen - BLOCK]
+            dv_acc[seen - BLOCK : seen] = dv[seen - BLOCK :]
+            dk_acc[seen - BLOCK : seen] = dk[seen - BLOCK :]
+        else:
+            dv_acc[...] += dv
+            dk_acc[...] += dk
+    dq_ref[...] = (dq_acc[...].T * (HD**-0.5)).astype(dq_ref.dtype)
+    dk_ref[...] = dk_acc[...].astype(dk_ref.dtype)
+    dv_ref[...] = dv_acc[...].astype(dv_ref.dtype)
+
+
+def cols(length, first):
+    return pl.BlockSpec((length, PAIR), lambda j: (0, first + j))
+
+
+def whole(length):
+    return pl.BlockSpec((length, PAIR), lambda j: (0, 0))
+
+
+def attention_forward(q_src, q_at, kv_src, k_at, v_at, fq, fk, causal):
+    length, mem = q_src.shape[0], kv_src.shape[0]
+    pairs = NH // 2
+    return pl.pallas_call(
+        functools.partial(attention_fwd_kernel, causal),
+        grid=(pairs,),
+        in_specs=[cols(length, q_at), cols(mem, k_at), cols(mem, v_at), whole(length), whole(mem)],
+        out_specs=[cols(length, 0), cols(length, 0)],
+        out_shape=[
+            jax.ShapeDtypeStruct((length, D), jnp.bfloat16),
+            jax.ShapeDtypeStruct((length, D), jnp.float32),
+        ],
+        compiler_params=pltpu.CompilerParams(vmem_limit_bytes=48 * 2**20),
+        name="attention_forward",
+    )(q_src, kv_src, kv_src, fq, fk)
+
+
+def attention_backward(q_src, q_at, kv_src, k_at, v_at, fq, fk, mixed, lse, d_mixed, causal):
+    length, mem = q_src.shape[0], kv_src.shape[0]
+    pairs = NH // 2
+    return pl.pallas_call(
+        functools.partial(attention_bwd_kernel, causal),
+        grid=(pairs,),
+        in_specs=[cols(length, q_at), cols(mem, k_at), cols(mem, v_at), whole(length), whole(mem),
+                  cols(length, 0), cols(length, 0), cols(length, 0)],
+        out_specs=[cols(length, 0), cols(mem, 0), cols(mem, 0)],
+        out_shape=[
+            jax.ShapeDtypeStruct((length, D), jnp.bfloat16),
+            jax.ShapeDtypeStruct((mem, D), jnp.bfloat16),
+            jax.ShapeDtypeStruct((mem, D), jnp.bfloat16),
+        ],
+        scratch_shapes=[
+            pltpu.VMEM((mem, PAIR), jnp.float32),
+            pltpu.VMEM((mem, PAIR), jnp.float32),
+            pltpu.VMEM((PAIR, length), jnp.float32),
+        ],
+        compiler_params=pltpu.CompilerParams(vmem_limit_bytes=48 * 2**20),
+        name="attention_backward",
+    )(q_src, kv_src, kv_src, fq, fk, mixed, lse, d_mixed)
+
+
+def document_features(query_ids, key_ids):
+    half = jnp.arange(PAIR, dtype=jnp.int32)[None, :] % HD
+    fq = (half == query_ids[:, None]).astype(jnp.bfloat16)
+    fk = jnp.where((half < 2) & (half != key_ids[:, None]), MASK_STEP, 0.0).astype(jnp.bfloat16)
+    return fq, fk
 
 
 def shortened(array):
@@ -48,7 +241,7 @@
     return jnp.where(allowed[:, None], scores, MASKED)
 
 
-def attention_forward(queries, key_rows, value_rows, allowed):
+def plain_attention_forward(queries, key_rows, value_rows, allowed):
     scores = attention_scores(queries, key_rows, allowed)
     row_peak = jnp.max(scores, axis=-1, keepdims=True)
     raised = jnp.exp(scores - row_peak)
@@ -63,7 +256,7 @@
     return (attended.reshape(queries.shape).astype(jnp.bfloat16), row_peak, row_total)
 
 
-def attention_backward(queries, key_rows, value_rows, allowed, row_peak, row_total, d_attended):
+def plain_attention_backward(queries, key_rows, value_rows, allowed, row_peak, row_total, d_attended):
     scores = attention_scores(queries, key_rows, allowed)
     probabilities = jnp.exp(scores - row_peak) / row_total
     d_heads = split_heads(d_attended)
@@ -96,7 +289,7 @@
     return tuple((first_term + second_term for first_term, second_term in zip(running, fresh)))
 
 
-def per_device(
+def split_row_device(
     inputs,
     memory,
     target_ids,
@@ -150,7 +343,7 @@
             lax.all_gather(seg_rows, "blk", axis=1, tiled=True),
         )
         self_allowed = (seg_rows[:, :, None] == key_segs[:, None, :]) & causal[None]
-        self_mixed, self_peak, self_total = attention_forward(
+        self_mixed, self_peak, self_total = plain_attention_forward(
             self_queries, key_pairs[:, :, :D], key_pairs[:, :, D:], self_allowed
         )
         mixed_flat = self_mixed.reshape(token_count, D)
@@ -174,7 +367,7 @@
             lax.all_gather(memory_seg_rows, "blk", axis=1, tiled=True),
         )
         cross_allowed = seg_rows[:, :, None] == memory_segs[:, None, :]
-        cross_mixed, cross_peak, cross_total = attention_forward(
+        cross_mixed, cross_peak, cross_total = plain_attention_forward(
             cross_queries, memory_pairs[:, :, :D], memory_pairs[:, :, D:], cross_allowed
         )
         cross_flat = cross_mixed.reshape(token_count, D)
@@ -232,7 +425,7 @@
             .astype(jnp.bfloat16)
             .reshape(MB_ROWS, tokens_here, D)
         )
-        d_cross_queries, d_memory_all = attention_backward(
+        d_cross_queries, d_memory_all = plain_attention_backward(
             cross_queries,
             memory_pairs[:, :, :D],
             memory_pairs[:, :, D:],
@@ -258,7 +451,7 @@
         d_self = (
             back_prod(d_branch_one, out_full).astype(jnp.bfloat16).reshape(MB_ROWS, tokens_here, D)
         )
-        d_self_queries, d_key_all = attention_backward(
+        d_self_queries, d_key_all = plain_attention_backward(
             self_queries,
             key_pairs[:, :, :D],
             key_pairs[:, :, D:],
@@ -338,6 +531,230 @@
     )
 
 
+def swap_pair(array):
+    return lax.ppermute(array, "blk", [(0, 1), (1, 0)])
+
+
+def rows_in(array):
+    count = lax.axis_size("blk")
+    here = array.shape[0] // count
+    parts = array.reshape((count, here) + array.shape[1:])
+    if count == 1:
+        return parts[0]
+    if count == 2:
+        me = lax.axis_index("blk")
+        kept = lax.dynamic_index_in_dim(parts, me, 0, keepdims=False)
+        got = swap_pair(lax.dynamic_index_in_dim(parts, 1 - me, 0, keepdims=False))
+        first = jnp.where(me == 0, kept, got)
+        second = jnp.where(me == 0, got, kept)
+        return jnp.concatenate([first, second], axis=1)
+    moved = lax.all_to_all(parts, "blk", 0, 0)
+    moved = jnp.moveaxis(moved, 0, 1)
+    return moved.reshape((here, count * array.shape[1]) + array.shape[2:])
+
+
+def rows_out(array, kind):
+    count = lax.axis_size("blk")
+    here, length = array.shape[:2]
+    tokens = length // count
+    parts = array.reshape((here, count, tokens) + array.shape[2:])
+    if count == 1:
+        return parts[:, 0].astype(kind)
+    if count == 2:
+        me = lax.axis_index("blk")
+        kept = lax.dynamic_index_in_dim(parts, me, 1, keepdims=False).astype(kind)
+        sent = lax.dynamic_index_in_dim(parts, 1 - me, 1, keepdims=False).astype(jnp.bfloat16)
+        got = swap_pair(sent).astype(kind)
+        first = jnp.where(me == 0, kept, got)
+        second = jnp.where(me == 0, got, kept)
+        return jnp.concatenate([first, second], axis=0)
+    moved = lax.all_to_all(jnp.moveaxis(parts, 1, 0).astype(jnp.bfloat16), "blk", 0, 0)
+    return moved.reshape((count * here, tokens) + array.shape[2:]).astype(kind)
+
+
+def gathered(shard, axis=0):
+    return lax.all_gather(shard, "batch", axis=axis, tiled=True)
+
+
+def shared_out(grad, axis=0):
+    part = lax.psum_scatter(
+        grad.astype(jnp.bfloat16), "batch", scatter_dimension=axis, tiled=True
+    )
+    return lax.psum(part, "blk").astype(jnp.float32)
+
+
+def each_row(function, rows, *arrays):
+    if rows == 1:
+        return function(*arrays)
+    cut = [a.reshape((rows, a.shape[0] // rows) + a.shape[1:]) for a in arrays]
+    results = [function(*(c[n] for c in cut)) for n in range(rows)]
+    return tuple(jnp.concatenate(group, axis=0) for group in zip(*results))
+
+
+def dot32(left, right):
+    return jnp.dot(left, right, preferred_element_type=jnp.float32)
+
+
+def whole_row_device(
+    inputs,
+    memory,
+    target_ids,
+    memory_ids,
+    cotangent,
+    w_self_qkv,
+    w_self_out,
+    w_cross_q,
+    w_cross_kv,
+    w_cross_out,
+    w_up,
+    w_down,
+    b_up,
+    gains,
+    shifts,
+):
+    low = jnp.bfloat16
+    x_rows = rows_in(inputs)
+    rows, length = x_rows.shape[:2]
+    x_flat = x_rows.reshape(-1, D)
+    memory_flat = rows_in(memory).reshape(-1, D)
+    ids = rows_in(jnp.stack([target_ids, memory_ids], axis=2))
+    target_flat = ids[:, :, 0].reshape(-1)
+    memory_id_flat = ids[:, :, 1].reshape(-1)
+    cot_flat = rows_in(cotangent).reshape(-1, D).astype(jnp.float32)
+
+    qkv_full = gathered(w_self_qkv)
+    out_full = gathered(w_self_out)
+    cross_q_full = gathered(w_cross_q)
+    cross_kv_full = gathered(w_cross_kv)
+    cross_out_full = gathered(w_cross_out)
+    up_full = gathered(w_up)
+    down_full = gathered(w_down)
+    small = gathered(jnp.concatenate([gains, shifts], axis=0), 1).astype(jnp.float32)
+    gain_full, shift_full = small[:3], small[3:]
+    bias_full = gathered(b_up).astype(jnp.float32)
+
+    projected = dot32(x_flat, qkv_full).astype(low)
+
+    def self_forward(rows_proj, rows_ids):
+        fq, fk = document_features(rows_ids, rows_ids)
+        return attention_forward(rows_proj, 0, rows_proj, 8, 16, fq, fk, True)
+
+    mixed_flat, self_lse = each_row(self_forward, rows, projected, target_flat)
+    first_sum = ALPHA * x_flat.astype(jnp.float32) + dot32(mixed_flat, out_full)
+    first = layer_norm(first_sum, gain_full[0], shift_full[0])
+    first_low = first.astype(low)
+    cross_queries = dot32(first_low, cross_q_full).astype(low)
+    memory_pairs = dot32(memory_flat, cross_kv_full).astype(low)
+
+    def cross_forward(rows_q, rows_kv, rows_ids, rows_memory_ids):
+        fq, fk = document_features(rows_ids, rows_memory_ids)
+        return attention_forward(rows_q, 0, rows_kv, 0, 8, fq, fk, False)
+
+    cross_flat, cross_lse = each_row(
+        cross_forward, rows, cross_queries, memory_pairs, target_flat, memory_id_flat
+    )
+    second_sum = ALPHA * first + dot32(cross_flat, cross_out_full)
+    second = layer_norm(second_sum, gain_full[1], shift_full[1])
+    second_low = second.astype(low)
+    hidden_pre = dot32(second_low, up_full) + bias_full
+    hidden_low = jax.nn.gelu(hidden_pre).astype(low)
+    third_sum = ALPHA * second + dot32(hidden_low, down_full) + shift_full[3]
+    result, third_back = jax.vjp(layer_norm, third_sum, gain_full[2], shift_full[2])
+    output = rows_out(result.reshape(rows, length, D), low)
+
+    d_third, d_gain_three, d_shift_three = third_back(cot_flat)
+    d_branch_three = d_third.astype(low)
+    grad_down = shared_out(weight_grad(hidden_low, d_branch_three))
+    grad_bias_down = jnp.sum(d_branch_three.astype(jnp.float32), axis=0)
+    d_hidden = back_prod(d_branch_three, down_full).astype(low)
+    gelu_back = jax.vjp(jax.nn.gelu, hidden_pre)[1]
+    d_pre = gelu_back(d_hidden.astype(jnp.float32))[0].astype(low)
+    grad_up = shared_out(weight_grad(second_low, d_pre))
+    grad_bias_up = shared_out(jnp.sum(d_pre.astype(jnp.float32), axis=0))
+    d_second = ALPHA * d_third + back_prod(d_pre, up_full)
+    second_back = jax.vjp(layer_norm, second_sum, gain_full[1], shift_full[1])[1]
+    d_second_sum, d_gain_two, d_shift_two = second_back(d_second)
+    d_branch_two = d_second_sum.astype(low)
+    grad_cross_out = shared_out(weight_grad(cross_flat, d_branch_two))
+    d_cross = back_prod(d_branch_two, cross_out_full).astype(low)
+
+    def cross_backward(rows_q, rows_kv, rows_ids, rows_memory_ids, mixed, lse, d_mixed):
+        fq, fk = document_features(rows_ids, rows_memory_ids)
+        return attention_backward(rows_q, 0, rows_kv, 0, 8, fq, fk, mixed, lse, d_mixed, False)
+
+    d_cross_low, d_memory_keys, d_memory_values = each_row(
+        cross_backward,
+        rows,
+        cross_queries,
+        memory_pairs,
+        target_flat,
+        memory_id_flat,
+        cross_flat,
+        cross_lse,
+        d_cross,
+    )
+    d_memory_pairs = jnp.concatenate([d_memory_keys, d_memory_values], axis=1)
+    grad_cross_kv = shared_out(weight_grad(memory_flat, d_memory_pairs))
+    d_memory = rows_out(
+        back_prod(d_memory_pairs, cross_kv_full).reshape(rows, length, D), jnp.float32
+    )
+    grad_cross_q = shared_out(weight_grad(first_low, d_cross_low))
+    d_first = ALPHA * d_second_sum + back_prod(d_cross_low, cross_q_full)
+    first_back = jax.vjp(layer_norm, first_sum, gain_full[0], shift_full[0])[1]
+    d_first_sum, d_gain_one, d_shift_one = first_back(d_first)
+    d_branch_one = d_first_sum.astype(low)
+    grad_self_out = shared_out(weight_grad(mixed_flat, d_branch_one))
+    d_self = back_prod(d_branch_one, out_full).astype(low)
+
+    def self_backward(rows_proj, rows_ids, mixed, lse, d_mixed):
+        fq, fk = document_features(rows_ids, rows_ids)
+        return attention_backward(
+            rows_proj, 0, rows_proj, 8, 16, fq, fk, mixed, lse, d_mixed, True
+        )
+
+    d_projected = jnp.concatenate(
+        each_row(self_backward, rows, projected, target_flat, mixed_flat, self_lse, d_self), axis=1
+    )
+    grad_self_qkv = shared_out(weight_grad(x_flat, d_projected))
+    d_input = rows_out(
+        (ALPHA * d_first_sum + back_prod(d_projected, qkv_full)).reshape(rows, length, D),
+        jnp.float32,
+    )
+    grad_rows = jnp.stack(
+        [
+            d_gain_one,
+            d_gain_two,
+            d_gain_three,
+            d_shift_one,
+            d_shift_two,
+            d_shift_three,
+            grad_bias_down,
+        ]
+    )
+    grad_rows = shared_out(grad_rows, 1)
+    return (
+        output,
+        d_input,
+        d_memory,
+        grad_self_qkv,
+        grad_self_out,
+        grad_cross_q,
+        grad_cross_kv,
+        grad_cross_out,
+        grad_up,
+        grad_down,
+        grad_bias_up,
+        grad_rows[:3],
+        grad_rows[3:],
+    )
+
+
+def per_device(inputs, *others):
+    if inputs.shape[0] % lax.axis_size("blk") == 0:
+        return whole_row_device(inputs, *others)
+    return split_row_device(inputs, *others)
+
+
 def solution(mesh):
     return jax.shard_map(
         per_device,

time: 2740 us -> 1270 us (0.46)
  waiting for transfers between devices: 1630 us -> 695 us
  matrix products: 629 us -> 215 us
  Pallas kernels: 0 us -> 158 us
  other arithmetic: 168 us -> 49.6 us
  local copies, waits for them, and re-layouts: 143 us -> 44.3 us
  blocking collectives: 137 us -> 77.4 us
    unnamed x42 -> x17, waiting for transfers between devices: 396 us -> 19 us
    reduce_scatter x14 -> x7, waiting for transfers between devices: 795 us -> 425 us  [shared_out(): lax.psum_scatter(grad.astype(jnp.bfloat16), 'batch', scatter_dimension=ax...]
    dot_general x34 -> x7, matrix products: 375 us -> 72.9 us  [dot32(): return jnp.dot(left, right, preferred_element_type=jnp.float32)]
    all_gather x11 -> x7, waiting for transfers between devices: 377 us -> 190 us  [gathered(): return lax.all_gather(shard, 'batch', axis=axis, tiled=True)]
    pallas_call x0 -> x4, Pallas kernels: none -> 158 us  [the longest x2 93.8 us: attention_backward(): pl.pallas_call(functools.partial(attention_bwd_kernel, causal), grid=(pai...]
    convert_element_type x25 -> x12, other arithmetic: 131 us -> 12.9 us  [the longest x8 12.4 us: shared_out(): return lax.psum(part, 'blk').astype(jnp.float32)]
    sub x4 -> x0, matrix products: 72.1 us -> none  [attention_forward(): raised = jnp.exp(scores - row_peak)]
    unnamed x344 -> x138, local copies, waits for them, and re-layouts: 83.7 us -> 32.9 us
  transfers between devices with their start and end apart: 34 -> 23, of which waited for: 27 -> 13; matrix products, arithmetic and copies ran while one was open for 20% -> 14% of each run, Pallas kernels for 0% -> 8%
where the time goes in v1:
time: 1270 us
  waiting for transfers between devices  695 us (55%)
  matrix products  215 us (17%)
  Pallas kernels  158 us (12%)
  blocking collectives  77.4 us (6%)
  other arithmetic  49.6 us (4%)
  local copies, waits for them, and re-layouts  44.3 us (3%)
  between operations  16 us (1%)
    reduce_scatter x7, waiting for transfers between devices, shared_out(): lax.psum_scatter(grad.astype(jnp.bfloat16), 'batch', scatter_dimension=ax...  425 us
    all_gather x7, waiting for transfers between devices, gathered(): return lax.all_gather(shard, 'batch', axis=axis, tiled=True)  190 us
    pallas_call x2, Pallas kernels, attention_backward(): pl.pallas_call(functools.partial(attention_bwd_kernel, causal), grid=(pai...  93.8 us
    dot_general x7, matrix products, back_prod(): jnp.einsum('tn,kn->tk', grad_rows, matrix, preferred_element_type=jnp.flo...  75.6 us
    dot_general x7, matrix products, dot32(): return jnp.dot(left, right, preferred_element_type=jnp.float32)  72.9 us
    dot_general x7, matrix products, weight_grad(): jnp.einsum('tk,tn->kn', left_rows, right_rows, preferred_element_type=jnp...  66.2 us
    pallas_call x2, Pallas kernels, attention_forward(): pl.pallas_call(functools.partial(attention_fwd_kernel, causal), grid=(pai...  63.7 us
    psum x1, waiting for transfers between devices, shared_out(): return lax.psum(part, 'blk').astype(jnp.float32)  45.3 us
  transfers between devices with their start and end apart: 23, of which 13 were waited for; matrix products, arithmetic and copies ran while one was open for 14% of the time, Pallas kernels for 8%

profile of v1, /device:TPU:0, one launch (start us, length us, event | category | flops | bytes accessed | tf_op | source)
XLA Modules:
  0.0 1265.2 jit_solution(11017917054417485004)
XLA Ops:
  14.4 3.0 collective-permute-start
  22.8 22.4 %all-gather = bf16[16,64,7]{1,2,0:T(8,128)(2,1)S(1)} all-gather(bf16[1,64,7]{1,2,0:T(8,128)(2,1)S(1)} %maximum_bitcast_fusion.7), channel_id=1, replica_groups=mesh['batch'=16,'blk'=2] {'batch'}, dimensions={0}, use_global_device_ids=true | all-gather | bytes 15232 | tf_op jit(solution)/shard_map/all_gather | solution.py:576
  46.0 17.5 %all-gather.1 = bf16[16,1,256]{2,1,0:T(2,128)(2,1)S(1)} all-gather(bf16[1,1,256]{2,1,0:T(2,128)(2,1)S(1)} %reshape.239), channel_id=1, replica_groups=mesh['batch'=16,'blk'=2] {'batch'}, dimensions={0}, use_global_device_ids=true | all-gather | bytes 8704 | tf_op jit(solution)/shard_map/all_gather | solution.py:576
  64.2 2.8 broadcast_select_fusion.7
  69.7 16.2 %collective-permute-done.4 = bf16[1,512,1024]{2,1,0:T(8,128)(2,1)} collective-permute-done((bf16[1,512,1024]{2,1,0:T(8,128)(2,1)}, bf16[1,512,1024]{2,1,0:T(8,128)(2,1)}, u32[]{:S(2)}, u32[]{:S(2)}) %collective-permute-start.4) | collective-permute-done | bytes 1048608 | tf_op jit(solution)/shard_map/ppermute | solution.py:535
  85.9 3.8 fusion.37
  89.7 9.5 convolution_convert_fusion.5.k_ref.v_ref
  99.2 27.1 %all-gather.10.cloned.1.call-done = bf16[1024,3072]{1,0:T(8,128)(2,1)} async-done(((bf16[64,3072]{1,0:T(8,128)(2,1)}), bf16[1024,3072]{1,0:T(8,128)(2,1)}) %all-gather.10.cloned.1.call-update) | async-done | bytes 6291472 | tf_op jit(solution)/shard_map/all_gather | solution.py:576
  126.3 12.4 convolution_convert_fusion.3.q_ref.k_ref.v_ref
  138.7 28.2 %attention_forward.2 = (bf16[1024,1024]{1,0:T(8,128)(2,1)S(1)}, f32[1024,1024]{1,0:T(8,128)}) custom-call(bf16[1024,3072]{1,0:T(8,128)(2,1)} %convolution_convert_fusion.3.q_ref.k_ref.v_ref, bf16[1024,3072]{1,0:T(8,128)(2,1)} %convolution_convert_fusion.3.q_ref.k_ref.v_ref, bf16[1024,3072]{1,0:T(8,128)(2,1)} %convolution_convert_fusion.3.q_ref.k_ref.v_ref, ...), custom_call_target="tpu_custom_call" | custom-call | tf_op jit(solution)/shard_map/attention_forward/pallas_call | solution.py:166
  168.5 4.6 fusion.43
  175.7 35.0 %all-gather.14.cloned.1.call-done = bf16[1024,1024]{1,0:T(8,128)(2,1)} async-done(((bf16[64,1024]{1,0:T(8,128)(2,1)}), bf16[1024,1024]{1,0:T(8,128)(2,1)}) %all-gather.14.cloned.1.call-update) | async-done | bytes 2097168 | tf_op jit(solution)/shard_map/all_gather | solution.py:576
  210.8 5.3 convolution_convert_fusion.11.q_ref
  216.0 35.6 %attention_forward.3 = (bf16[1024,1024]{1,0:T(8,128)(2,1)S(1)}, f32[1024,1024]{1,0:T(8,128)}) custom-call(bf16[1024,1024]{1,0:T(8,128)(2,1)S(1)} %convolution_convert_fusion.11.q_ref, bf16[1024,2048]{1,0:T(8,128)(2,1)} %convolution_convert_fusion.5.k_ref.v_ref, bf16[1024,2048]{1,0:T(8,128)(2,1)} %convolution_convert_fusion.5.k_ref.v_ref, ...), custom_call_target="tpu_custom_call" | custom-call | tf_op jit(solution)/shard_map/attention_forward/pallas_call | solution.py:166
  253.0 6.1 fusion.44
  261.6 67.1 %all-gather.20.cloned.1.call-done = bf16[1024,4096]{1,0:T(8,128)(2,1)} async-done(((bf16[64,4096]{1,0:T(8,128)(2,1)}), bf16[1024,4096]{1,0:T(8,128)(2,1)}) %all-gather.20.cloned.1.call-update) | async-done | bytes 8388624 | tf_op jit(solution)/shard_map/all_gather | solution.py:576
  328.7 16.7 %fusion.31 = f32[1024,4096]{1,0:T(8,128)} fusion(bf16[1024,4096]{1,0:T(8,128)(2,1)} %all-gather.20.cloned.1.call-done, f32[1024,1024]{1,0:T(8,128)} %copy-done.10, f32[1024]{0:T(1024)S(1)} %bitcast.124, f32[1024]{0:T(1024)S(1)} %bitcast.105, f32[1024]{0:T(1024)S(1)} %fusion.24, f32[1024]{0:T(1024)S(1)} %broadcast_multiply_fusion.1), kind=kOutput, calls=%fused_computation.129 | convolution fusion | flops 8595177472 | bytes 29376512 | tf_op jit(solution)/shard_map/dot_general | solution.py:595
  345.3 58.7 %all-gather.22.cloned.1.call-done = bf16[4096,1024]{1,0:T(8,128)(2,1)} async-done(((bf16[256,1024]{1,0:T(8,128)(2,1)}), bf16[4096,1024]{1,0:T(8,128)(2,1)}) %all-gather.22.cloned.1.call-update) | async-done | bytes 8388624 | tf_op jit(solution)/shard_map/all_gather | solution.py:576
  404.0 18.4 %fusion.45 = (f32[1024]{0:T(1024)S(1)}, f32[1024,1024]{1,0:T(8,128)S(1)}) fusion(f32[1024]{0:T(1024)S(1)} %bitcast.130, bf16[4096,1024]{1,0:T(8,128)(2,1)} %all-gather.22.cloned.1.call-done, f32[1024,4096]{1,0:T(8,128)} %fusion.31, f32[4096]{0:T(1024)S(1)} %bitcast.117, f32[1024]{0:T(1024)S(1)} %bitcast.125, f32[1024]{0:T(1024)S(1)} %bitcast.106, ...), kind=kOutput, calls=%fused_computation.139 | convolution fusion | flops 8640265216 | bytes 33595392 | tf_op jit(solution)/shard_map/dot_general | solution.py:595
  425.5 3.4 fusion.13
  428.9 2.7 fusion.40
  434.8 25.4 %fusion.46 = (bf16[4096]{0:T(1024)(128)(2,1)}, bf16[1024,4096]{1,0:T(8,128)(2,1)}) fusion(f32[1024,4096]{1,0:T(8,128)} %fusion.31, f32[4096]{0:T(1024)S(1)} %bitcast.118, bf16[1024,1024]{1,0:T(8,128)(2,1)S(1)} %get-tuple-element.51, bf16[4096,1024]{1,0:T(8,128)(2,1)} %all-gather.22.cloned.1.call-done), kind=kOutput, calls=%fused_computation.140 | convolution fusion | flops 8690593792 | bytes 35676160 | tf_op jit(solution)/shard_map/tn,kn->tk/dot_general | solution.py:231
  460.2 18.2 %multiply_reduce_fusion = (bf16[1024]{0:T(1024)(128)(2,1)S(1)}, f32[1024]{0:T(1024)S(1)}, bf16[1024]{0:T(1024)(128)(2,1)S(1)}, f32[1024,1024]{1,0:T(8,128)}) fusion(f32[1024,1024]{1,0:T(8,128)} %copy-done.10, f32[1024]{0:T(1024)S(1)} %fusion.24, f32[1024]{0:T(1024)S(1)} %broadcast_multiply_fusion.1, f32[1024]{0:T(1024)S(1)} %bitcast.107, ...), kind=kOutput, calls=%fused_computation.30 | convolution fusion | flops 8601465856 | bytes 29384704 | tf_op jit(solution)/shard_map/tn,kn->tk/dot_general | solution.py:231
  478.5 3.4 fusion.39
  481.9 3.7 convolution_convert_fusion.10.do_ref
  485.6 54.0 %attention_backward.2 = (bf16[1024,1024]{1,0:T(8,128)(2,1)S(1)}, bf16[1024,1024]{1,0:T(8,128)(2,1)S(1)}, bf16[1024,1024]{1,0:T(8,128)(2,1)}) custom-call(bf16[1024,1024]{1,0:T(8,128)(2,1)} %copy-done, bf16[1024,2048]{1,0:T(8,128)(2,1)} %convolution_convert_fusion.5.k_ref.v_ref, bf16[1024,2048]{1,0:T(8,128)(2,1)} %convolution_convert_fusion.5.k_ref.v_ref, ...), custom_call_target="tpu_custom_call" | custom-call | tf_op jit(solution)/shard_map/attention_backward/pallas_call | solution.py:183
  539.7 3.4 multiply_reduce_fusion.1
  546.9 3.9 convolution_convert_fusion.8
  551.2 7.1 convolution_convert_fusion.7
  558.4 6.1 convolution_convert_fusion.6
  569.0 6.3 convolution_convert_fusion.4
  576.9 5.9 convolution_convert_fusion.9.do_ref
  582.8 39.8 %attention_backward.3 = (bf16[1024,1024]{1,0:T(8,128)(2,1)S(1)}, bf16[1024,1024]{1,0:T(8,128)(2,1)S(1)}, bf16[1024,1024]{1,0:T(8,128)(2,1)}) custom-call(bf16[1024,3072]{1,0:T(8,128)(2,1)} %convolution_convert_fusion.3.q_ref.k_ref.v_ref, bf16[1024,3072]{1,0:T(8,128)(2,1)} %convolution_convert_fusion.3.q_ref.k_ref.v_ref, ...), custom_call_target="tpu_custom_call" | custom-call | tf_op jit(solution)/shard_map/attention_backward/pallas_call | solution.py:183
  627.1 8.9 convolution_convert_fusion.2
  636.3 15.5 %convolution_convert_fusion.1 = bf16[1024,4096]{1,0:T(8,128)(2,1)} fusion(bf16[1024,4096]{1,0:T(8,128)(2,1)} %get-tuple-element.96, f32[1024,1024]{1,0:T(8,128)} %copy-done.10, f32[1024]{0:T(1024)S(1)} %bitcast.126, f32[1024]{0:T(1024)S(1)} %bitcast.109, f32[1024]{0:T(1024)S(1)} %fusion.24, f32[1024]{0:T(1024)S(1)} %broadcast_multiply_fusion.1), kind=kOutput, calls=%fused_computation.16 | convolution fusion | flops 8599371776 | bytes 20987904 | tf_op jit(solution)/shard_map/tk,tn->kn/dot_general | solution.py:227
  653.5 18.5 %convolution_convert_fusion = bf16[4096,1024]{1,0:T(8,128)(2,1)} fusion(bf16[1024,1024]{1,0:T(8,128)(2,1)S(1)} %copy-done.26, f32[1024,4096]{1,0:T(8,128)} %fusion.31, f32[4096]{0:T(1024)S(1)} %bitcast.119), kind=kOutput, calls=%fused_computation.15 | convolution fusion | flops 8636071936 | bytes 27279360 | tf_op jit(solution)/shard_map/tk,tn->kn/dot_general | solution.py:227
  673.9 2.9 multiply_add_fusion.3
  680.8 11.4 multiply_add_fusion
  695.8 43.9 %reduce-scatter.19.cloned.1.call-done = bf16[64,1024]{1,0:T(8,128)(2,1)} async-done(((bf16[1024,1024]{1,0:T(8,128)(2,1)}), bf16[64,1024]{1,0:T(8,128)(2,1)}) %reduce-scatter.19.cloned.1.call-update) | async-done | bytes 131088 | tf_op jit(solution)/shard_map/reduce_scatter | solution.py:580
  739.7 76.0 %reduce-scatter.17.cloned.1.call-done = bf16[64,2048]{1,0:T(8,128)(2,1)} async-done(((bf16[1024,2048]{1,0:T(8,128)(2,1)}), bf16[64,2048]{1,0:T(8,128)(2,1)}) %reduce-scatter.17.cloned.1.call-update) | async-done | bytes 262160 | tf_op jit(solution)/shard_map/reduce_scatter | solution.py:580
  815.7 88.2 %reduce-scatter.11.cloned.1.call-done = bf16[64,3072]{1,0:T(8,128)(2,1)} async-done(((bf16[1024,3072]{1,0:T(8,128)(2,1)}), bf16[64,3072]{1,0:T(8,128)(2,1)}) %reduce-scatter.11.cloned.1.call-update) | async-done | bytes 393232 | tf_op jit(solution)/shard_map/reduce_scatter | solution.py:580
  903.9 108.4 %reduce-scatter.21.cloned.1.call-done = bf16[64,4096]{1,0:T(8,128)(2,1)} async-done(((bf16[1024,4096]{1,0:T(8,128)(2,1)}), bf16[64,4096]{1,0:T(8,128)(2,1)}) %reduce-scatter.21.cloned.1.call-update) | async-done | bytes 524304 | tf_op jit(solution)/shard_map/reduce_scatter | solution.py:580
  1012.3 108.8 %reduce-scatter.23.cloned.1.call-done = bf16[256,1024]{1,0:T(8,128)(2,1)} async-done(((bf16[4096,1024]{1,0:T(8,128)(2,1)}), bf16[256,1024]{1,0:T(8,128)(2,1)}) %reduce-scatter.23.cloned.1.call-update) | async-done | bytes 524304 | tf_op jit(solution)/shard_map/reduce_scatter | solution.py:580
  1121.2 7.6 fusion.47
  1133.4 32.6 %all-reduce = bf16[4096]{0:T(1024)(128)(2,1)S(1)} all-reduce(bf16[4096]{0:T(1024)(128)(2,1)S(1)} %copy-done.55), channel_id=9, replica_groups=mesh['batch'=16,'blk'=2] {'batch'}, use_global_device_ids=true, to_apply=%region_27.28.clone | all-reduce | flops 4096 | bytes 16384
  1166.1 14.5 %reduce-scatter.25.cloned.1.call-done = bf16[64,7]{1,0:T(8,128)(2,1)} async-done(((bf16[1024,7]{1,0:T(8,128)(2,1)}), bf16[64,7]{1,0:T(8,128)(2,1)}) %reduce-scatter.25.cloned.1.call-update) | async-done | bytes 912
  1181.4 4.9 all-reduce.1
  1201.1 45.3 %all-reduce.5.cloned.1.call-done = (bf16[64,3072]{1,0:T(8,128)(2,1)}, bf16[64,1024]{1,0:T(8,128)(2,1)}, bf16[64,1024]{1,0:T(8,128)(2,1)}, bf16[64,2048]{1,0:T(8,...) async-done(((bf16[64,3072]{1,0:T(8,128)(2,1)}, bf16[64,1024]{1,0:T(8,128)(2,1)}, bf16[64,1024]{1,0:T(8,128)(2,1)}, ...) | async-done | bytes 2097168 | tf_op jit(solution)/shard_map/psum | solution.py:583
  (251 shorter events, 88.2 us)
Async XLA Ops:
  7.2 10.2 copy-start.49
  7.2 10.2 copy-start.50
  7.2 15.6 %copy-start.58 = (bf16[4,64]{1,0:T(4,128)(2,1)S(1)}, bf16[4,64]{1,0:T(4,128)(2,1)}, u32[]{:S(2)}) copy-start(bf16[4,64]{1,0:T(4,128)(2,1)} %param.29) | copy-start | bytes 1540
  7.2 15.6 %copy-start.59 = (bf16[3,64]{1,0:T(4,128)(2,1)S(1)}, bf16[3,64]{1,0:T(4,128)(2,1)}, u32[]{:S(2)}) copy-start(bf16[3,64]{1,0:T(4,128)(2,1)} %param.28) | copy-start | bytes 1156
  7.2 82.5 %all-gather.16.cloned.1.call-start = ((), (), s32[]{:S(2)}) async-start(), calls=%async_computation.11 | async-start | bytes 4456448 | tf_op jit(solution)/shard_map/all_gather | solution.py:576
  8.0 38.0 %copy-start.63 = (bf16[256]{0:T(256)(128)(2,1)S(1)}, bf16[256]{0:T(256)(128)(2,1)}, u32[]{:S(2)}) copy-start(bf16[256]{0:T(256)(128)(2,1)} %param.27) | copy-start | bytes 1540
  8.0 118.3 %all-gather.10.cloned.1.call-start = ((), (), s32[]{:S(2)}) async-start(), calls=%async_computation.8 | async-start | bytes 6684672 | tf_op jit(solution)/shard_map/all_gather | solution.py:576
  8.7 159.8 %all-gather.12.cloned.1.call-start = ((), (), s32[]{:S(2)}) async-start(), calls=%async_computation.9 | async-start | bytes 2228224 | tf_op jit(solution)/shard_map/all_gather | solution.py:576
  9.4 201.3 %all-gather.14.cloned.1.call-start = ((), (), s32[]{:S(2)}) async-start(), calls=%async_computation.10 | async-start | bytes 2228224 | tf_op jit(solution)/shard_map/all_gather | solution.py:576
  10.0 242.9 %all-gather.18.cloned.1.call-start = ((), (), s32[]{:S(2)}) async-start(), calls=%async_computation.12 | async-start | bytes 2228224 | tf_op jit(solution)/shard_map/all_gather | solution.py:576
  10.6 53.6 %copy-start.23 = (bf16[2,512,1024]{2,1,0:T(8,128)(2,1)S(1)}, bf16[2,512,1024]{2,1,0:T(8,128)(2,1)}, u32[]{:S(2)}) copy-start(bf16[2,512,1024]{2,1,0:T(8,128)(2,1)} %param.15) | copy-start | bytes 6291460
  10.6 318.1 %all-gather.20.cloned.1.call-start = ((), (), s32[]{:S(2)}) async-start(), calls=%async_computation.13 | async-start | bytes 8912896 | tf_op jit(solution)/shard_map/all_gather | solution.py:576
  11.2 392.8 %all-gather.22.cloned.1.call-start = ((), (), s32[]{:S(2)}) async-start(), calls=%async_computation.14 | async-start | bytes 8912896 | tf_op jit(solution)/shard_map/all_gather | solution.py:576
  11.9 683.9 %reduce-scatter.13.cloned.1.call-start = ((), (), s32[]{:S(2)}) async-start(), calls=%async_computation.16 | async-start | bytes 2228224 | tf_op jit(solution)/shard_map/reduce_scatter | solution.py:580
  12.0 9.8 copy-start.27
  14.4 49.7 %collective-permute-start = (bf16[1,512,1024]{2,1,0:T(8,128)(2,1)}, bf16[1,512,1024]{2,1,0:T(8,128)(2,1)}, u32[]{:S(2)}, u32[]{:S(2)}) collective-permute-start(bf16[1,512,1024]{2,1,0:T(8,128)(2,1)} %constant_dynamic-slice_fusion.2), channel_id=1, source_target_pairs={{0,1},{1,0},{2,3},{3,2},{4,5},{5,4},{6,7},{7,6},{8,9},{9,8},{10,11... | collective-permute-start | bytes 3145736 | tf_op jit(solution)/shard_map/ppermute | solution.py:535
  17.4 46.1 %collective-permute-start.1 = (s32[1,512,2]{1,0,2:T(1,128)S(1)}, s32[1,512,2]{1,0,2:T(1,128)S(1)}, u32[]{:S(2)}, u32[]{:S(2)}) collective-permute-start(s32[1,512,2]{1,0,2:T(1,128)S(1)} %fusion.21), channel_id=1, source_target_pairs={{0,1},{1,0},{2,3},{3,2},{4,5},{5,4},{6,7},{7,6},{8,9},{9,8},{10,11... | collective-permute-start | bytes 12296 | tf_op jit(solution)/shard_map/ppermute | solution.py:535
  19.8 47.3 %collective-permute-start.2 = (bf16[1,512,1024]{2,1,0:T(8,128)(2,1)}, bf16[1,512,1024]{2,1,0:T(8,128)(2,1)}, u32[]{:S(2)}, u32[]{:S(2)}) collective-permute-start(bf16[1,512,1024]{2,1,0:T(8,128)(2,1)} %constant_dynamic-slice_fusion.1), channel_id=1, source_target_pairs={{0,1},{1,0},{2,3},{3,2},{4,5},{5,4},{6,7},{7,6},{8,9},{9,8},{10,11... | collective-permute-start | bytes 3145736 | tf_op jit(solution)/shard_map/ppermute | solution.py:535
  22.8 63.1 %collective-permute-start.4 = (bf16[1,512,1024]{2,1,0:T(8,128)(2,1)}, bf16[1,512,1024]{2,1,0:T(8,128)(2,1)}, u32[]{:S(2)}, u32[]{:S(2)}) collective-permute-start(bf16[1,512,1024]{2,1,0:T(8,128)(2,1)} %constant_dynamic-slice_fusion), channel_id=1, source_target_pairs={{0,1},{1,0},{2,3},{3,2},{4,5},{5,4},{6,7},{7,6},{8,9},{9,8},{10,11... | collective-permute-start | bytes 3145736 | tf_op jit(solution)/shard_map/ppermute | solution.py:535
  46.0 207.0 %copy-start.56 = (f32[1,1024]{1,0:T(1,128)}, f32[1,1024]{1,0:T(1,128)S(1)}, u32[]{:S(2)}) copy-start(f32[1,1024]{1,0:T(1,128)S(1)} %get-tuple-element.81) | copy-start | bytes 12292
  46.0 382.9 %copy-start.42 = (f32[1,1024]{1,0:T(1,128)}, f32[1,1024]{1,0:T(1,128)S(1)}, u32[]{:S(2)}) copy-start(f32[1,1024]{1,0:T(1,128)S(1)} %get-tuple-element.76) | copy-start | bytes 12292
  64.1 74.6 %copy-start.1 = (bf16[1024,128]{1,0:T(8,128)(2,1)}, bf16[1024,128]{1,0:T(8,128)(2,1)S(1)}, u32[]{:S(2)}) copy-start(bf16[1024,128]{1,0:T(8,128)(2,1)S(1)} %get-tuple-element.86.fk_ref) | copy-start | bytes 786436
  64.2 21.7 %copy-start.28 = (bf16[2,512,1024]{2,1,0:T(8,128)(2,1)S(1)}, bf16[2,512,1024]{2,1,0:T(8,128)(2,1)}, u32[]{:S(2)}) copy-start(bf16[2,512,1024]{2,1,0:T(8,128)(2,1)} %param.19) | copy-start | bytes 6291460
  89.7 36.6 %copy-start.31 = (bf16[1,512,1024]{2,1,0:T(8,128)(2,1)S(1)}, bf16[1,512,1024]{2,1,0:T(8,128)(2,1)}, u32[]{:S(2)}) copy-start(bf16[1,512,1024]{2,1,0:T(8,128)(2,1)} %get-tuple-element.74) | copy-start | bytes 3145732
  89.7 36.6 %copy-start.33 = (bf16[1,512,1024]{2,1,0:T(8,128)(2,1)S(1)}, bf16[1,512,1024]{2,1,0:T(8,128)(2,1)}, u32[]{:S(2)}) copy-start(bf16[1,512,1024]{2,1,0:T(8,128)(2,1)} %get-tuple-element.75) | copy-start | bytes 3145732
  175.7 40.3 %copy-start.46 = (f32[1024]{0:T(1024)}, f32[1024]{0:T(1024)S(1)}, u32[]{:S(2)}) copy-start(f32[1024]{0:T(1024)S(1)} %multiply_reduce_fusion.6) | copy-start | bytes 12292
  216.0 35.6 %copy-start = (bf16[1024,1024]{1,0:T(8,128)(2,1)}, bf16[1024,1024]{1,0:T(8,128)(2,1)S(1)}, u32[]{:S(2)}) copy-start(bf16[1024,1024]{1,0:T(8,128)(2,1)S(1)} %convolution_convert_fusion.11.q_ref) | copy-start | bytes 6291460
  423.0 8.6 copy-start.44
  434.8 25.4 %copy-start.25 = (bf16[1024,1024]{1,0:T(8,128)(2,1)}, bf16[1024,1024]{1,0:T(8,128)(2,1)S(1)}, u32[]{:S(2)}) copy-start(bf16[1024,1024]{1,0:T(8,128)(2,1)S(1)} %get-tuple-element.51) | copy-start | bytes 6291460
  460.2 18.2 %copy-start.11 = (f32[1024,1024]{1,0:T(8,128)S(1)}, f32[1024,1024]{1,0:T(8,128)}, u32[]{:S(2)}) copy-start(f32[1024,1024]{1,0:T(8,128)} %copy-done.10) | copy-start | bytes 12582916
  481.9 57.7 %copy-start.18 = (f32[1024,1024]{1,0:T(8,128)}, f32[1024,1024]{1,0:T(8,128)S(1)}, u32[]{:S(2)}) copy-start(f32[1024,1024]{1,0:T(8,128)S(1)} %get-tuple-element.59) | copy-start | bytes 12582916
  485.6 54.0 %copy-start.13 = (f32[1024,1024]{1,0:T(8,128)S(1)}, f32[1024,1024]{1,0:T(8,128)}, u32[]{:S(2)}) copy-start(f32[1024,1024]{1,0:T(8,128)} %copy-done.12) | copy-start | bytes 12582916
  485.6 54.0 %copy-start.61 = (bf16[1024,1024]{1,0:T(8,128)(2,1)S(1)}, bf16[1024,1024]{1,0:T(8,128)(2,1)}, u32[]{:S(2)}) copy-start(bf16[1024,1024]{1,0:T(8,128)(2,1)} %all-gather.14.cloned.1.call-done) | copy-start | bytes 6291460
  550.7 7.6 copy-start.4
  550.8 145.1 %reduce-scatter.15.cloned.1.call-start = ((), (), s32[]{:S(2)}) async-start(), calls=%async_computation.17 | async-start | bytes 2228224 | tf_op jit(solution)/shard_map/reduce_scatter | solution.py:580
  558.3 181.4 %reduce-scatter.19.cloned.1.call-start = ((), (), s32[]{:S(2)}) async-start(), calls=%async_computation.19 | async-start | bytes 2228224 | tf_op jit(solution)/shard_map/reduce_scatter | solution.py:580
  564.5 251.3 %reduce-scatter.17.cloned.1.call-start = ((), (), s32[]{:S(2)}) async-start(), calls=%async_computation.18 | async-start | bytes 4456448 | tf_op jit(solution)/shard_map/reduce_scatter | solution.py:580
  575.3 7.5 copy-start.2
  575.3 328.6 %reduce-scatter.11.cloned.1.call-start = ((), (), s32[]{:S(2)}) async-start(), calls=%async_computation.15 | async-start | bytes 6684672 | tf_op jit(solution)/shard_map/reduce_scatter | solution.py:580
  636.1 376.3 %reduce-scatter.21.cloned.1.call-start = ((), (), s32[]{:S(2)}) async-start(), calls=%async_computation.20 | async-start | bytes 8912896 | tf_op jit(solution)/shard_map/reduce_scatter | solution.py:580
  651.9 469.3 %reduce-scatter.23.cloned.1.call-start = ((), (), s32[]{:S(2)}) async-start(), calls=%async_computation.21 | async-start | bytes 8912896 | tf_op jit(solution)/shard_map/reduce_scatter | solution.py:580
  672.0 508.6 %reduce-scatter.25.cloned.1.call-start = ((), (), s32[]{:S(2)}) async-start(), calls=%async_computation.22 | async-start | bytes 278528
  677.9 510.1 %collective-permute-start.3 = (bf16[1,512,1024]{2,1,0:T(8,128)(2,1)}, bf16[1,512,1024]{2,1,0:T(8,128)(2,1)S(1)}, u32[]{:S(2)}, u32[]{:S(2)}) collective-permute-start(bf16[1,512,1024]{2,1,0:T(8,128)(2,1)} %fusion.17), channel_id=1, source_target_pairs={{0,1},{1,0},{2,3},{3,2},{4,5},{5,4},{6,7},{7,6},{8,9},{9,8},{10,11... | collective-permute-start | bytes 3145736 | tf_op jit(solution)/shard_map/ppermute | solution.py:535
  680.5 566.0 %all-reduce.5.cloned.1.call-start = ((), (), s32[]{:S(2)}) async-start(), calls=%async_computation.23 | async-start | bytes 4194304 | tf_op jit(solution)/shard_map/psum | solution.py:583
  695.4 494.4 %collective-permute-start.5 = (bf16[1,512,1024]{2,1,0:T(8,128)(2,1)}, bf16[1,512,1024]{2,1,0:T(8,128)(2,1)}, u32[]{:S(2)}, u32[]{:S(2)}) collective-permute-start(bf16[1,512,1024]{2,1,0:T(8,128)(2,1)} %fusion.18), channel_id=1, source_target_pairs={{0,1},{1,0},{2,3},{3,2},{4,5},{5,4},{6,7},{7,6},{8,9},{9,8},{10,11... | collective-permute-start | bytes 3145736 | tf_op jit(solution)/shard_map/ppermute | solution.py:535
  1121.2 12.2 copy-start.55
  1131.9 63.6 %collective-permute-start.6 = (bf16[1,512,1024]{2,1,0:T(8,128)(2,1)}, bf16[1,512,1024]{2,1,0:T(8,128)(2,1)}, u32[]{:S(2)}, u32[]{:S(2)}) collective-permute-start(bf16[1,512,1024]{2,1,0:T(8,128)(2,1)} %fusion.19), channel_id=1, source_target_pairs={{0,1},{1,0},{2,3},{3,2},{4,5},{5,4},{6,7},{7,6},{8,9},{9,8},{10,11... | collective-permute-start | bytes 3145736 | tf_op jit(solution)/shard_map/ppermute | solution.py:535
  1246.4 10.7 copy-start.39
  (40 other events, 122.6 us)
Sparse Core Ops, SparseCore 0:
  10.2 53.3 all-gather.15
  65.9 60.3 all-gather.9
  128.5 40.0 all-gather.11
  170.5 40.1 all-gather.13
  212.8 40.1 all-gather.17
  255.0 73.6 all-gather.19
  330.8 73.1 all-gather.21
  550.9 59.8 reduce-scatter.12
  614.9 60.5 reduce-scatter.14
  679.1 60.5 reduce-scatter.18
  744.1 71.6 reduce-scatter.16
  819.5 84.3 reduce-scatter.10
  908.5 103.7 reduce-scatter.20
  1016.8 104.3 reduce-scatter.22
  1125.5 55.0 reduce-scatter.24
  1183.4 63.0 all-reduce.4

commit v2 on v1

--- a/solution.py
+++ b/solution.py
@@ -160,45 +160,201 @@
     return pl.BlockSpec((length, PAIR), lambda j: (0, 0))
 
 
-def attention_forward(q_src, q_at, kv_src, k_at, v_at, fq, fk, causal):
-    length, mem = q_src.shape[0], kv_src.shape[0]
-    pairs = NH // 2
+SHORT = pl.CostEstimate(flops=1024, bytes_accessed=1024, transcendentals=0)
+
+
+def attention_call(kernel, name, pairs, causal, arrays, shared, outs, scratch, into):
+    first, count = pairs
+    into = [] if into is None else list(into)
+
+    def body(*refs):
+        kernel(causal, *refs[: len(arrays) + 2], *refs[len(arrays) + 2 + len(into) :])
+
     return pl.pallas_call(
-        functools.partial(attention_fwd_kernel, causal),
-        grid=(pairs,),
-        in_specs=[cols(length, q_at), cols(mem, k_at), cols(mem, v_at), whole(length), whole(mem)],
-        out_specs=[cols(length, 0), cols(length, 0)],
+        body,
+        grid=(count,),
+        in_specs=[cols(a.shape[0], first) for a in arrays[:3]]
+        + [whole(a.shape[0]) for a in shared]
+        + [cols(a.shape[0], first) for a in arrays[3:]]
+        + [pl.BlockSpec(memory_space=pl.ANY)] * len(into),
+        out_specs=[cols(o.shape[0], first) for o in outs],
+        out_shape=outs,
+        scratch_shapes=scratch,
+        input_output_aliases={len(arrays) + 2 + n: n for n in range(len(into))},
+        compiler_params=pltpu.CompilerParams(vmem_limit_bytes=48 * 2**20),
+        cost_estimate=SHORT,
+        name=name,
+    )(*arrays[:3], *shared, *arrays[3:], *into)
+
+
+def attention_forward(queries, keys, values, fq, fk, causal, pairs, into):
+    length = queries.shape[0]
+    outs = [
+        jax.ShapeDtypeStruct(queries.shape, jnp.bfloat16),
+        jax.ShapeDtypeStruct(queries.shape, jnp.float32),
+    ]
+    arrays = (queries, keys, values)
+    return attention_call(
+        attention_fwd_kernel, "attention_forward", pairs, causal, arrays, (fq, fk), outs, [], into
+    )
+
+
+def attention_backward(fq, fk, queries, keys, values, mixed, lse, d_mixed, causal, pairs, into):
+    length, mem = queries.shape[0], keys.shape[0]
+    outs = [jax.ShapeDtypeStruct(a.shape, jnp.bfloat16) for a in (queries, keys, values)]
+    scratch = [
+        pltpu.VMEM((mem, PAIR), jnp.float32),
+        pltpu.VMEM((mem, PAIR), jnp.float32),
+        pltpu.VMEM((PAIR, length), jnp.float32),
+    ]
+    arrays = (queries, keys, values, mixed, lse, d_mixed)
+    return attention_call(
+        attention_bwd_kernel,
+        "attention_backward",
+        pairs,
+        causal,
+        arrays,
+        (fq, fk),
+        outs,
+        scratch,
+        into,
+    )
+
+
+def gelu_kernel(left_ref, right_ref, bias_ref, hidden_ref, slope_ref):
+    slope_in = 0.7978845608028654
+    right = right_ref[...].reshape(-1, right_ref.shape[-1])
+    bias = bias_ref[...]
+    step = min(256, left_ref.shape[0])
+    for first in range(0, left_ref.shape[0], step):
+        rows = slice(first, first + step)
+        pre = nn(left_ref[rows, :], right) + bias
+        square = pre * pre
+        bent = jnp.tanh(slope_in * (pre + 0.044715 * (square * pre)))
+        gate = 0.5 * (1.0 + bent)
+        hidden_ref[rows, :] = (pre * gate).astype(hidden_ref.dtype)
+        bend = (1.0 - bent * bent) * (slope_in + (slope_in * 0.134145) * square)
+        slope_ref[rows, :] = gate + (0.5 * pre) * bend
+
+
+def gelu_rows(left, ffn, bias):
+    rows, inner = left.shape
+    count, parts, tall_shard, wide = ffn.shape
+    columns = wide * parts // 2
+    tall = min(rows, 1024)
+    return pl.pallas_call(
+        gelu_kernel,
+        grid=(rows // tall, parts // 2),
+        in_specs=[
+            pl.BlockSpec((tall, inner), lambda i, j: (i, 0)),
+            pl.BlockSpec((count, 1, tall_shard, wide), lambda i, j: (0, j, 0, 0)),
+            pl.BlockSpec((1, wide), lambda i, j: (0, j)),
+        ],
+        out_specs=[pl.BlockSpec((tall, wide), lambda i, j: (i, j))] * 2,
         out_shape=[
-            jax.ShapeDtypeStruct((length, D), jnp.bfloat16),
-            jax.ShapeDtypeStruct((length, D), jnp.float32),
+            jax.ShapeDtypeStruct((rows, columns), jnp.bfloat16),
+            jax.ShapeDtypeStruct((rows, columns), jnp.float32),
+        ],
+        compiler_params=pltpu.CompilerParams(vmem_limit_bytes=56 * 2**20),
+        cost_estimate=SHORT,
+        name="gelu_rows",
+    )(left, ffn, bias.reshape(1, columns))
+
+
+def down_kernel(left_ref, right_ref, out_ref):
+    right = right_ref[...].reshape(-1, right_ref.shape[-1])
+    out_ref[...] = nn(left_ref[...], right)
+
+
+def down_rows(left, ffn):
+    rows, inner = left.shape
+    count, parts, tall_shard, columns = ffn.shape
+    tall, wide = min(rows, 1024), 256
+    return pl.pallas_call(
+        down_kernel,
+        grid=(rows // tall, columns // wide),
+        in_specs=[
+            pl.BlockSpec((tall, inner), lambda i, j: (i, 0)),
+            pl.BlockSpec((count, parts // 2, tall_shard, wide), lambda i, j: (0, 1, 0, j)),
+        ],
+        out_specs=pl.BlockSpec((tall, wide), lambda i, j: (i, j)),
+        out_shape=jax.ShapeDtypeStruct((rows, columns), jnp.float32),
+        compiler_params=pltpu.CompilerParams(vmem_limit_bytes=48 * 2**20),
+        cost_estimate=SHORT,
+        name="down_rows",
+    )(left, ffn)
+
+
+def up_back_kernel(left_ref, right_ref, out_ref):
+    _, parts, _, wide = right_ref.shape
+    total = None
+    for n in range(parts):
+        right = right_ref[:, n].reshape(-1, wide)
+        part = nt(left_ref[:, n * wide : (n + 1) * wide], right)
+        total = part if total is None else total + part
+    out_ref[...] = total
+
+
+def up_back_rows(left, ffn):
+    rows, inner = left.shape
+    count, parts, tall_shard, wide = ffn.shape
+    tall, group = min(rows, 1024), 4
+    return pl.pallas_call(
+        up_back_kernel,
+        grid=(rows // tall, count // group),
+        in_specs=[
+            pl.BlockSpec((tall, inner), lambda i, j: (i, 0)),
+            pl.BlockSpec((group, parts // 2, tall_shard, wide), lambda i, j: (j, 0, 0, 0)),
+        ],
+        out_specs=pl.BlockSpec((tall, group * tall_shard), lambda i, j: (i, j)),
+        out_shape=jax.ShapeDtypeStruct((rows, count * tall_shard), jnp.float32),
+        compiler_params=pltpu.CompilerParams(vmem_limit_bytes=48 * 2**20),
+        cost_estimate=SHORT,
+        name="up_back_rows",
+    )(left, ffn)
+
+
+def gelu_back_kernel(left_ref, right_ref, slope_ref, out_ref, sum_ref):
+    right = right_ref[...].reshape(-1, right_ref.shape[-1])
+    step = min(256, left_ref.shape[0])
+    total = None
+    for first in range(0, left_ref.shape[0], step):
+        rows = slice(first, first + step)
+        d_hidden = nt(left_ref[rows, :], right).astype(jnp.bfloat16).astype(jnp.float32)
+        d_pre = (d_hidden * slope_ref[rows, :]).astype(jnp.bfloat16)
+        out_ref[rows, :] = d_pre
+        part = jnp.sum(d_pre.astype(jnp.float32), axis=0, keepdims=True)
+        total = part if total is None else total + part
+    sum_ref[...] = total[None]
+
+
+def gelu_back_rows(left, ffn, slope):
+    rows, inner = left.shape
+    count, parts, tall_shard, _ = ffn.shape
+    columns = count * parts // 2 * tall_shard
+    tall, group = min(rows, 1024), 2
+    wide = group * parts // 2 * tall_shard
+    out, sums = pl.pallas_call(
+        gelu_back_kernel,
+        grid=(rows // tall, columns // wide),
+        in_specs=[
+            pl.BlockSpec((tall, inner), lambda i, j: (i, 0)),
+            pl.BlockSpec((group, parts // 2, tall_shard, inner), lambda i, j: (j, 1, 0, 0)),
+            pl.BlockSpec((tall, wide), lambda i, j: (i, j)),
+        ],
+        out_specs=[
+            pl.BlockSpec((tall, wide), lambda i, j: (i, j)),
+            pl.BlockSpec((1, 1, wide), lambda i, j: (i, 0, j)),
+        ],
+        out_shape=[
+            jax.ShapeDtypeStruct((rows, columns), jnp.bfloat16),
+            jax.ShapeDtypeStruct((rows // tall, 1, columns), jnp.float32),
         ],
         compiler_params=pltpu.CompilerParams(vmem_limit_bytes=48 * 2**20),
-        name="attention_forward",
-    )(q_src, kv_src, kv_src, fq, fk)
-
-
-def attention_backward(q_src, q_at, kv_src, k_at, v_at, fq, fk, mixed, lse, d_mixed, causal):
-    length, mem = q_src.shape[0], kv_src.shape[0]
-    pairs = NH // 2
-    return pl.pallas_call(
-        functools.partial(attention_bwd_kernel, causal),
-        grid=(pairs,),
-        in_specs=[cols(length, q_at), cols(mem, k_at), cols(mem, v_at), whole(length), whole(mem),
-                  cols(length, 0), cols(length, 0), cols(length, 0)],
-        out_specs=[cols(length, 0), cols(mem, 0), cols(mem, 0)],
-        out_shape=[
-            jax.ShapeDtypeStruct((length, D), jnp.bfloat16),
-            jax.ShapeDtypeStruct((mem, D), jnp.bfloat16),
-            jax.ShapeDtypeStruct((mem, D), jnp.bfloat16),
-        ],
-        scratch_shapes=[
-            pltpu.VMEM((mem, PAIR), jnp.float32),
-            pltpu.VMEM((mem, PAIR), jnp.float32),
-            pltpu.VMEM((PAIR, length), jnp.float32),
-        ],
-        compiler_params=pltpu.CompilerParams(vmem_limit_bytes=48 * 2**20),
-        name="attention_backward",
-    )(q_src, kv_src, kv_src, fq, fk, mixed, lse, d_mixed)
+        cost_estimate=SHORT,
+        name="gelu_back_rows",
+    )(left, ffn, slope)
+    return out, jnp.sum(sums, axis=(0, 1))
 
 
 def document_features(query_ids, key_ids):
@@ -583,12 +739,369 @@
     return lax.psum(part, "blk").astype(jnp.float32)
 
 
-def each_row(function, rows, *arrays):
+class Flight:
+    def __init__(self, steps):
+        self.steps = steps
+        self.result = None
+        self.wanted = next(steps)
+        self.pending = None
+
+    def launch(self):
+        self.pending = [send(array) for send, array in self.wanted]
+
+    def advance(self, arrived):
+        try:
+            self.wanted = self.steps.send(arrived)
+        except StopIteration as stop:
+            self.wanted, self.result = [], stop.value
+
+    def finish(self):
+        while self.result is None:
+            if self.pending is None:
+                self.launch()
+            self.advance(self.pending)
+            self.pending = None
+        return self.result
+
+
+def tick(value, *flights):
+    flying = [f for f in flights if f.result is None]
+    value, arrived = lax.optimization_barrier((value, [f.pending or [] for f in flying]))
+    for flight, got in zip(flying, arrived):
+        if flight.pending is not None:
+            flight.advance(got)
+    flying = [f for f in flying if f.result is None]
+    value, ready = lax.optimization_barrier((value, [[a for _, a in f.wanted] for f in flying]))
+    for flight, arrays in zip(flying, ready):
+        flight.wanted = [(send, a) for (send, _), a in zip(flight.wanted, arrays)]
+        flight.launch()
+    return value
+
+
+def grid_place():
+    batch = lax.axis_index("batch")
+    return batch // 4, batch // 2 % 2, batch % 2, lax.axis_index("blk")
+
+
+def z_sender(step):
+    return lambda array: to_z(array, step)
+
+
+def to_core(array):
+    return lax.ppermute(array, "batch", [(n, n ^ 1) for n in range(16)])
+
+
+def to_x(array):
+    return lax.ppermute(array, "batch", [(n, n ^ 2) for n in range(16)])
+
+
+def to_z(array, step):
+    return lax.ppermute(array, "batch", [(n, (n + 4 * step) % 16) for n in range(16)])
+
+
+def to_core_blk(array):
+    pairs = [(2 * n + m, 2 * (n ^ 1) + (1 - m)) for n in range(16) for m in range(2)]
+    return lax.ppermute(array, ("batch", "blk"), pairs)
+
+
+def piece(array, axis, at, size):
+    return lax.dynamic_slice_in_dim(array, at * size, size, axis)
+
+
+def summed_low(terms):
+    total = terms[0].astype(jnp.float32)
+    for term in terms[1:]:
+        total = total + term.astype(jnp.float32)
+    return total.astype(jnp.bfloat16)
+
+
+def in_order(at, own, other, axis):
+    first = jnp.where(at == 0, own, other)
+    second = jnp.where(at == 0, other, own)
+    return jnp.concatenate([first, second], axis=axis)
+
+
+FLIP = {"x": (0, 1, 0, 0), "c": (0, 0, 1, 0), "y": (0, 0, 0, 1)}
+SEND = {"x": to_x, "c": to_core, "y": swap_pair}
+
+
+def weight_gather(shards, path):
+    blk = lax.axis_index("blk")
+    if "y" in path:
+        shards = [piece(s, 1, blk, s.shape[1] // 2) for s in shards]
+    held = [(jnp.concatenate(shards, axis=1)[None], [(0, 0, 0, 0)])]
+    return (yield from gather_steps(held, [s.shape for s in shards], path, "y" in path))
+
+
+def gather_steps(held, shapes, path, split):
+    for axis in path:
+        if axis == "/":
+            (block, labels), count = held[0], (len(shapes) + 1) // 2
+            wide = sum(shape[1] for shape in shapes[:count])
+            ways = [
+                gather_steps([(block[:, :, :wide], labels)], shapes[:count], "yxc", split),
+                gather_steps([(block[:, :, wide:], labels)], shapes[count:], "xyc", split),
+            ]
+            return (yield from together(ways))
+        if axis == "z":
+            block = jnp.concatenate([a for a, _ in held], axis=0) if len(held) > 1 else held[0][0]
+            labels = sum((near for _, near in held), [])
+            got = yield [(z_sender(step), block) for step in (1, 2, 3)]
+            block = jnp.concatenate([block] + list(got), axis=0)
+            held = [(block, [(d, b, c, e) for d in range(4) for _, b, c, e in labels])]
+        else:
+            got = yield [(SEND[axis], a) for a, _ in held]
+            flip = FLIP[axis]
+            held = held + [
+                (g, [tuple(p + f for p, f in zip(label, flip)) for label in near])
+                for g, (_, near) in zip(got, held)
+            ]
+    return placed_blocks(held, shapes, split)
+
+
+def together(ways):
+    wanted = [next(way) for way in ways]
+    results = []
+    while not results:
+        got = yield sum(wanted, [])
+        for n, way in enumerate(ways):
+            mine, got = got[: len(wanted[n])], got[len(wanted[n]) :]
+            try:
+                wanted[n] = way.send(mine)
+            except StopIteration as stop:
+                results += stop.value
+    return results
+
+
+def place_kernel(near_lists, shapes, split, place, *refs):
+    sources, targets = refs[: len(near_lists)], refs[len(near_lists) :]
+    for source, near in zip(sources, near_lists):
+        for n, (dx, dc, dy) in enumerate(near):
+            row = (place[1] + dx) % 2 * 2 + (place[2] + dc) % 2
+            first = 0
+            for target, (tall, wide) in zip(targets, shapes):
+                at = pl.ds(pl.multiple_of(row * tall, tall), tall)
+                block = source[n, :, first : first + wide]
+                if split:
+                    side = (place[3] + dy) % 2
+                    target[at, pl.ds(pl.multiple_of(side * wide, wide), wide)] = block
+                else:
+                    target[at, :] = block
+                first += wide
+
+
+def placed_blocks(held, shapes, split):
+    place = jnp.stack(grid_place()).astype(jnp.int32)
+    counts = [len(near) // 4 for _, near in held]
+    near_lists = [[label[1:] for label in near[:n]] for n, (_, near) in zip(counts, held)]
+    outs = [(tall, wide * (2 if split else 1)) for tall, wide in shapes]
+    return pl.pallas_call(
+        functools.partial(place_kernel, near_lists, shapes, split),
+        grid_spec=pltpu.PrefetchScalarGridSpec(
+            num_scalar_prefetch=1,
+            grid=(4,),
+            in_specs=[
+                pl.BlockSpec((n,) + a.shape[1:], lambda d, p: (d, 0, 0))
+                for n, (a, _) in zip(counts, held)
+            ],
+            out_specs=[
+                pl.BlockSpec((4 * tall, wide), lambda d, p: ((p[0] + 4 - d) % 4, 0))
+                for tall, wide in outs
+            ],
+        ),
+        out_shape=[jax.ShapeDtypeStruct((tall * 16, wide), jnp.bfloat16) for tall, wide in outs],
+        compiler_params=pltpu.CompilerParams(vmem_limit_bytes=40 * 2**20),
+        cost_estimate=SHORT,
+        name="place_weights",
+    )(place, *[a for a, _ in held])
+
+
+def halves(terms, axis, at):
+    size = terms[0].shape[axis] // 2
+    return (
+        summed_low([piece(t, axis, 1 - at, size) for t in terms]),
+        [piece(t, axis, at, size) for t in terms],
+    )
+
+
+def joined_grads(products, at):
+    blocks = []
+    for left, rights in products:
+        halves_of = [piece(r, 1, at, r.shape[1] // 2) for r in rights]
+        right = halves_of[0] if len(rights) == 1 else jnp.concatenate(halves_of, axis=1)
+        blocks.append(weight_grad(left, right).astype(jnp.bfloat16))
+    return blocks[0] if len(blocks) == 1 else jnp.concatenate(blocks, axis=1)
+
+
+def gradient_reduce(products, path):
+    z, x, core, blk = grid_place()
+    given = joined_grads(products, 1 - core)
+    kept = joined_grads(products, core)
+    (got,) = yield [(to_core, given)]
+    rows, columns = kept.shape
+    terms = [t.reshape(4, 2, rows // 8, columns) for t in (kept, got)]
+    for axis in path:
+        if axis == "z":
+            out = []
+            for step in (1, 2, 3):
+                parts = [piece(t, 0, (z + step) % 4, 1) for t in terms]
+                out.append((z_sender(step), summed_low(parts)))
+            out = yield out
+            terms = [piece(t, 0, z, 1) for t in terms] + list(out)
+        else:
+            out, terms = halves(terms, 1, x) if axis == "x" else halves(terms, 3, blk)
+            out = yield [(to_x if axis == "x" else swap_pair, out)]
+            terms = terms + list(out)
+    total = summed_low(terms).reshape(rows // 8, columns // 2)
+    mine = piece(total, 0, core, rows // 16)
+    theirs = piece(total, 0, 1 - core, rows // 16)
+    from_blk, from_core, from_both = yield [
+        (swap_pair, mine),
+        (to_core, theirs),
+        (to_core_blk, theirs),
+    ]
+    near = in_order(blk, mine, from_blk, 1).astype(jnp.float32)
+    far = in_order(blk, from_core, from_both, 1).astype(jnp.float32)
+    left, right = jnp.where(core == 0, near, far), jnp.where(core == 0, far, near)
+    results, first = [], 0
+    for _, rights in products:
+        for wide in [r.shape[1] // 2 for r in rights]:
+            part = slice(first, first + wide)
+            results.append(jnp.concatenate([left[:, part], right[:, part]], axis=1))
+            first += wide
+    return results
+
+
+def over_batch(array):
+    return lax.psum_scatter(array, "batch", scatter_dimension=0, tiled=True)
+
+
+def whole_reduce(products):
+    grads = [weight_grad(left, right).astype(jnp.bfloat16) for left, right in products]
+    grad = grads[0] if len(grads) == 1 else jnp.concatenate(grads, axis=1)
+    if not on_small_slice():
+        yield []
+        return shared_out(grad)
+    (part,) = yield [(over_batch, grad)]
+    (got,) = yield [(swap_pair, part)]
+    return part.astype(jnp.float32) + got.astype(jnp.float32)
+
+
+def batch_sender(bit):
+    return lambda array: lax.ppermute(array, "batch", [(n, n ^ bit) for n in range(16)])
+
+
+def total_of_all(array):
+    for send in (to_core, to_x, swap_pair, batch_sender(4), batch_sender(8)):
+        (got,) = yield [(send, array)]
+        array = array + got
+    return array
+
+
+def small_gather(gains, shifts, bias):
+    packed = jnp.concatenate([gains, shifts, bias.reshape(-1, gains.shape[1])], axis=0)
+    place = jnp.arange(16)[:, None, None] == lax.axis_index("batch")
+    held = jnp.where(place, packed[None], jnp.zeros_like(packed)[None])
+    for bit in (1, 2, 4, 8):
+        (got,) = yield [(batch_sender(bit), held)]
+        held = held + got
+    rows = jnp.moveaxis(held[:, :7], 0, 1).reshape(7, -1)
+    return rows[:3], rows[3:], held[:, 7:].reshape(-1)
+
+
+def rows_in_steps(array):
+    if lax.axis_size("blk") != 2:
+        yield []
+        return rows_in(array)
+    here = array.shape[0] // 2
+    parts = array.reshape((2, here) + array.shape[1:])
+    me = lax.axis_index("blk")
+    (got,) = yield [(swap_pair, lax.dynamic_index_in_dim(parts, 1 - me, 0, keepdims=False))]
+    return in_order(me, lax.dynamic_index_in_dim(parts, me, 0, keepdims=False), got, 1)
+
+
+def rows_out_steps(array, kind):
+    if lax.axis_size("blk") != 2:
+        yield []
+        return rows_out(array, kind)
+    here, length = array.shape[:2]
+    parts = array.reshape((here, 2, length // 2) + array.shape[2:])
+    me = lax.axis_index("blk")
+    sent = lax.dynamic_index_in_dim(parts, 1 - me, 1, keepdims=False).astype(jnp.bfloat16)
+    (got,) = yield [(swap_pair, sent)]
+    kept = lax.dynamic_index_in_dim(parts, me, 1, keepdims=False).astype(kind)
+    return in_order(me, kept, got.astype(kind), 0)
+
+
+def plain_gather(shards):
+    yield []
+    return [gathered(s) for s in shards]
+
+
+def plain_small_gather(gains, shifts, bias):
+    yield []
+    return gathered(gains, 1), gathered(shifts, 1), gathered(bias)
+
+
+def plain_reduce(products):
+    yield []
+    return [
+        shared_out(weight_grad(left, right)) for left, rights in products for right in rights
+    ]
+
+
+def on_small_slice():
+    return lax.axis_size("batch") == 16 and lax.axis_size("blk") == 2
+
+
+def start_gather(shards, path):
+    return Flight(weight_gather(shards, path) if on_small_slice() else plain_gather(shards))
+
+
+def whole_gather(shard):
+    (full,) = yield [(gathered, shard)]
+    return [full]
+
+
+def start_whole_gather(shard):
+    return Flight(whole_gather(shard))
+
+
+def start_reduce(products, path):
+    return Flight(gradient_reduce(products, path) if on_small_slice() else plain_reduce(products))
+
+
+def start_small(gains, shifts, bias):
+    steps = small_gather if on_small_slice() else plain_small_gather
+    return Flight(steps(gains, shifts, bias))
+
+
+def small_reduce(rows, bias):
+    if not on_small_slice():
+        yield []
+        return shared_out(rows, 1), shared_out(bias)
+    packed = yield from total_of_all(jnp.concatenate([rows, bias.reshape(-1, D)], axis=0))
+    me = lax.axis_index("batch")
+    bias = packed[rows.shape[0] :].reshape(-1)
+    return (
+        piece(packed[: rows.shape[0]], 1, me, D // 16),
+        piece(bias, 0, me, bias.shape[0] // 16),
+    )
+
+
+def each_row(function, rows, arrays, into=None):
     if rows == 1:
-        return function(*arrays)
-    cut = [a.reshape((rows, a.shape[0] // rows) + a.shape[1:]) for a in arrays]
-    results = [function(*(c[n] for c in cut)) for n in range(rows)]
-    return tuple(jnp.concatenate(group, axis=0) for group in zip(*results))
+        return function(*arrays, into=into)
+
+    def cut(array, n):
+        size = array.shape[0] // rows
+        return array[n * size : (n + 1) * size]
+
+    results = []
+    for n in range(rows):
+        kept = None if into is None else [cut(a, n) for a in into]
+        results.append(function(*(cut(a, n) for a in arrays), into=kept))
+    return [jnp.concatenate(group, axis=0) for group in zip(*results)]
 
 
 def dot32(left, right):
@@ -613,136 +1126,157 @@
     shifts,
 ):
     low = jnp.bfloat16
-    x_rows = rows_in(inputs)
+    half = NH // 4
+    shard_rows = w_self_qkv.shape[0]
+    columns = [w_self_qkv, w_self_out, w_cross_q, w_cross_kv, w_cross_out]
+    columns += [gains.T, shifts.T, b_up.reshape(shard_rows, -1)]
+    spare = -sum(c.shape[1] for c in columns) % PAIR
+    columns.append(jnp.zeros((shard_rows, spare), low))
+    attn_full = gathered(jnp.concatenate(columns, axis=1))
+    at, fulls = 0, []
+    for wide in [D] * 8 + [c.shape[1] for c in columns[5:8]]:
+        fulls.append(attn_full[:, at : at + wide])
+        at += wide
+    qkv_full, (out_full, cross_q_full, mk_full, mv_full, cross_out_full) = fulls[:3], fulls[3:8]
+    gain_full = fulls[8].T.astype(jnp.float32)
+    shift_full = fulls[9].T.astype(jnp.float32)
+    bias_full = fulls[10].reshape(-1).astype(jnp.float32)
+    up_parts = jnp.moveaxis(w_up.reshape(shard_rows, -1, D), 1, 0)
+    ffn_shard = jnp.concatenate([up_parts, w_down.reshape(-1, shard_rows, D)], axis=0)
+    ffn_full = lax.all_gather(ffn_shard, "batch", axis=0)
+    x_rows = Flight(rows_in_steps(inputs))
+    ids = Flight(rows_in_steps(jnp.stack([target_ids, memory_ids], axis=2)))
+    memory = tick(memory, x_rows, ids)
+    memory_rows = Flight(rows_in_steps(memory))
+    cotangent = tick(cotangent, x_rows, ids, memory_rows)
+    cot_rows = Flight(rows_in_steps(cotangent))
+    x_rows = x_rows.finish()
     rows, length = x_rows.shape[:2]
     x_flat = x_rows.reshape(-1, D)
-    memory_flat = rows_in(memory).reshape(-1, D)
-    ids = rows_in(jnp.stack([target_ids, memory_ids], axis=2))
+    ids = ids.finish()
     target_flat = ids[:, :, 0].reshape(-1)
     memory_id_flat = ids[:, :, 1].reshape(-1)
-    cot_flat = rows_in(cotangent).reshape(-1, D).astype(jnp.float32)
-
-    qkv_full = gathered(w_self_qkv)
-    out_full = gathered(w_self_out)
-    cross_q_full = gathered(w_cross_q)
-    cross_kv_full = gathered(w_cross_kv)
-    cross_out_full = gathered(w_cross_out)
-    up_full = gathered(w_up)
-    down_full = gathered(w_down)
-    small = gathered(jnp.concatenate([gains, shifts], axis=0), 1).astype(jnp.float32)
-    gain_full, shift_full = small[:3], small[3:]
-    bias_full = gathered(b_up).astype(jnp.float32)
-
-    projected = dot32(x_flat, qkv_full).astype(low)
-
-    def self_forward(rows_proj, rows_ids):
-        fq, fk = document_features(rows_ids, rows_ids)
-        return attention_forward(rows_proj, 0, rows_proj, 8, 16, fq, fk, True)
-
-    mixed_flat, self_lse = each_row(self_forward, rows, projected, target_flat)
+    memory_flat = memory_rows.finish().reshape(-1, D)
+
+    def self_forward(q, k, v, id_row, into, pairs):
+        fq, fk = document_features(id_row, id_row)
+        return attention_forward(q, k, v, fq, fk, True, pairs, into)
+
+    qkv = [dot32(x_flat, w).astype(low) for w in qkv_full]
+    mixed_flat, self_lse = each_row(
+        functools.partial(self_forward, pairs=(0, 2 * half)), rows, (*qkv, target_flat)
+    )
     first_sum = ALPHA * x_flat.astype(jnp.float32) + dot32(mixed_flat, out_full)
     first = layer_norm(first_sum, gain_full[0], shift_full[0])
     first_low = first.astype(low)
     cross_queries = dot32(first_low, cross_q_full).astype(low)
-    memory_pairs = dot32(memory_flat, cross_kv_full).astype(low)
-
-    def cross_forward(rows_q, rows_kv, rows_ids, rows_memory_ids):
-        fq, fk = document_features(rows_ids, rows_memory_ids)
-        return attention_forward(rows_q, 0, rows_kv, 0, 8, fq, fk, False)
-
-    cross_flat, cross_lse = each_row(
-        cross_forward, rows, cross_queries, memory_pairs, target_flat, memory_id_flat
-    )
+    cross_queries = tick(cross_queries, cot_rows)
+    memory_keys = dot32(memory_flat, mk_full).astype(low)
+    memory_values = dot32(memory_flat, mv_full).astype(low)
+
+    def cross_forward(q, k, v, id_row, memory_id_row, into, pairs):
+        fq, fk = document_features(id_row, memory_id_row)
+        return attention_forward(q, k, v, fq, fk, False, pairs, into)
+
+    arrays = (cross_queries, memory_keys, memory_values, target_flat, memory_id_flat)
+    mixed = each_row(functools.partial(cross_forward, pairs=(0, 2 * half)), rows, arrays)
+    cross_flat, cross_lse = tick(mixed, cot_rows)
     second_sum = ALPHA * first + dot32(cross_flat, cross_out_full)
     second = layer_norm(second_sum, gain_full[1], shift_full[1])
     second_low = second.astype(low)
-    hidden_pre = dot32(second_low, up_full) + bias_full
-    hidden_low = jax.nn.gelu(hidden_pre).astype(low)
-    third_sum = ALPHA * second + dot32(hidden_low, down_full) + shift_full[3]
+    hidden_low, slope = gelu_rows(second_low, ffn_full, bias_full)
+    cot_flat = cot_rows.finish().reshape(-1, D)
+    third_sum = ALPHA * second + down_rows(hidden_low, ffn_full) + shift_full[3]
     result, third_back = jax.vjp(layer_norm, third_sum, gain_full[2], shift_full[2])
-    output = rows_out(result.reshape(rows, length, D), low)
-
-    d_third, d_gain_three, d_shift_three = third_back(cot_flat)
+
+    d_third, d_gain_three, d_shift_three = third_back(cot_flat.astype(jnp.float32))
     d_branch_three = d_third.astype(low)
-    grad_down = shared_out(weight_grad(hidden_low, d_branch_three))
+    output = Flight(rows_out_steps(result.reshape(rows, length, D), low))
+    down_grad = Flight(whole_reduce([(hidden_low, d_branch_three)]))
+    d_branch_three, d_third = tick((d_branch_three, d_third), output, down_grad)
     grad_bias_down = jnp.sum(d_branch_three.astype(jnp.float32), axis=0)
-    d_hidden = back_prod(d_branch_three, down_full).astype(low)
-    gelu_back = jax.vjp(jax.nn.gelu, hidden_pre)[1]
-    d_pre = gelu_back(d_hidden.astype(jnp.float32))[0].astype(low)
-    grad_up = shared_out(weight_grad(second_low, d_pre))
-    grad_bias_up = shared_out(jnp.sum(d_pre.astype(jnp.float32), axis=0))
-    d_second = ALPHA * d_third + back_prod(d_pre, up_full)
+    d_pre, grad_bias_up = gelu_back_rows(d_branch_three, ffn_full, slope)
+    up_grad = Flight(whole_reduce([(second_low, d_pre)]))
+    d_pre = tick(d_pre, up_grad)
+    d_second = ALPHA * d_third + up_back_rows(d_pre, ffn_full)
     second_back = jax.vjp(layer_norm, second_sum, gain_full[1], shift_full[1])[1]
     d_second_sum, d_gain_two, d_shift_two = second_back(d_second)
     d_branch_two = d_second_sum.astype(low)
-    grad_cross_out = shared_out(weight_grad(cross_flat, d_branch_two))
     d_cross = back_prod(d_branch_two, cross_out_full).astype(low)
 
-    def cross_backward(rows_q, rows_kv, rows_ids, rows_memory_ids, mixed, lse, d_mixed):
-        fq, fk = document_features(rows_ids, rows_memory_ids)
-        return attention_backward(rows_q, 0, rows_kv, 0, 8, fq, fk, mixed, lse, d_mixed, False)
-
-    d_cross_low, d_memory_keys, d_memory_values = each_row(
-        cross_backward,
-        rows,
-        cross_queries,
-        memory_pairs,
-        target_flat,
-        memory_id_flat,
-        cross_flat,
-        cross_lse,
-        d_cross,
-    )
-    d_memory_pairs = jnp.concatenate([d_memory_keys, d_memory_values], axis=1)
-    grad_cross_kv = shared_out(weight_grad(memory_flat, d_memory_pairs))
-    d_memory = rows_out(
-        back_prod(d_memory_pairs, cross_kv_full).reshape(rows, length, D), jnp.float32
-    )
-    grad_cross_q = shared_out(weight_grad(first_low, d_cross_low))
+    def cross_backward(id_row, memory_id_row, *arrays, into, pairs):
+        fq, fk = document_features(id_row, memory_id_row)
+        return attention_backward(fq, fk, *arrays, False, pairs, into)
+
+    arrays = (target_flat, memory_id_flat, cross_queries, memory_keys, memory_values)
+    arrays += (cross_flat, cross_lse, d_cross)
+    grads = each_row(functools.partial(cross_backward, pairs=(0, 2 * half)), rows, arrays)
+    d_cross_low, d_memory_keys, d_memory_values = tick(grads, output)
+    cross_grad = Flight(
+        whole_reduce(
+            [
+                (memory_flat, d_memory_keys),
+                (memory_flat, d_memory_values),
+                (first_low, d_cross_low),
+                (cross_flat, d_branch_two),
+            ]
+        )
+    )
+    d_cross_low = tick(d_cross_low, cross_grad)
     d_first = ALPHA * d_second_sum + back_prod(d_cross_low, cross_q_full)
     first_back = jax.vjp(layer_norm, first_sum, gain_full[0], shift_full[0])[1]
     d_first_sum, d_gain_one, d_shift_one = first_back(d_first)
     d_branch_one = d_first_sum.astype(low)
-    grad_self_out = shared_out(weight_grad(mixed_flat, d_branch_one))
+    grad_rows = [d_gain_one, d_gain_two, d_gain_three]
+    grad_rows += [d_shift_one, d_shift_two, d_shift_three, grad_bias_down]
+    grad_small = Flight(small_reduce(jnp.stack(grad_rows), grad_bias_up))
     d_self = back_prod(d_branch_one, out_full).astype(low)
-
-    def self_backward(rows_proj, rows_ids, mixed, lse, d_mixed):
-        fq, fk = document_features(rows_ids, rows_ids)
-        return attention_backward(
-            rows_proj, 0, rows_proj, 8, 16, fq, fk, mixed, lse, d_mixed, True
-        )
-
-    d_projected = jnp.concatenate(
-        each_row(self_backward, rows, projected, target_flat, mixed_flat, self_lse, d_self), axis=1
-    )
-    grad_self_qkv = shared_out(weight_grad(x_flat, d_projected))
-    d_input = rows_out(
-        (ALPHA * d_first_sum + back_prod(d_projected, qkv_full)).reshape(rows, length, D),
-        jnp.float32,
-    )
-    grad_rows = jnp.stack(
-        [
-            d_gain_one,
-            d_gain_two,
-            d_gain_three,
-            d_shift_one,
-            d_shift_two,
-            d_shift_three,
-            grad_bias_down,
-        ]
-    )
-    grad_rows = shared_out(grad_rows, 1)
+    d_self_halves = jnp.split(d_self, 2, axis=1)
+    d_self_halves = tick(d_self_halves, grad_small)
+
+    def self_backward(id_row, *arrays, into, pairs):
+        fq, fk = document_features(id_row, id_row)
+        return attention_backward(fq, fk, *arrays, True, pairs, into)
+
+    halves_of = [jnp.split(a, 2, axis=1) for a in (*qkv, mixed_flat, self_lse)]
+    arrays = (target_flat, *[a[0] for a in halves_of], d_self_halves[0])
+    grads_a = each_row(functools.partial(self_backward, pairs=(0, half)), rows, arrays)
+    d_memory = back_prod(d_memory_keys, mk_full) + back_prod(d_memory_values, mv_full)
+    d_memory = Flight(rows_out_steps(d_memory.reshape(rows, length, D), jnp.float32))
+    grads_a, d_self_b = tick((grads_a, d_self_halves[1]), grad_small)
+    early_grad = start_reduce([(x_flat, grads_a), (mixed_flat, [d_branch_one])], "xyz")
+    d_self_b = tick(d_self_b, grad_small, early_grad, d_memory)
+    arrays = (target_flat, *[a[1] for a in halves_of], d_self_b)
+    grads_b = each_row(functools.partial(self_backward, pairs=(0, half)), rows, arrays)
+    grads_b = tick(grads_b, grad_small, early_grad, d_memory)
+    late_grad = start_reduce([(x_flat, grads_b)], "xyz")
+    grads_b = tick(grads_b, grad_small, late_grad)
+    d_input = ALPHA * d_first_sum
+    for grad_a, grad_b, weight in zip(grads_a, grads_b, qkv_full):
+        d_input = d_input + back_prod(jnp.concatenate([grad_a, grad_b], axis=1), weight)
+    d_input = Flight(rows_out_steps(d_input.reshape(rows, length, D), jnp.float32))
+    flights = [late_grad, early_grad, grad_small, d_memory, d_input, down_grad, up_grad]
+    token = grad_bias_up
+    for _ in range(3):
+        token = tick(token, *flights)
+    flights.append(cross_grad)
+    while any(f.result is None for f in flights):
+        token = tick(token, *flights)
+    grad_rows, grad_bias_up = grad_small.finish()
+    grad_kv, grad_cross_q, grad_cross_out = jnp.split(cross_grad.finish(), [2 * D, 3 * D], axis=1)
+    grad_qa, grad_ka, grad_va, grad_self_out = early_grad.finish()
+    grad_qb, grad_kb, grad_vb = late_grad.finish()
     return (
-        output,
-        d_input,
-        d_memory,
-        grad_self_qkv,
+        output.finish(),
+        d_input.finish(),
+        d_memory.finish(),
+        jnp.concatenate([grad_qa, grad_qb, grad_ka, grad_kb, grad_va, grad_vb], axis=1),
         grad_self_out,
         grad_cross_q,
-        grad_cross_kv,
+        grad_kv,
         grad_cross_out,
-        grad_up,
-        grad_down,
+        up_grad.finish(),
+        down_grad.finish(),
         grad_bias_up,
         grad_rows[:3],
         grad_rows[3:],

time: 1270 us -> 740 us (0.58)
  waiting for transfers between devices: 695 us -> 165 us
  matrix products: 215 us -> 132 us
  blocking collectives: 77.4 us -> 0 us
  Pallas kernels: 158 us -> 227 us
  local copies, waits for them, and re-layouts: 44.3 us -> 85.6 us
  starting transfers between devices: 10.2 us -> 33.2 us
  other arithmetic: 49.6 us -> 71.6 us
    reduce_scatter x7 -> x2, waiting for transfers between devices: 425 us -> 0.01 us  [over_batch(): return lax.psum_scatter(array, 'batch', scatter_dimension=0, tiled=True)]
    all_gather x7 -> x1, waiting for transfers between devices: 190 us -> 52.7 us  [gathered(): return lax.all_gather(shard, 'batch', axis=axis, tiled=True)]
    pallas_call x4 -> x9, Pallas kernels: 158 us -> 227 us  [the longest x5 159 us: attention_call(): pl.pallas_call(body, grid=(count,), in_specs=[cols(a.shape[0], first) for...]
    ppermute x7 -> x15, waiting for transfers between devices: 16.2 us -> 80 us  [swap_pair(): return lax.ppermute(array, 'blk', [(0, 1), (1, 0)])]
    psum x1 -> x0, waiting for transfers between devices: 45.3 us -> none  [shared_out(): return lax.psum(part, 'blk').astype(jnp.float32)]
    all_gather x2 -> x0, blocking collectives: 39.9 us -> none  [gathered(): return lax.all_gather(shard, 'batch', axis=axis, tiled=True)]
    dot_general x7 -> x8, matrix products: 75.6 us -> 38.3 us  [back_prod(): jnp.einsum('tn,kn->tk', grad_rows, matrix, preferred_element_type=jnp.flo...]
    unnamed x1 -> x0, blocking collectives: 32.6 us -> none
  transfers between devices with their start and end apart: 23 -> 38, of which waited for: 13 -> 9; matrix products, arithmetic and copies ran while one was open for 14% -> 32% of each run, Pallas kernels for 8% -> 26%
where the time goes in v2:
time: 740 us; the launch traced here: 729 us
  Pallas kernels  227 us (31%)
  waiting for transfers between devices  165 us (22%)
  matrix products  132 us (18%)
  local copies, waits for them, and re-layouts  85.6 us (12%)
  other arithmetic  71.6 us (10%)
  starting transfers between devices  33.2 us (4%)
  between operations  15.9 us (2%)
    pallas_call x5, Pallas kernels, attention_call(): pl.pallas_call(body, grid=(count,), in_specs=[cols(a.shape[0], first) for...  159 us
    ppermute x15, waiting for transfers between devices, swap_pair(): return lax.ppermute(array, 'blk', [(0, 1), (1, 0)])  80 us
    all_gather x1, waiting for transfers between devices, gathered(): return lax.all_gather(shard, 'batch', axis=axis, tiled=True)  52.7 us
    dot_general x12, matrix products, weight_grad(): jnp.einsum('tk,tn->kn', left_rows, right_rows, preferred_element_type=jnp...  51.9 us
    dot_general x8, matrix products, dot32(): return jnp.dot(left, right, preferred_element_type=jnp.float32)  41.5 us
    dot_general x8, matrix products, back_prod(): jnp.einsum('tn,kn->tk', grad_rows, matrix, preferred_element_type=jnp.flo...  38.3 us
    unnamed x179, local copies, waits for them, and re-layouts  35 us
    pallas_call x1, Pallas kernels, gelu_rows(): pl.pallas_call(gelu_kernel, grid=(rows // tall, parts // 2), in_specs=[pl...  20.6 us
  transfers between devices with their start and end apart: 38, of which 9 were waited for; matrix products, arithmetic and copies ran while one was open for 32% of the time, Pallas kernels for 26%

profile of v2, /device:TPU:0, one launch (start us, length us, event | category | flops | bytes accessed | tf_op | source)
XLA Modules:
  0.0 729.4 jit_solution(10753732177393076091)
XLA Ops:
  9.6 3.1 concatenate.79
  19.0 3.0 collective-permute-start
  24.4 21.1 %collective-permute-done.1 = s32[1,512,2]{1,0,2:T(1,128)S(1)} collective-permute-done((s32[1,512,2]{1,0,2:T(1,128)S(1)}, s32[1,512,2]{1,0,2:T(1,128)S(1)}, u32[]{:S(2)}, u32[]{:S(2)}) %collective-permute-start.1) | collective-permute-done | bytes 4128 | tf_op jit(solution)/shard_map/ppermute | solution.py:691
  50.2 3.0 broadcast_select_fusion.7
  53.2 52.7 %all-gather.4.cloned.1.call-done = bf16[1024,8320]{1,0:T(8,128)(2,1)} async-done(((bf16[64,8320]{1,0:T(8,128)(2,1)}), bf16[1024,8320]{1,0:T(8,128)(2,1)}) %all-gather.4.cloned.1.call-update) | async-done | bytes 17039376 | tf_op jit(solution)/shard_map/all_gather | solution.py:732
  105.8 4.7 convolution_convert_fusion.13.refs_0_
  110.6 6.0 convolution_convert_fusion.12.refs_1_
  116.6 5.4 convolution_convert_fusion.11.refs_2_
  122.0 28.7 %attention_forward.2 = (bf16[1024,1024]{1,0:T(8,128)(2,1)S(1)}, f32[1024,1024]{1,0:T(8,128)}) custom-call(bf16[1024,1024]{1,0:T(8,128)(2,1)S(1)} %convolution_convert_fusion.13.refs_0_, bf16[1024,1024]{1,0:T(8,128)(2,1)} %convolution_convert_fusion.12.refs_1_, bf16[1024,1024]{1,0:T(8,128)(2,1)} %convolution_convert_fusion.11.refs_2_, ...), custom_call_target="tpu_custom_call" | custom-call | flops 1024 | bytes 1024 | tf_op jit(solution)/shard_map/attention_forward/pallas_call | solution.py:173
  153.4 4.0 fusion.97
  160.0 4.8 convolution_convert_fusion.10.refs_0_
  167.8 6.1 convolution_convert_fusion.9.refs_1_
  173.8 5.3 convolution_convert_fusion.8.refs_2_
  179.2 35.2 %attention_forward.3 = (bf16[1024,1024]{1,0:T(8,128)(2,1)S(1)}, f32[1024,1024]{1,0:T(8,128)}) custom-call(bf16[1024,1024]{1,0:T(8,128)(2,1)S(1)} %convolution_convert_fusion.10.refs_0_, bf16[1024,1024]{1,0:T(8,128)(2,1)} %convolution_convert_fusion.9.refs_1_, bf16[1024,1024]{1,0:T(8,128)(2,1)} %convolution_convert_fusion.8.refs_2_, ...), custom_call_target="tpu_custom_call" | custom-call | flops 1024 | bytes 1024 | tf_op jit(solution)/shard_map/attention_forward/pallas_call | solution.py:173
  215.6 5.2 fusion.98
  224.9 10.1 %all-gather.6.cloned.1.call-done = bf16[128,64,1024]{2,1,0:T(8,128)(2,1)} async-done(((bf16[8,64,1024]{2,1,0:T(8,128)(2,1)}), bf16[128,64,1024]{2,1,0:T(8,128)(2,1)}) %all-gather.6.cloned.1.call-update) | async-done | bytes 16777232 | tf_op jit(solution)/shard_map/all_gather | solution.py:1146
  234.9 20.6 %gelu_rows.1 = (bf16[1024,4096]{1,0:T(8,128)(2,1)}, f32[1024,4096]{1,0:T(8,128)}) custom-call(bf16[1024,1024]{1,0:T(8,128)(2,1)} %fusion.7.left_ref, bf16[16,8,64,1024]{3,2,1,0:T(8,128)(2,1)} %bitcast.109, f32[1,4096]{1,0:T(1,128)} %reshape.294.bias_ref), custom_call_target="tpu_custom_call" | custom-call | flops 1024 | bytes 1024 | tf_op jit(solution)/shard_map/gelu_rows/pallas_call | solution.py:245
  255.5 14.0 %down_rows.1 = f32[1024,1024]{1,0:T(8,128)S(1)} custom-call(bf16[1024,4096]{1,0:T(8,128)(2,1)} %get-tuple-element.163.left_ref, bf16[16,8,64,1024]{3,2,1,0:T(8,128)(2,1)} %bitcast.110), custom_call_target="tpu_custom_call" | custom-call | flops 1024 | bytes 1024 | tf_op jit(solution)/shard_map/down_rows/pallas_call | solution.py:273
  274.2 2.9 fusion.5
  285.6 11.3 %convolution_convert_fusion.1 = bf16[4096,1024]{1,0:T(8,128)(2,1)} fusion(bf16[1024,4096]{1,0:T(8,128)(2,1)S(1)} %bitcast.122, bf16[1024,1024]{1,0:T(8,128)(2,1)S(1)} %get-tuple-element.366), kind=kOutput, calls=%fused_computation.2 | convolution fusion | flops 8594128896 | bytes 18874368 | tf_op jit(solution)/shard_map/tk,tn->kn/dot_general | solution.py:383
  297.0 19.0 %gelu_back_rows.1 = (bf16[1024,4096]{1,0:T(8,128)(2,1)}, f32[1,1,4096]{2,1,0:T(1,128)S(1)}) custom-call(bf16[1024,1024]{1,0:T(8,128)(2,1)S(1)} %get-tuple-element.366, bf16[16,8,64,1024]{3,2,1,0:T(8,128)(2,1)} %bitcast.111, f32[1024,4096]{1,0:T(8,128)} %get-tuple-element.170.slope_ref), custom_call_target="tpu_custom_call" | custom-call | flops 1024 | bytes 1024 | tf_op jit(solution)/shard_map/gelu_back_rows/pallas_call | solution.py:337
  316.0 14.8 %convolution_convert_fusion = bf16[1024,4096]{1,0:T(8,128)(2,1)} fusion(bf16[1024,1024]{1,0:T(8,128)(2,1)S(1)} %copy-done.44, bf16[1024,4096]{1,0:T(8,128)(2,1)} %get-tuple-element.172.left_ref), kind=kOutput, calls=%fused_computation.1 | convolution fusion | flops 8594128896 | bytes 18874368 | tf_op jit(solution)/shard_map/tk,tn->kn/dot_general | solution.py:383
  341.6 14.5 %up_back_rows.1 = f32[1024,1024]{1,0:T(8,128)S(1)} custom-call(bf16[1024,4096]{1,0:T(8,128)(2,1)} %get-tuple-element.172.left_ref, bf16[16,8,64,1024]{3,2,1,0:T(8,128)(2,1)} %bitcast.112), custom_call_target="tpu_custom_call" | custom-call | flops 1024 | bytes 1024 | tf_op jit(solution)/shard_map/up_back_rows/pallas_call | solution.py:302
  361.7 6.8 convolution_convert_fusion.7.refs_7_
  368.5 53.7 %attention_backward.3 = (bf16[1024,1024]{1,0:T(8,128)(2,1)S(1)}, bf16[1024,1024]{1,0:T(8,128)(2,1)S(1)}, bf16[1024,1024]{1,0:T(8,128)(2,1)}) custom-call(bf16[1024,1024]{1,0:T(8,128)(2,1)} %copy-done.1, bf16[1024,1024]{1,0:T(8,128)(2,1)} %convolution_convert_fusion.9.refs_1_, bf16[1024,1024]{1,0:T(8,128)(2,1)} %convolution_convert_fusion.8.refs_2_, ...), custom_call_target="tpu_custom_call" | custom-call | flops 1024 | bytes 1024 | tf_op jit(solution)/shard_map/attention_backward/pallas_call | solution.py:173
  428.6 4.8 convolution_convert_fusion.3
  441.6 4.6 pad_maximum_fusion
  446.2 5.1 multiply_reduce_fusion.1
  453.4 5.6 convolution_convert_fusion.2
  460.7 12.1 %copy.104 = bf16[1024,4096]{1,0:T(8,128)(2,1)} copy(bf16[1024,4096]{0,1:T(8,128)(2,1)} %pad_maximum_fusion) | data formatting | bytes 16777216
  472.9 4.2 fusion.24
  478.7 4.2 convolution_add_fusion
  484.2 20.6 %attention_backward.4 = (bf16[1024,512]{1,0:T(8,128)(2,1)S(1)}, bf16[1024,512]{1,0:T(8,128)(2,1)S(1)}, bf16[1024,512]{1,0:T(8,128)(2,1)S(1)}) custom-call(bf16[1024,512]{1,0:T(8,128)(2,1)S(1)} %copy-done.3, bf16[1024,512]{1,0:T(8,128)(2,1)S(1)} %copy-done.4, bf16[1024,512]{1,0:T(8,128)(2,1)} %get-tuple-element.402.refs_2_, ...), custom_call_target="tpu_custom_call" | custom-call | flops 1024 | bytes 1024 | tf_op jit(solution)/shard_map/attention_backward/pallas_call | solution.py:173
  512.8 3.3 convolution_convert_fusion.18
  520.9 4.6 copy.106
  525.5 20.4 %attention_backward.5 = (bf16[1024,512]{1,0:T(8,128)(2,1)S(1)}, bf16[1024,512]{1,0:T(8,128)(2,1)S(1)}, bf16[1024,512]{1,0:T(8,128)(2,1)S(1)}) custom-call(bf16[1024,512]{1,0:T(8,128)(2,1)S(1)} %get-tuple-element.407.refs_0_, bf16[1024,512]{1,0:T(8,128)(2,1)S(1)} %copy-done.2, bf16[1024,512]{1,0:T(8,128)(2,1)} %get-tuple-element.403.refs_2_, ...), custom_call_target="tpu_custom_call" | custom-call | flops 1024 | bytes 1024 | tf_op jit(solution)/shard_map/attention_backward/pallas_call | solution.py:173
  548.9 4.7 copy.107
  559.4 3.1 convolution_convert_fusion.14
  562.5 3.8 collective-permute-done.10
  566.5 4.1 fusion.12
  570.7 4.2 fusion.8
  574.9 4.1 add_add_fusion.3
  582.3 15.5 %collective-permute-done.12 = bf16[4,1,128,1280]{3,2,1,0:T(8,128)(2,1)S(1)} collective-permute-done((bf16[4,1,128,1280]{3,2,1,0:T(8,128)(2,1)S(1)}, bf16[4,1,128,1280]{3,2,1,0:T(8,128)(2,1)S(1)}, u32[]{:S(2)}, u32[]{:S(2)}) %collective-permute-start.12) | collective-permute-done | bytes 1310752 | tf_op jit(solution)/shard_map/ppermute | solution.py:795
  597.8 2.9 add_convert_fusion.4
  613.1 41.5 %collective-permute-done.17 = bf16[256,1024]{1,0:T(8,128)(2,1)S(1)} collective-permute-done((bf16[256,1024]{1,0:T(8,128)(2,1)}, bf16[256,1024]{1,0:T(8,128)(2,1)S(1)}, u32[]{:S(2)}, u32[]{:S(2)}) %collective-permute-start.17) | collective-permute-done | bytes 524320 | tf_op jit(solution)/shard_map/ppermute | solution.py:691
  654.7 6.6 collective-permute-done.18
  670.6 3.2 convert_select_fusion.1
  701.6 10.7 %collective-permute-done.32 = bf16[64,4096]{1,0:T(8,128)(2,1)S(1)} collective-permute-done((bf16[64,4096]{1,0:T(8,128)(2,1)S(1)}, bf16[64,4096]{1,0:T(8,128)(2,1)S(1)}, u32[]{:S(2)}, u32[]{:S(2)}) %collective-permute-start.32) | collective-permute-done | bytes 524320 | tf_op jit(solution)/shard_map/ppermute | solution.py:691
  (370 shorter events, 163.9 us)
Async XLA Ops:
  7.2 98.7 %all-gather.4.cloned.1.call-start = ((), (), s32[]{:S(2)}) async-start(), calls=%async_computation.3 | async-start | bytes 18104320 | tf_op jit(solution)/shard_map/all_gather | solution.py:732
  12.7 222.2 %all-gather.6.cloned.1.call-start = ((), (), s32[]{:S(2)}) async-start(), calls=%async_computation.6 | async-start | bytes 17825792 | tf_op jit(solution)/shard_map/all_gather | solution.py:1146
  17.9 579.9 %reduce-scatter.6.cloned.1.call-start = ((), (), s32[]{:S(2)}) async-start(), calls=%async_computation.4 | async-start | bytes 8912896 | tf_op jit(solution)/shard_map/reduce_scatter | solution.py:976
  19.0 26.5 %collective-permute-start = (bf16[1,512,1024]{2,1,0:T(8,128)(2,1)}, bf16[1,512,1024]{2,1,0:T(8,128)(2,1)}, u32[]{:S(2)}, u32[]{:S(2)}) collective-permute-start(bf16[1,512,1024]{2,1,0:T(8,128)(2,1)} %constant_dynamic-slice_fusion.19), channel_id=1, source_target_pairs={{0,1},{1,0},{2,3},{3,2},{4,5},{5,4},{6,7},{7,6},{8,9},{9,8},{10,11... | collective-permute-start | bytes 3145736 | tf_op jit(solution)/shard_map/ppermute | solution.py:691
  22.0 23.5 %collective-permute-start.1 = (s32[1,512,2]{1,0,2:T(1,128)S(1)}, s32[1,512,2]{1,0,2:T(1,128)S(1)}, u32[]{:S(2)}, u32[]{:S(2)}) collective-permute-start(s32[1,512,2]{1,0,2:T(1,128)S(1)} %fusion.70), channel_id=1, source_target_pairs={{0,1},{1,0},{2,3},{3,2},{4,5},{5,4},{6,7},{7,6},{8,9},{9,8},{10,11... | collective-permute-start | bytes 12296 | tf_op jit(solution)/shard_map/ppermute | solution.py:691
  45.5 120.9 %collective-permute-start.2 = (bf16[1,512,1024]{2,1,0:T(8,128)(2,1)}, bf16[1,512,1024]{2,1,0:T(8,128)(2,1)}, u32[]{:S(2)}, u32[]{:S(2)}) collective-permute-start(bf16[1,512,1024]{2,1,0:T(8,128)(2,1)} %constant_dynamic-slice_fusion.16), channel_id=1, source_target_pairs={{0,1},{1,0},{2,3},{3,2},{4,5},{5,4},{6,7},{7,6},{8,9},{9,8},{10,11... | collective-permute-start | bytes 3145736 | tf_op jit(solution)/shard_map/ppermute | solution.py:691
  50.2 71.8 %copy-start.5 = (bf16[1024,128]{1,0:T(8,128)(2,1)}, bf16[1024,128]{1,0:T(8,128)(2,1)S(1)}, u32[]{:S(2)}) copy-start(bf16[1024,128]{1,0:T(8,128)(2,1)S(1)} %get-tuple-element.439.refs_4_) | copy-start | bytes 786436
  50.2 129.0 %copy-start.7 = (bf16[1024,128]{1,0:T(8,128)(2,1)}, bf16[1024,128]{1,0:T(8,128)(2,1)S(1)}, u32[]{:S(2)}) copy-start(bf16[1024,128]{1,0:T(8,128)(2,1)S(1)} %get-tuple-element.438.refs_4_) | copy-start | bytes 786436
  164.8 50.7 %collective-permute-start.3 = (bf16[1,512,1024]{2,1,0:T(8,128)(2,1)}, bf16[1,512,1024]{2,1,0:T(8,128)(2,1)}, u32[]{:S(2)}, u32[]{:S(2)}) collective-permute-start(bf16[1,512,1024]{2,1,0:T(8,128)(2,1)} %constant_dynamic-slice_fusion.15), channel_id=1, source_target_pairs={{0,1},{1,0},{2,3},{3,2},{4,5},{5,4},{6,7},{7,6},{8,9},{9,8},{10,11... | collective-permute-start | bytes 3145736 | tf_op jit(solution)/shard_map/ppermute | solution.py:691
  297.0 300.9 %reduce-scatter.8.cloned.1.call-start = ((), (), s32[]{:S(2)}) async-start(), calls=%async_computation.5 | async-start | bytes 8912896 | tf_op jit(solution)/shard_map/reduce_scatter | solution.py:976
  297.0 19.0 %copy-start.44 = (bf16[1024,1024]{1,0:T(8,128)(2,1)S(1)}, bf16[1024,1024]{1,0:T(8,128)(2,1)}, u32[]{:S(2)}) copy-start(bf16[1024,1024]{1,0:T(8,128)(2,1)} %fusion.7.left_ref) | copy-start | bytes 6291460
  330.9 361.6 %reduce-scatter.10.cloned.1.call-start = ((), (), s32[]{:S(2)}) async-start(), calls=%async_computation.7 | async-start | bytes 8912896
  341.6 16.1 %copy-start.33 = (f32[1024,1024]{1,0:T(8,128)S(1)}, f32[1024,1024]{1,0:T(8,128)}, u32[]{:S(2)}) copy-start(f32[1024,1024]{1,0:T(8,128)} %get-tuple-element.168) | copy-start | bytes 12582916
  356.2 77.3 %collective-permute-start.4 = (bf16[1,512,1024]{2,1,0:T(8,128)(2,1)}, bf16[1,512,1024]{2,1,0:T(8,128)(2,1)}, u32[]{:S(2)}, u32[]{:S(2)}) collective-permute-start(bf16[1,512,1024]{2,1,0:T(8,128)(2,1)} %fusion.62), channel_id=1, source_target_pairs={{0,1},{1,0},{2,3},{3,2},{4,5},{5,4},{6,7},{7,6},{8,9},{9,8},{10,11... | collective-permute-start | bytes 3145736 | tf_op jit(solution)/shard_map/ppermute | solution.py:691
  460.7 44.2 %collective-permute-start.5 = (f32[11,1024]{1,0:T(8,128)S(1)}, f32[11,1024]{1,0:T(8,128)S(1)}, u32[]{:S(2)}, u32[]{:S(2)}) collective-permute-start(f32[11,1024]{1,0:T(8,128)S(1)} %concatenate.86), channel_id=1, source_target_pairs={{0,2},{2,0},{4,6},{6,4},{8,10},{10,8},{12,14},{14,12},{16,18},{18,... | collective-permute-start | bytes 135176 | tf_op jit(solution)/shard_map/ppermute | solution.py:791
  482.9 21.9 %copy-start.48 = (f32[1024,1024]{1,0:T(8,128)}, f32[1024,1024]{1,0:T(8,128)S(1)}, u32[]{:S(2)}) copy-start(f32[1024,1024]{1,0:T(8,128)S(1)} %convolution_add_fusion) | copy-start | bytes 12582916
  504.9 6.6 collective-permute-start.6
  511.5 37.3 %collective-permute-start.8 = (bf16[1024,1280]{0,1:T(8,128)(2,1)}, bf16[1024,1280]{0,1:T(8,128)(2,1)}, u32[]{:S(2)}, u32[]{:S(2)}) collective-permute-start(bf16[1024,1280]{0,1:T(8,128)(2,1)} %pad_maximum_fusion.3), channel_id=1, source_target_pairs={{0,2},{2,0},{4,6},{6,4},{8,10},{10,8},{12,14},{14,12},{16,18},{18,... | collective-permute-start | bytes 7864328 | tf_op jit(solution)/shard_map/ppermute | solution.py:791
  511.9 36.9 %collective-permute-start.9 = (bf16[1,512,1024]{2,1,0:T(8,128)(2,1)}, bf16[1,512,1024]{2,1,0:T(8,128)(2,1)}, u32[]{:S(2)}, u32[]{:S(2)}) collective-permute-start(bf16[1,512,1024]{2,1,0:T(8,128)(2,1)} %fusion.63), channel_id=1, source_target_pairs={{0,1},{1,0},{2,3},{3,2},{4,5},{5,4},{6,7},{7,6},{8,9},{9,8},{10,11... | collective-permute-start | bytes 3145736 | tf_op jit(solution)/shard_map/ppermute | solution.py:691
  518.0 30.9 %collective-permute-start.7 = (f32[11,1024]{1,0:T(8,128)S(1)}, f32[11,1024]{1,0:T(8,128)S(1)}, u32[]{:S(2)}, u32[]{:S(2)}) collective-permute-start(f32[11,1024]{1,0:T(8,128)S(1)} %add.621), channel_id=1, source_target_pairs={{0,1},{1,0},{2,3},{3,2},{4,5},{5,4},{6,7},{7,6},{8,9},{9,8},{10,11... | collective-permute-start | bytes 135176 | tf_op jit(solution)/shard_map/ppermute | solution.py:691
  555.8 10.5 %collective-permute-start.10 = (f32[11,1024]{1,0:T(8,128)S(1)}, f32[11,1024]{1,0:T(8,128)S(1)}, u32[]{:S(2)}, u32[]{:S(2)}) collective-permute-start(f32[11,1024]{1,0:T(8,128)S(1)} %add.626), channel_id=1, source_target_pairs={{0,8},{2,10},{4,12},{6,14},{8,0},{10,2},{12,4},{14,6},{16,24},{18,... | collective-permute-start | bytes 135176 | tf_op jit(solution)/shard_map/ppermute | solution.py:991
  556.3 41.6 %collective-permute-start.12 = (bf16[4,1,128,1280]{3,2,1,0:T(8,128)(2,1)S(1)}, bf16[4,1,128,1280]{3,2,1,0:T(8,128)(2,1)S(1)}, u32[]{:S(2)}, u32[]{:S(2)}) collective-permute-start(bf16[4,1,128,1280]{3,2,1,0:T(8,128)(2,1)S(1)} %add_convert_fusion.2), channel_id=1, source_target_pairs={{0,4},{2,6},{4,0},{6,2},{8,12},{10,14},{12,8},{14,10},{16,20},{18,... | collective-permute-start | bytes 3932168 | tf_op jit(solution)/shard_map/ppermute | solution.py:795
  566.3 31.5 %collective-permute-start.11 = (bf16[1024,768]{1,0:T(8,128)(2,1)S(1)}, bf16[1024,768]{1,0:T(8,128)(2,1)}, u32[]{:S(2)}, u32[]{:S(2)}) collective-permute-start(bf16[1024,768]{1,0:T(8,128)(2,1)S(1)} %convolution_convert_fusion.15), channel_id=1, source_target_pairs={{0,2},{2,0},{4,6},{6,4},{8,10},{10,8},{12,14},{14,12},{16,18},{18,... | collective-permute-start | bytes 4718600 | tf_op jit(solution)/shard_map/ppermute | solution.py:791
  566.4 15.9 %collective-permute-start.13 = (f32[11,1024]{1,0:T(8,128)S(1)}, f32[11,1024]{1,0:T(8,128)S(1)}, u32[]{:S(2)}, u32[]{:S(2)}) collective-permute-start(f32[11,1024]{1,0:T(8,128)S(1)} %add.632), channel_id=1, source_target_pairs={{0,16},{2,18},{4,20},{6,22},{8,24},{10,26},{12,28},{14,30},{16,0},... | collective-permute-start | bytes 135176 | tf_op jit(solution)/shard_map/ppermute | solution.py:991
  579.0 29.1 %copy-start.41 = (bf16[1024,1024]{1,0:T(8,128)(2,1)S(1)}, bf16[1024,1024]{1,0:T(8,128)(2,1)}, u32[]{:S(2)}) copy-start(bf16[1024,1024]{1,0:T(8,128)(2,1)} %copy-done.40) | copy-start | bytes 6291460
  603.1 58.2 %collective-permute-start.16 = (bf16[1,512,1024]{2,1,0:T(8,128)(2,1)}, bf16[1,512,1024]{2,1,0:T(8,128)(2,1)}, u32[]{:S(2)}, u32[]{:S(2)}) collective-permute-start(bf16[1,512,1024]{2,1,0:T(8,128)(2,1)} %fusion.64), channel_id=1, source_target_pairs={{0,1},{1,0},{2,3},{3,2},{4,5},{5,4},{6,7},{7,6},{8,9},{9,8},{10,11... | collective-permute-start | bytes 3145736 | tf_op jit(solution)/shard_map/ppermute | solution.py:691
  603.1 58.2 %collective-permute-start.14 = (bf16[4,1,128,768]{3,2,1,0:T(8,128)(2,1)}, bf16[4,1,128,768]{3,2,1,0:T(8,128)(2,1)S(1)}, u32[]{:S(2)}, u32[]{:S(2)}) collective-permute-start(bf16[4,1,128,768]{3,2,1,0:T(8,128)(2,1)} %add_convert_fusion.3), channel_id=1, source_target_pairs={{0,4},{2,6},{4,0},{6,2},{8,12},{10,14},{12,8},{14,10},{16,20},{18,... | collective-permute-start | bytes 2359304 | tf_op jit(solution)/shard_map/ppermute | solution.py:795
  605.0 56.3 %collective-permute-start.15 = (bf16[4,1,128,640]{3,2,1,0:T(8,128)(2,1)}, bf16[4,1,128,640]{3,2,1,0:T(8,128)(2,1)S(1)}, u32[]{:S(2)}, u32[]{:S(2)}) collective-permute-start(bf16[4,1,128,640]{3,2,1,0:T(8,128)(2,1)} %add_convert_fusion.4), channel_id=1, source_target_pairs={{0,1},{1,0},{2,3},{3,2},{4,5},{5,4},{6,7},{7,6},{8,9},{9,8},{10,11... | collective-permute-start | bytes 1966088 | tf_op jit(solution)/shard_map/ppermute | solution.py:691
  606.0 48.6 %collective-permute-start.17 = (bf16[256,1024]{1,0:T(8,128)(2,1)}, bf16[256,1024]{1,0:T(8,128)(2,1)S(1)}, u32[]{:S(2)}, u32[]{:S(2)}) collective-permute-start(bf16[256,1024]{1,0:T(8,128)(2,1)} %reduce-scatter.6.cloned.1.call-done), channel_id=1, source_target_pairs={{0,1},{1,0},{2,3},{3,2},{4,5},{5,4},{6,7},{7,6},{8,9},{9,8},{10,11... | collective-permute-start | bytes 1572872 | tf_op jit(solution)/shard_map/ppermute | solution.py:691
  607.0 54.3 %collective-permute-start.18 = (bf16[64,4096]{1,0:T(8,128)(2,1)}, bf16[64,4096]{1,0:T(8,128)(2,1)S(1)}, u32[]{:S(2)}, u32[]{:S(2)}) collective-permute-start(bf16[64,4096]{1,0:T(8,128)(2,1)} %reduce-scatter.8.cloned.1.call-done), channel_id=1, source_target_pairs={{0,1},{1,0},{2,3},{3,2},{4,5},{5,4},{6,7},{7,6},{8,9},{9,8},{10,11... | collective-permute-start | bytes 1572872 | tf_op jit(solution)/shard_map/ppermute | solution.py:691
  609.4 60.1 %copy-start.70 = (bf16[64,4096]{1,0:T(8,128)(2,1)S(1)}, bf16[64,4096]{1,0:T(8,128)(2,1)}, u32[]{:S(2)}) copy-start(bf16[64,4096]{1,0:T(8,128)(2,1)} %reduce-scatter.8.cloned.1.call-done) | copy-start | bytes 1572868
  609.5 61.1 %copy-start.51 = (f32[1024,1024]{1,0:T(8,128)S(1)}, f32[1024,1024]{1,0:T(8,128)}, u32[]{:S(2)}) copy-start(f32[1024,1024]{1,0:T(8,128)} %copy-done.50) | copy-start | bytes 12582916
  611.2 59.4 %copy-start.49 = (f32[1024,1024]{1,0:T(8,128)S(1)}, f32[1024,1024]{1,0:T(8,128)}, u32[]{:S(2)}) copy-start(f32[1024,1024]{1,0:T(8,128)} %copy-done.48) | copy-start | bytes 12582916
  661.3 17.4 %copy-start.68 = (bf16[4,1,128,768]{3,2,1,0:T(8,128)(2,1)}, bf16[4,1,128,768]{3,2,1,0:T(8,128)(2,1)S(1)}, u32[]{:S(2)}) copy-start(bf16[4,1,128,768]{3,2,1,0:T(8,128)(2,1)S(1)} %collective-permute-done.14) | copy-start | bytes 2359300
  665.3 12.2 %collective-permute-start.19 = (bf16[4,1,128,384]{3,2,1,0:T(8,128)(2,1)S(1)}, bf16[4,1,128,384]{3,2,1,0:T(8,128)(2,1)S(1)}, u32[]{:S(2)}, u32[]{:S(2)}) collective-permute-start(bf16[4,1,128,384]{3,2,1,0:T(8,128)(2,1)S(1)} %add_convert_fusion.5), channel_id=1, source_target_pairs={{0,1},{1,0},{2,3},{3,2},{4,5},{5,4},{6,7},{7,6},{8,9},{9,8},{10,11... | collective-permute-start | bytes 1179656 | tf_op jit(solution)/shard_map/ppermute | solution.py:691
  665.7 9.3 %collective-permute-start.20 = (bf16[1,1,128,640]{3,2,1,0:T(8,128)(2,1)S(1)}, bf16[1,1,128,640]{3,2,1,0:T(8,128)(2,1)S(1)}, u32[]{:S(2)}, u32[]{:S(2)}) collective-permute-start(bf16[1,1,128,640]{3,2,1,0:T(8,128)(2,1)S(1)} %get-tuple-element.249), channel_id=1, source_target_pairs={{0,8},{2,10},{4,12},{6,14},{8,16},{10,18},{12,20},{14,22},{16,24},... | collective-permute-start | bytes 491528 | tf_op jit(solution)/shard_map/ppermute | solution.py:799
  666.7 10.8 %collective-permute-start.21 = (bf16[1,1,128,640]{3,2,1,0:T(8,128)(2,1)S(1)}, bf16[1,1,128,640]{3,2,1,0:T(8,128)(2,1)S(1)}, u32[]{:S(2)}, u32[]{:S(2)}) collective-permute-start(bf16[1,1,128,640]{3,2,1,0:T(8,128)(2,1)S(1)} %get-tuple-element.250), channel_id=1, source_target_pairs={{0,16},{2,18},{4,20},{6,22},{8,24},{10,26},{12,28},{14,30},{16,0},... | collective-permute-start | bytes 491528 | tf_op jit(solution)/shard_map/ppermute | solution.py:799
  669.1 8.3 %collective-permute-start.22 = (bf16[1,1,128,640]{3,2,1,0:T(8,128)(2,1)S(1)}, bf16[1,1,128,640]{3,2,1,0:T(8,128)(2,1)S(1)}, u32[]{:S(2)}, u32[]{:S(2)}) collective-permute-start(bf16[1,1,128,640]{3,2,1,0:T(8,128)(2,1)S(1)} %get-tuple-element.251), channel_id=1, source_target_pairs={{0,24},{2,26},{4,28},{6,30},{8,0},{10,2},{12,4},{14,6},{16,8},{18,... | collective-permute-start | bytes 491528 | tf_op jit(solution)/shard_map/ppermute | solution.py:799
  680.4 8.9 %collective-permute-start.26 = (bf16[64,640]{1,0:T(8,128)(2,1)S(1)}, bf16[64,640]{1,0:T(8,128)(2,1)S(1)}, u32[]{:S(2)}, u32[]{:S(2)}) collective-permute-start(bf16[64,640]{1,0:T(8,128)(2,1)S(1)} %get-tuple-element.259), channel_id=1, source_target_pairs={{0,1},{1,0},{2,3},{3,2},{4,5},{5,4},{6,7},{7,6},{8,9},{9,8},{10,11... | collective-permute-start | bytes 245768 | tf_op jit(solution)/shard_map/ppermute | solution.py:691
  684.7 9.4 %collective-permute-start.23 = (bf16[1,1,128,384]{3,2,1,0:T(8,128)(2,1)S(1)}, bf16[1,1,128,384]{3,2,1,0:T(8,128)(2,1)S(1)}, u32[]{:S(2)}, u32[]{:S(2)}) collective-permute-start(bf16[1,1,128,384]{3,2,1,0:T(8,128)(2,1)S(1)} %get-tuple-element.256), channel_id=1, source_target_pairs={{0,8},{2,10},{4,12},{6,14},{8,16},{10,18},{12,20},{14,22},{16,24},... | collective-permute-start | bytes 294920 | tf_op jit(solution)/shard_map/ppermute | solution.py:799
  687.0 7.1 collective-permute-start.24
  688.1 6.0 collective-permute-start.25
  689.4 4.7 collective-permute-start.27
  689.4 4.7 collective-permute-start.28
  695.3 6.3 collective-permute-start.29
  697.0 4.7 collective-permute-start.30
  697.0 4.7 collective-permute-start.31
  697.9 14.4 %collective-permute-start.32 = (bf16[64,4096]{1,0:T(8,128)(2,1)S(1)}, bf16[64,4096]{1,0:T(8,128)(2,1)S(1)}, u32[]{:S(2)}, u32[]{:S(2)}) collective-permute-start(bf16[64,4096]{1,0:T(8,128)(2,1)S(1)} %copy.99), channel_id=1, source_target_pairs={{0,1},{1,0},{2,3},{3,2},{4,5},{5,4},{6,7},{7,6},{8,9},{9,8},{10,11... | collective-permute-start | bytes 1572872 | tf_op jit(solution)/shard_map/ppermute | solution.py:691
  (71 other events, 349.4 us)
Sparse Core Ops, SparseCore 0:
  12.8 93.0 all-gather.3
  108.0 126.8 all-gather.5
  297.1 102.7 reduce-scatter.5
  403.8 104.3 reduce-scatter.7
  512.1 118.2 reduce-scatter.9

commit v3 on v2

--- a/solution.py
+++ b/solution.py
@@ -16,7 +16,6 @@
 MASKED = -1e30
 EPSILON = 1e-05
 PAIR = 2 * HD
-BLOCK = 256
 MASK_STEP = -(2.0**100)
 
 
@@ -33,6 +32,7 @@
 
 
 def attention_fwd_kernel(causal, q_ref, k_ref, v_ref, fq_ref, fk_ref, out_ref, lse_ref):
+    block = 256
     length = q_ref.shape[0]
     mem = k_ref.shape[0]
     low_q = lane_of(length) < HD
@@ -46,26 +46,37 @@
     queries = (jnp.where(low_q, q, fq), jnp.where(low_q, fq, q))
     keys = (jnp.where(low_k, k, fk), jnp.where(low_k, fk, k))
     values = (jnp.where(low_k, v, ones), jnp.where(low_k, ones, v))
-    low_blk = lane_of(BLOCK) < HD
-    for i in range(length // BLOCK):
-        seen = (i + 1) * BLOCK if causal else mem
-        rows = slice(i * BLOCK, (i + 1) * BLOCK)
-        accs, peaks = [], []
-        for h in range(2):
-            scores = nt(queries[h][rows], keys[h][:seen])
-            if causal:
-                tri = lax.broadcasted_iota(jnp.int32, (BLOCK, BLOCK), 0) >= lax.broadcasted_iota(
-                    jnp.int32, (BLOCK, BLOCK), 1
-                )
-                diag = jnp.where(tri, scores[:, seen - BLOCK :], MASK_STEP)
-                scores = diag if i == 0 else jnp.concatenate([scores[:, : seen - BLOCK], diag], axis=1)
-            peak = jnp.max(scores, axis=1, keepdims=True)
-            raised = jnp.exp(scores - peak).astype(jnp.bfloat16)
-            accs.append(nn(raised, values[h][:seen]))
-            peaks.append(peak)
-        total = pltpu.roll(jnp.where(low_blk, accs[1], accs[0]), HD, 1)
-        out_ref[rows, :] = (jnp.where(low_blk, accs[0], accs[1]) / total).astype(out_ref.dtype)
-        lse_ref[rows, :] = jnp.where(low_blk, peaks[0], peaks[1]) + jnp.log(total)
+    low_blk = lane_of(block) < HD
+    units = [(i, h) for i in range(length // block) for h in range(2)]
+
+    def score(unit):
+        i, h = unit
+        seen = (i + 1) * block if causal else mem
+        scores = nt(queries[h][i * block : (i + 1) * block], keys[h][:seen])
+        if causal:
+            tri = lax.broadcasted_iota(jnp.int32, (block, block), 0) >= lax.broadcasted_iota(
+                jnp.int32, (block, block), 1
+            )
+            diag = jnp.where(tri, scores[:, seen - block :], MASK_STEP)
+            scores = diag if i == 0 else jnp.concatenate([scores[:, : seen - block], diag], axis=1)
+        return scores
+
+    ahead = score(units[0])
+    accs, peaks = [], []
+    for n, (i, h) in enumerate(units):
+        rows = slice(i * block, (i + 1) * block)
+        scores = ahead
+        if n + 1 < len(units):
+            ahead = score(units[n + 1])
+        peak = jnp.max(scores, axis=1, keepdims=True)
+        raised = jnp.exp(scores - peak).astype(jnp.bfloat16)
+        accs.append(nn(raised, values[h][: scores.shape[1]]))
+        peaks.append(peak)
+        if h == 1:
+            total = pltpu.roll(jnp.where(low_blk, accs[1], accs[0]), HD, 1)
+            out_ref[rows, :] = (jnp.where(low_blk, accs[0], accs[1]) / total).astype(out_ref.dtype)
+            lse_ref[rows, :] = jnp.where(low_blk, peaks[0], peaks[1]) + jnp.log(total)
+            accs, peaks = [], []
 
 
 def split3(value):
@@ -83,6 +94,7 @@
 
 
 def attention_bwd_kernel(causal, q_ref, k_ref, v_ref, fq_ref, fk_ref, out_ref, lse_ref, do_ref, dq_ref, dk_ref, dv_ref, dk_acc, dv_acc, dq_acc):
+    block = 256 if causal else 512
     length = q_ref.shape[0]
     mem = k_ref.shape[0]
     lane_q = lane_of(length)
@@ -117,36 +129,42 @@
     plain_q = (jnp.where(low_q, q, zero_q), jnp.where(low_q, zero_q, q))
     plain_do = (jnp.where(low_q, do, zero_q), jnp.where(low_q, zero_q, do))
     k_t = k.T
-    blocks = length // BLOCK
-    for i in range(blocks):
-        rows = slice(i * BLOCK, (i + 1) * BLOCK)
-        seen = (i + 1) * BLOCK if causal else mem
-        probs, d_scores = [], []
-        for h in range(2):
-            p = jnp.exp(nt(keys[h][:seen], queries[h][rows]))
-            if causal:
-                tri = lax.broadcasted_iota(jnp.int32, (BLOCK, BLOCK), 0) <= lax.broadcasted_iota(
-                    jnp.int32, (BLOCK, BLOCK), 1
-                )
-                diag = jnp.where(tri, p[seen - BLOCK :], 0.0)
-                p = diag if i == 0 else jnp.concatenate([p[: seen - BLOCK], diag], axis=0)
-            ds = (p * nt(values[h][:seen], grads[h][rows])).astype(jnp.bfloat16)
-            probs.append(p.astype(jnp.bfloat16))
-            d_scores.append(ds)
-            dq_acc[h * HD : (h + 1) * HD, rows] = nn(k_t[h * HD : (h + 1) * HD, :seen], ds)
-        dv = nn(probs[0], plain_do[0][rows]) + nn(probs[1], plain_do[1][rows])
-        dk = nn(d_scores[0], plain_q[0][rows]) + nn(d_scores[1], plain_q[1][rows])
-        if i == 0:
-            dv_acc[:seen] = dv
-            dk_acc[:seen] = dk
-        elif causal:
-            dv_acc[: seen - BLOCK] += dv[: seen - BLOCK]
-            dk_acc[: seen - BLOCK] += dk[: seen - BLOCK]
-            dv_acc[seen - BLOCK : seen] = dv[seen - BLOCK :]
-            dk_acc[seen - BLOCK : seen] = dk[seen - BLOCK :]
+    units = [(i, h) for i in range(length // block) for h in range(2)]
+
+    def scores_of(unit):
+        i, h = unit
+        rows = slice(i * block, (i + 1) * block)
+        seen = (i + 1) * block if causal else mem
+        return nt(keys[h][:seen], queries[h][rows]), nt(values[h][:seen], grads[h][rows])
+
+    ahead = scores_of(units[0])
+    dv = dk = None
+    for n, (i, h) in enumerate(units):
+        rows = slice(i * block, (i + 1) * block)
+        seen = (i + 1) * block if causal else mem
+        s, dp = ahead
+        if n + 1 < len(units):
+            ahead = scores_of(units[n + 1])
+        p = jnp.exp(s)
+        if causal:
+            tri = lax.broadcasted_iota(jnp.int32, (block, block), 0) <= lax.broadcasted_iota(
+                jnp.int32, (block, block), 1
+            )
+            diag = jnp.where(tri, p[seen - block :], 0.0)
+            p = diag if i == 0 else jnp.concatenate([p[: seen - block], diag], axis=0)
+        ds = (p * dp).astype(jnp.bfloat16)
+        dq_acc[h * HD : (h + 1) * HD, rows] = nn(k_t[h * HD : (h + 1) * HD, :seen], ds)
+        dv_part = nn(p.astype(jnp.bfloat16), plain_do[h][rows])
+        dk_part = nn(ds, plain_q[h][rows])
+        if n == 0:
+            dv_acc[:seen] = dv_part
+            dk_acc[:seen] = dk_part
+            if seen < mem:
+                dv_acc[seen:] = jnp.zeros((mem - seen, PAIR), jnp.float32)
+                dk_acc[seen:] = jnp.zeros((mem - seen, PAIR), jnp.float32)
         else:
-            dv_acc[...] += dv
-            dk_acc[...] += dk
+            dv_acc[:seen] += dv_part
+            dk_acc[:seen] += dk_part
     dq_ref[...] = (dq_acc[...].T * (HD**-0.5)).astype(dq_ref.dtype)
     dk_ref[...] = dk_acc[...].astype(dk_ref.dtype)
     dv_ref[...] = dv_acc[...].astype(dv_ref.dtype)
@@ -163,61 +181,52 @@
 SHORT = pl.CostEstimate(flops=1024, bytes_accessed=1024, transcendentals=0)
 
 
-def attention_call(kernel, name, pairs, causal, arrays, shared, outs, scratch, into):
+def attention_call(kernel, name, pairs, causal, arrays, shared, lengths, kinds, scratch):
     first, count = pairs
-    into = [] if into is None else list(into)
-
-    def body(*refs):
-        kernel(causal, *refs[: len(arrays) + 2], *refs[len(arrays) + 2 + len(into) :])
 
     return pl.pallas_call(
-        body,
+        functools.partial(kernel, causal),
         grid=(count,),
         in_specs=[cols(a.shape[0], first) for a in arrays[:3]]
         + [whole(a.shape[0]) for a in shared]
-        + [cols(a.shape[0], first) for a in arrays[3:]]
-        + [pl.BlockSpec(memory_space=pl.ANY)] * len(into),
-        out_specs=[cols(o.shape[0], first) for o in outs],
-        out_shape=outs,
+        + [cols(a.shape[0], first) for a in arrays[3:]],
+        out_specs=[cols(n, 0) for n in lengths],
+        out_shape=[
+            jax.ShapeDtypeStruct((n, count * PAIR), kind) for n, kind in zip(lengths, kinds)
+        ],
         scratch_shapes=scratch,
-        input_output_aliases={len(arrays) + 2 + n: n for n in range(len(into))},
         compiler_params=pltpu.CompilerParams(vmem_limit_bytes=48 * 2**20),
         cost_estimate=SHORT,
         name=name,
-    )(*arrays[:3], *shared, *arrays[3:], *into)
-
-
-def attention_forward(queries, keys, values, fq, fk, causal, pairs, into):
-    length = queries.shape[0]
-    outs = [
-        jax.ShapeDtypeStruct(queries.shape, jnp.bfloat16),
-        jax.ShapeDtypeStruct(queries.shape, jnp.float32),
-    ]
-    arrays = (queries, keys, values)
+    )(*arrays[:3], *shared, *arrays[3:])
+
+
+def attention_forward(queries, keys, values, fq, fk, causal, pairs):
+    lengths = (queries.shape[0],) * 2
+    kinds = (jnp.bfloat16, jnp.float32)
+    arrays, shared = (queries, keys, values), (fq, fk)
     return attention_call(
-        attention_fwd_kernel, "attention_forward", pairs, causal, arrays, (fq, fk), outs, [], into
-    )
-
-
-def attention_backward(fq, fk, queries, keys, values, mixed, lse, d_mixed, causal, pairs, into):
+        attention_fwd_kernel, "attention_forward", pairs, causal, arrays, shared, lengths, kinds, []
+    )
+
+
+def attention_backward(fq, fk, queries, keys, values, mixed, lse, d_mixed, causal, pairs):
     length, mem = queries.shape[0], keys.shape[0]
-    outs = [jax.ShapeDtypeStruct(a.shape, jnp.bfloat16) for a in (queries, keys, values)]
     scratch = [
         pltpu.VMEM((mem, PAIR), jnp.float32),
         pltpu.VMEM((mem, PAIR), jnp.float32),
         pltpu.VMEM((PAIR, length), jnp.float32),
     ]
-    arrays = (queries, keys, values, mixed, lse, d_mixed)
     return attention_call(
         attention_bwd_kernel,
         "attention_backward",
         pairs,
         causal,
-        arrays,
+        (queries, keys, values, mixed, lse, d_mixed),
         (fq, fk),
-        outs,
+        (length, mem, mem),
+        (jnp.bfloat16,) * 3,
         scratch,
-        into,
     )
 
 
@@ -239,15 +248,16 @@
 
 def gelu_rows(left, ffn, bias):
     rows, inner = left.shape
-    count, parts, tall_shard, wide = ffn.shape
-    columns = wide * parts // 2
+    count, wide = ffn.shape[0], ffn.shape[2]
+    tall_shard = inner // count
+    columns = bias.shape[0]
     tall = min(rows, 1024)
     return pl.pallas_call(
         gelu_kernel,
-        grid=(rows // tall, parts // 2),
+        grid=(rows // tall, columns // wide),
         in_specs=[
             pl.BlockSpec((tall, inner), lambda i, j: (i, 0)),
-            pl.BlockSpec((count, 1, tall_shard, wide), lambda i, j: (0, j, 0, 0)),
+            pl.BlockSpec((count, tall_shard, wide), lambda i, j: (0, j, 0)),
             pl.BlockSpec((1, wide), lambda i, j: (0, j)),
         ],
         out_specs=[pl.BlockSpec((tall, wide), lambda i, j: (i, j))] * 2,
@@ -268,14 +278,14 @@
 
 def down_rows(left, ffn):
     rows, inner = left.shape
-    count, parts, tall_shard, columns = ffn.shape
+    count, columns = ffn.shape[0], ffn.shape[2]
     tall, wide = min(rows, 1024), 256
     return pl.pallas_call(
         down_kernel,
         grid=(rows // tall, columns // wide),
         in_specs=[
             pl.BlockSpec((tall, inner), lambda i, j: (i, 0)),
-            pl.BlockSpec((count, parts // 2, tall_shard, wide), lambda i, j: (0, 1, 0, j)),
+            pl.BlockSpec((count, inner // count, wide), lambda i, j: (0, 1, j)),
         ],
         out_specs=pl.BlockSpec((tall, wide), lambda i, j: (i, j)),
         out_shape=jax.ShapeDtypeStruct((rows, columns), jnp.float32),
@@ -286,10 +296,11 @@
 
 
 def up_back_kernel(left_ref, right_ref, out_ref):
-    _, parts, _, wide = right_ref.shape
+    wide = right_ref.shape[2]
+    tall_shard = out_ref.shape[1] // right_ref.shape[0]
     total = None
-    for n in range(parts):
-        right = right_ref[:, n].reshape(-1, wide)
+    for n in range(right_ref.shape[1] // tall_shard):
+        right = right_ref[:, n * tall_shard : (n + 1) * tall_shard].reshape(-1, wide)
         part = nt(left_ref[:, n * wide : (n + 1) * wide], right)
         total = part if total is None else total + part
     out_ref[...] = total
@@ -297,14 +308,15 @@
 
 def up_back_rows(left, ffn):
     rows, inner = left.shape
-    count, parts, tall_shard, wide = ffn.shape
+    count, wide = ffn.shape[0], ffn.shape[2]
+    tall_shard = D // count
     tall, group = min(rows, 1024), 4
     return pl.pallas_call(
         up_back_kernel,
         grid=(rows // tall, count // group),
         in_specs=[
             pl.BlockSpec((tall, inner), lambda i, j: (i, 0)),
-            pl.BlockSpec((group, parts // 2, tall_shard, wide), lambda i, j: (j, 0, 0, 0)),
+            pl.BlockSpec((group, inner // wide * tall_shard, wide), lambda i, j: (j, 0, 0)),
         ],
         out_specs=pl.BlockSpec((tall, group * tall_shard), lambda i, j: (i, j)),
         out_shape=jax.ShapeDtypeStruct((rows, count * tall_shard), jnp.float32),
@@ -316,7 +328,7 @@
 
 def gelu_back_kernel(left_ref, right_ref, slope_ref, out_ref, sum_ref):
     right = right_ref[...].reshape(-1, right_ref.shape[-1])
-    step = min(256, left_ref.shape[0])
+    step = min(512, left_ref.shape[0])
     total = None
     for first in range(0, left_ref.shape[0], step):
         rows = slice(first, first + step)
@@ -330,16 +342,15 @@
 
 def gelu_back_rows(left, ffn, slope):
     rows, inner = left.shape
-    count, parts, tall_shard, _ = ffn.shape
-    columns = count * parts // 2 * tall_shard
-    tall, group = min(rows, 1024), 2
-    wide = group * parts // 2 * tall_shard
+    count, columns = ffn.shape[0], slope.shape[1]
+    tall, group = min(rows, 1024), 4
+    wide = columns // count * group
     out, sums = pl.pallas_call(
         gelu_back_kernel,
         grid=(rows // tall, columns // wide),
         in_specs=[
             pl.BlockSpec((tall, inner), lambda i, j: (i, 0)),
-            pl.BlockSpec((group, parts // 2, tall_shard, inner), lambda i, j: (j, 1, 0, 0)),
+            pl.BlockSpec((group, columns // count, inner), lambda i, j: (j, 1, 0)),
             pl.BlockSpec((tall, wide), lambda i, j: (i, j)),
         ],
         out_specs=[
@@ -924,19 +935,107 @@
     )
 
 
-def joined_grads(products, at):
-    blocks = []
-    for left, rights in products:
-        halves_of = [piece(r, 1, at, r.shape[1] // 2) for r in rights]
-        right = halves_of[0] if len(rights) == 1 else jnp.concatenate(halves_of, axis=1)
-        blocks.append(weight_grad(left, right).astype(jnp.bfloat16))
-    return blocks[0] if len(blocks) == 1 else jnp.concatenate(blocks, axis=1)
+def grads_kernel(plan, halved, *refs):
+    lefts = 1 + max(p[0] for p in plan)
+    rights = 1 + max(p[1] for p in plan)
+    outs = refs[-4 - (2 if halved else 1) : -4]
+    extra = refs[lefts + rights : -4 - len(outs)]
+    left_buf, right_buf, out_buf, sems = refs[-4:]
+    core = lax.axis_index("batch") % 2
+
+    def loads(n):
+        left, right, first, wide = plan[n]
+        copies = []
+        if n == 0 or plan[n - 1][0] != left:
+            slot = left % 2
+            copies.append(pltpu.make_async_copy(refs[left], left_buf.at[slot], sems.at[0, slot]))
+        source = refs[lefts + right].at[:, pl.ds(first, wide)]
+        target = right_buf.at[n % 2, :, pl.ds(0, wide)]
+        copies.append(pltpu.make_async_copy(source, target, sems.at[1, n % 2]))
+        return copies
+
+    def stores(n):
+        wide = plan[n][3]
+        at = sum(p[3] for p in plan[:n])
+        held = out_buf.at[n % 2]
+        if not halved:
+            place = outs[0].at[:, pl.ds(at, wide)]
+            return [pltpu.make_async_copy(held.at[:, pl.ds(0, wide)], place, sems.at[2, n % 2])]
+        copies = []
+        for side, out in enumerate(outs):
+            first = pl.multiple_of((core + 1 - side) % 2 * (wide // 2), wide // 2)
+            place = out.at[:, pl.ds(at // 2, wide // 2)]
+            source = held.at[:, pl.ds(first, wide // 2)]
+            copies.append(pltpu.make_async_copy(source, place, sems.at[2 + side, n % 2]))
+        return copies
+
+    for copy in loads(0):
+        copy.start()
+    if extra:
+        wide = extra[0].shape[1]
+        held = out_buf.at[0, :, pl.ds(0, wide)]
+        place = outs[0].at[:, pl.ds(sum(p[3] for p in plan), wide)]
+        for source, target in ((extra[0], held), (held, place)):
+            copy = pltpu.make_async_copy(source, target, sems.at[3, 0])
+            copy.start()
+            copy.wait()
+    for n, (left, _, _, wide) in enumerate(plan):
+        if n + 1 < len(plan):
+            for copy in loads(n + 1):
+                copy.start()
+        for copy in loads(n):
+            copy.wait()
+        if n >= 2:
+            for copy in stores(n - 2):
+                copy.wait()
+        grad = lax.dot_general(
+            left_buf[left % 2],
+            right_buf[n % 2, :, :wide],
+            (((0,), (0,)), ((), ())),
+            preferred_element_type=jnp.float32,
+        )
+        out_buf[n % 2, :, :wide] = grad.astype(out_buf.dtype)
+        for copy in stores(n):
+            copy.start()
+    for n in range(max(0, len(plan) - 2), len(plan)):
+        for copy in stores(n):
+            copy.wait()
+
+
+def joined_grads(products, halved, extra=()):
+    lefts, rights, plan = [], [], []
+    for left, group in products:
+        lefts.append(left)
+        for right in group:
+            rights.append(right)
+            wide = min(right.shape[1], D)
+            for first in range(0, right.shape[1], wide):
+                plan.append((len(lefts) - 1, len(rights) - 1, first, wide))
+    tokens, rows = lefts[0].shape
+    total = sum(p[3] for p in plan) + sum(e.shape[1] for e in extra)
+    shape = jax.ShapeDtypeStruct((rows, total // 2 if halved else total), jnp.bfloat16)
+    anywhere = pl.BlockSpec(memory_space=pl.ANY)
+    widest = max(p[3] for p in plan)
+    return pl.pallas_call(
+        functools.partial(grads_kernel, plan, halved),
+        in_specs=[anywhere] * (len(lefts) + len(rights) + len(extra)),
+        out_specs=[anywhere] * (2 if halved else 1),
+        out_shape=[shape] * (2 if halved else 1),
+        scratch_shapes=[
+            pltpu.VMEM((2, tokens, rows), jnp.bfloat16),
+            pltpu.VMEM((2, tokens, widest), jnp.bfloat16),
+            pltpu.VMEM((2, rows, widest), jnp.bfloat16),
+            pltpu.SemaphoreType.DMA((4, 2)),
+        ],
+        compiler_params=pltpu.CompilerParams(vmem_limit_bytes=48 * 2**20),
+        cost_estimate=SHORT,
+        name="joined_grads",
+    )(*lefts, *rights, *extra)
 
 
 def gradient_reduce(products, path):
     z, x, core, blk = grid_place()
-    given = joined_grads(products, 1 - core)
-    kept = joined_grads(products, core)
+    given, kept = joined_grads(products, True)
     (got,) = yield [(to_core, given)]
     rows, columns = kept.shape
     terms = [t.reshape(4, 2, rows // 8, columns) for t in (kept, got)]
@@ -965,10 +1064,13 @@
     left, right = jnp.where(core == 0, near, far), jnp.where(core == 0, far, near)
     results, first = [], 0
     for _, rights in products:
-        for wide in [r.shape[1] // 2 for r in rights]:
-            part = slice(first, first + wide)
-            results.append(jnp.concatenate([left[:, part], right[:, part]], axis=1))
-            first += wide
+        for whole_wide in [r.shape[1] for r in rights]:
+            blocks = []
+            for _ in range(0, whole_wide, min(whole_wide, D)):
+                wide = min(whole_wide, D) // 2
+                blocks += [left[:, first : first + wide], right[:, first : first + wide]]
+                first += wide
+            results.append(jnp.concatenate(blocks, axis=1))
     return results
 
 
@@ -976,15 +1078,29 @@
     return lax.psum_scatter(array, "batch", scatter_dimension=0, tiled=True)
 
 
-def whole_reduce(products):
-    grads = [weight_grad(left, right).astype(jnp.bfloat16) for left, right in products]
-    grad = grads[0] if len(grads) == 1 else jnp.concatenate(grads, axis=1)
+def whole_reduce(products, small=None):
     if not on_small_slice():
         yield []
-        return shared_out(grad)
+        grads = [shared_out(weight_grad(left, r)) for left, rights in products for r in rights]
+        grad = jnp.concatenate(grads, axis=1)
+        return grad if small is None else (grad, shared_out(small[0], 1), shared_out(small[1]))
+    extra = ()
+    if small is not None:
+        columns = jnp.concatenate([small[0].T, small[1].reshape(D, -1)], axis=1)
+        columns = jnp.pad(columns, ((0, 0), (0, PAIR - columns.shape[1])))
+        extra = (columns.astype(jnp.bfloat16),)
+    if len(products) == 1:
+        grad = weight_grad(products[0][0], products[0][1][0]).astype(jnp.bfloat16)
+    else:
+        (grad,) = joined_grads(products, False, extra)
     (part,) = yield [(over_batch, grad)]
     (got,) = yield [(swap_pair, part)]
-    return part.astype(jnp.float32) + got.astype(jnp.float32)
+    total = part.astype(jnp.float32) + got.astype(jnp.float32)
+    if small is None:
+        return total
+    total, columns, count = total[:, :-PAIR], total[:, -PAIR:], small[0].shape[0]
+    bias = columns[:, count : count + small[1].shape[0] // D]
+    return total, columns[:, :count].T, bias.reshape(-1)
 
 
 def batch_sender(bit):
@@ -1089,18 +1205,15 @@
     )
 
 
-def each_row(function, rows, arrays, into=None):
+def each_row(function, rows, arrays):
     if rows == 1:
-        return function(*arrays, into=into)
+        return function(*arrays)
 
     def cut(array, n):
         size = array.shape[0] // rows
         return array[n * size : (n + 1) * size]
 
-    results = []
-    for n in range(rows):
-        kept = None if into is None else [cut(a, n) for a in into]
-        results.append(function(*(cut(a, n) for a in arrays), into=kept))
+    results = [function(*(cut(a, n) for a in arrays)) for n in range(rows)]
     return [jnp.concatenate(group, axis=0) for group in zip(*results)]
 
 
@@ -1141,8 +1254,8 @@
     gain_full = fulls[8].T.astype(jnp.float32)
     shift_full = fulls[9].T.astype(jnp.float32)
     bias_full = fulls[10].reshape(-1).astype(jnp.float32)
-    up_parts = jnp.moveaxis(w_up.reshape(shard_rows, -1, D), 1, 0)
-    ffn_shard = jnp.concatenate([up_parts, w_down.reshape(-1, shard_rows, D)], axis=0)
+    up_parts = [w_up[:, n : n + D] for n in range(0, w_up.shape[1], D)]
+    ffn_shard = jnp.concatenate(up_parts + [w_down, jnp.zeros((8, D), low)], axis=0)
     ffn_full = lax.all_gather(ffn_shard, "batch", axis=0)
     x_rows = Flight(rows_in_steps(inputs))
     ids = Flight(rows_in_steps(jnp.stack([target_ids, memory_ids], axis=2)))
@@ -1158,9 +1271,9 @@
     memory_id_flat = ids[:, :, 1].reshape(-1)
     memory_flat = memory_rows.finish().reshape(-1, D)
 
-    def self_forward(q, k, v, id_row, into, pairs):
+    def self_forward(q, k, v, id_row, pairs):
         fq, fk = document_features(id_row, id_row)
-        return attention_forward(q, k, v, fq, fk, True, pairs, into)
+        return attention_forward(q, k, v, fq, fk, True, pairs)
 
     qkv = [dot32(x_flat, w).astype(low) for w in qkv_full]
     mixed_flat, self_lse = each_row(
@@ -1174,9 +1287,9 @@
     memory_keys = dot32(memory_flat, mk_full).astype(low)
     memory_values = dot32(memory_flat, mv_full).astype(low)
 
-    def cross_forward(q, k, v, id_row, memory_id_row, into, pairs):
+    def cross_forward(q, k, v, id_row, memory_id_row, pairs):
         fq, fk = document_features(id_row, memory_id_row)
-        return attention_forward(q, k, v, fq, fk, False, pairs, into)
+        return attention_forward(q, k, v, fq, fk, False, pairs)
 
     arrays = (cross_queries, memory_keys, memory_values, target_flat, memory_id_flat)
     mixed = each_row(functools.partial(cross_forward, pairs=(0, 2 * half)), rows, arrays)
@@ -1192,79 +1305,78 @@
     d_third, d_gain_three, d_shift_three = third_back(cot_flat.astype(jnp.float32))
     d_branch_three = d_third.astype(low)
     output = Flight(rows_out_steps(result.reshape(rows, length, D), low))
-    down_grad = Flight(whole_reduce([(hidden_low, d_branch_three)]))
+    down_grad = Flight(whole_reduce([(hidden_low, [d_branch_three])]))
     d_branch_three, d_third = tick((d_branch_three, d_third), output, down_grad)
     grad_bias_down = jnp.sum(d_branch_three.astype(jnp.float32), axis=0)
     d_pre, grad_bias_up = gelu_back_rows(d_branch_three, ffn_full, slope)
-    up_grad = Flight(whole_reduce([(second_low, d_pre)]))
+    up_grad = start_reduce([(second_low, [d_pre])], "xyz")
     d_pre = tick(d_pre, up_grad)
     d_second = ALPHA * d_third + up_back_rows(d_pre, ffn_full)
     second_back = jax.vjp(layer_norm, second_sum, gain_full[1], shift_full[1])[1]
     d_second_sum, d_gain_two, d_shift_two = second_back(d_second)
-    d_branch_two = d_second_sum.astype(low)
+    d_branch_two = tick(d_second_sum.astype(low), up_grad)
     d_cross = back_prod(d_branch_two, cross_out_full).astype(low)
 
-    def cross_backward(id_row, memory_id_row, *arrays, into, pairs):
+    def cross_backward(id_row, memory_id_row, *arrays, pairs):
         fq, fk = document_features(id_row, memory_id_row)
-        return attention_backward(fq, fk, *arrays, False, pairs, into)
+        return attention_backward(fq, fk, *arrays, False, pairs)
 
     arrays = (target_flat, memory_id_flat, cross_queries, memory_keys, memory_values)
     arrays += (cross_flat, cross_lse, d_cross)
     grads = each_row(functools.partial(cross_backward, pairs=(0, 2 * half)), rows, arrays)
-    d_cross_low, d_memory_keys, d_memory_values = tick(grads, output)
-    cross_grad = Flight(
-        whole_reduce(
-            [
-                (memory_flat, d_memory_keys),
-                (memory_flat, d_memory_values),
-                (first_low, d_cross_low),
-                (cross_flat, d_branch_two),
-            ]
-        )
-    )
-    d_cross_low = tick(d_cross_low, cross_grad)
+    d_cross_low, d_memory_keys, d_memory_values = tick(grads, output, up_grad)
     d_first = ALPHA * d_second_sum + back_prod(d_cross_low, cross_q_full)
     first_back = jax.vjp(layer_norm, first_sum, gain_full[0], shift_full[0])[1]
     d_first_sum, d_gain_one, d_shift_one = first_back(d_first)
     d_branch_one = d_first_sum.astype(low)
     grad_rows = [d_gain_one, d_gain_two, d_gain_three]
     grad_rows += [d_shift_one, d_shift_two, d_shift_three, grad_bias_down]
-    grad_small = Flight(small_reduce(jnp.stack(grad_rows), grad_bias_up))
+    cross_grad = Flight(
+        whole_reduce(
+            [
+                (memory_flat, [d_memory_keys, d_memory_values]),
+                (first_low, [d_cross_low]),
+                (cross_flat, [d_branch_two]),
+                (mixed_flat, [d_branch_one]),
+            ],
+            (jnp.stack(grad_rows), grad_bias_up),
+        )
+    )
+    d_branch_one = tick(d_branch_one, cross_grad, up_grad)
     d_self = back_prod(d_branch_one, out_full).astype(low)
-    d_self_halves = jnp.split(d_self, 2, axis=1)
-    d_self_halves = tick(d_self_halves, grad_small)
-
-    def self_backward(id_row, *arrays, into, pairs):
+    d_memory = back_prod(d_memory_keys, mk_full) + back_prod(d_memory_values, mv_full)
+    d_self, d_memory = lax.optimization_barrier((d_self, d_memory))
+    d_memory = Flight(rows_out_steps(d_memory.reshape(rows, length, D), jnp.float32))
+    d_self = tick(d_self, down_grad, d_memory)
+
+    def self_backward(id_row, *arrays, pairs):
         fq, fk = document_features(id_row, id_row)
-        return attention_backward(fq, fk, *arrays, True, pairs, into)
-
-    halves_of = [jnp.split(a, 2, axis=1) for a in (*qkv, mixed_flat, self_lse)]
-    arrays = (target_flat, *[a[0] for a in halves_of], d_self_halves[0])
+        return attention_backward(fq, fk, *arrays, True, pairs)
+
+    arrays = (target_flat, *qkv, mixed_flat, self_lse, d_self)
     grads_a = each_row(functools.partial(self_backward, pairs=(0, half)), rows, arrays)
-    d_memory = back_prod(d_memory_keys, mk_full) + back_prod(d_memory_values, mv_full)
-    d_memory = Flight(rows_out_steps(d_memory.reshape(rows, length, D), jnp.float32))
-    grads_a, d_self_b = tick((grads_a, d_self_halves[1]), grad_small)
-    early_grad = start_reduce([(x_flat, grads_a), (mixed_flat, [d_branch_one])], "xyz")
-    d_self_b = tick(d_self_b, grad_small, early_grad, d_memory)
-    arrays = (target_flat, *[a[1] for a in halves_of], d_self_b)
-    grads_b = each_row(functools.partial(self_backward, pairs=(0, half)), rows, arrays)
-    grads_b = tick(grads_b, grad_small, early_grad, d_memory)
-    late_grad = start_reduce([(x_flat, grads_b)], "xyz")
-    grads_b = tick(grads_b, grad_small, late_grad)
+    grads_a = tick(grads_a, up_grad, down_grad)
+    early_grad = start_reduce([(x_flat, grads_a)], "xzy")
+    d_self = tick(d_self, early_grad, d_memory)
+    arrays = (target_flat, *qkv, mixed_flat, self_lse, d_self)
+    grads_b = each_row(functools.partial(self_backward, pairs=(half, half)), rows, arrays)
+    grads_b = tick(grads_b, early_grad, up_grad)
     d_input = ALPHA * d_first_sum
     for grad_a, grad_b, weight in zip(grads_a, grads_b, qkv_full):
         d_input = d_input + back_prod(jnp.concatenate([grad_a, grad_b], axis=1), weight)
     d_input = Flight(rows_out_steps(d_input.reshape(rows, length, D), jnp.float32))
-    flights = [late_grad, early_grad, grad_small, d_memory, d_input, down_grad, up_grad]
-    token = grad_bias_up
-    for _ in range(3):
-        token = tick(token, *flights)
-    flights.append(cross_grad)
+    grads_b = tick(grads_b, d_input)
+    late_grad = start_reduce([(x_flat, grads_b)], "xzy")
+    token = tick(grads_b[0], late_grad, early_grad)
+    token = tick(token, late_grad)
+    flights = [late_grad, early_grad, d_input, cross_grad]
     while any(f.result is None for f in flights):
         token = tick(token, *flights)
-    grad_rows, grad_bias_up = grad_small.finish()
-    grad_kv, grad_cross_q, grad_cross_out = jnp.split(cross_grad.finish(), [2 * D, 3 * D], axis=1)
-    grad_qa, grad_ka, grad_va, grad_self_out = early_grad.finish()
+    grads, grad_rows, grad_bias_up = cross_grad.finish()
+    grad_kv, grad_cross_q, grad_cross_out, grad_self_out = jnp.split(
+        grads, [2 * D, 3 * D, 4 * D], axis=1
+    )
+    grad_qa, grad_ka, grad_va = early_grad.finish()
     grad_qb, grad_kb, grad_vb = late_grad.finish()
     return (
         output.finish(),
@@ -1275,7 +1387,7 @@
         grad_cross_q,
         grad_kv,
         grad_cross_out,
-        up_grad.finish(),
+        up_grad.finish()[0],
         down_grad.finish(),
         grad_bias_up,
         grad_rows[:3],

time: 740 us -> 649 us (0.88)
  waiting for transfers between devices: 165 us -> 117 us
  local copies, waits for them, and re-layouts: 85.6 us -> 43.7 us
  matrix products: 132 us -> 95.4 us
  starting transfers between devices: 33.2 us -> 51.1 us
  Pallas kernels: 227 us -> 239 us
  other arithmetic: 71.6 us -> 79.8 us
    ppermute x15, waiting for transfers between devices: 80 us -> 34.7 us  [swap_pair(): return lax.ppermute(array, 'blk', [(0, 1), (1, 0)])]
    dot_general x12 -> x1, matrix products: 51.9 us -> 11.3 us  [weight_grad(): jnp.einsum('tk,tn->kn', left_rows, right_rows, preferred_element_type=jnp...]
    ppermute x6 -> x9, waiting for transfers between devices: 2.5 us -> 20.6 us  [to_z(): lax.ppermute(array, 'batch', [(n, (n + 4 * step) % 16) for n in range(16)])]
    ppermute x6 -> x9, starting transfers between devices: 8.51 us -> 26.3 us  [to_z(): lax.ppermute(array, 'batch', [(n, (n + 4 * step) % 16) for n in range(16)])]
    pallas_call x6 -> x10, Pallas kernels: 179 us -> 193 us  [the longest x5 130 us: attention_call(): pl.pallas_call(functools.partial(kernel, causal), grid=(count,), in_specs...]
    unnamed x179 -> x149, local copies, waits for them, and re-layouts: 35 us -> 21.9 us
    reshape x5 -> x8, local copies, waits for them, and re-layouts: 12.3 us -> 1.28 us  [the longest x1 0.68 us: whole_reduce(): return (total, columns[:, :count].T, bias.reshape(-1))]
    all_gather x1, waiting for transfers between devices: 10.1 us -> 0.01 us  [whole_row_device(): ffn_full = lax.all_gather(ffn_shard, 'batch', axis=0)]
  transfers between devices with their start and end apart: 38 -> 40, of which waited for: 9 -> 13; matrix products, arithmetic and copies ran while one was open for 32% -> 26% of each run, Pallas kernels for 26% -> 32%
where the time goes in v3:
time: 649 us; the launch traced here: 641 us
  Pallas kernels  239 us (37%)
  waiting for transfers between devices  117 us (18%)
  matrix products  95.4 us (15%)
  other arithmetic  79.8 us (12%)
  starting transfers between devices  51.1 us (8%)
  local copies, waits for them, and re-layouts  43.7 us (7%)
  between operations  15.7 us (2%)
    pallas_call x5, Pallas kernels, attention_call(): pl.pallas_call(functools.partial(kernel, causal), grid=(count,), in_specs...  130 us
    all_gather x1, waiting for transfers between devices, gathered(): return lax.all_gather(shard, 'batch', axis=axis, tiled=True)  51.4 us
    dot_general x8, matrix products, back_prod(): jnp.einsum('tn,kn->tk', grad_rows, matrix, preferred_element_type=jnp.flo...  43.5 us
    pallas_call x4, Pallas kernels, joined_grads(): pl.pallas_call(functools.partial(grads_kernel, plan, halved), in_specs=[a...  42.5 us
    dot_general x8, matrix products, dot32(): return jnp.dot(left, right, preferred_element_type=jnp.float32)  40.6 us
    ppermute x15, waiting for transfers between devices, swap_pair(): return lax.ppermute(array, 'blk', [(0, 1), (1, 0)])  34.7 us
    ppermute x9, starting transfers between devices, to_z(): lax.ppermute(array, 'batch', [(n, (n + 4 * step) % 16) for n in range(16)])  26.3 us
    convert_element_type x12, other arithmetic, summed_low(): return total.astype(jnp.bfloat16)  22.4 us
  transfers between devices with their start and end apart: 40, of which 13 were waited for; matrix products, arithmetic and copies ran while one was open for 26% of the time, Pallas kernels for 32%

profile of v3, /device:TPU:0, one launch (start us, length us, event | category | flops | bytes accessed | tf_op | source)
XLA Modules:
  0.0 641.0 jit_solution(13552858756572779260)
XLA Ops:
  9.8 3.1 concatenate.65
  27.0 21.1 %collective-permute-done.1 = s32[1,512,2]{1,0,2:T(1,128)S(1)} collective-permute-done((s32[1,512,2]{1,0,2:T(1,128)S(1)}, s32[1,512,2]{1,0,2:T(1,128)S(1)}, u32[]{:S(2)}, u32[]{:S(2)}) %collective-permute-start.1) | collective-permute-done | bytes 4128 | tf_op jit(solution)/shard_map/ppermute | solution.py:702
  54.6 51.4 %all-gather.4.cloned.1.call-done = bf16[1024,8320]{1,0:T(8,128)(2,1)} async-done(((bf16[64,8320]{1,0:T(8,128)(2,1)}), bf16[1024,8320]{1,0:T(8,128)(2,1)}) %all-gather.4.cloned.1.call-update) | async-done | bytes 17039376 | tf_op jit(solution)/shard_map/all_gather | solution.py:743
  106.0 3.9 convolution_convert_fusion.8.q_ref
  110.0 6.0 convolution_convert_fusion.7.k_ref
  115.9 5.3 convolution_convert_fusion.6.v_ref
  121.3 20.0 %attention_forward.2 = (bf16[1024,1024]{1,0:T(8,128)(2,1)S(1)}, f32[1024,1024]{1,0:T(8,128)}) custom-call(bf16[1024,1024]{1,0:T(8,128)(2,1)S(1)} %convolution_convert_fusion.8.q_ref, bf16[1024,1024]{1,0:T(8,128)(2,1)} %convolution_convert_fusion.7.k_ref, bf16[1024,1024]{1,0:T(8,128)(2,1)} %convolution_convert_fusion.6.v_ref, ...), custom_call_target="tpu_custom_call" | custom-call | flops 1024 | bytes 1024 | tf_op jit(solution)/shard_map/attention_forward/pallas_call | solution.py:187
  144.0 4.0 fusion.64
  151.3 4.7 convolution_convert_fusion.5.q_ref
  159.1 6.0 convolution_convert_fusion.4.k_ref
  165.1 5.4 convolution_convert_fusion.3.v_ref
  170.5 25.4 %attention_forward.3 = (bf16[1024,1024]{1,0:T(8,128)(2,1)S(1)}, f32[1024,1024]{1,0:T(8,128)}) custom-call(bf16[1024,1024]{1,0:T(8,128)(2,1)S(1)} %convolution_convert_fusion.5.q_ref, bf16[1024,1024]{1,0:T(8,128)(2,1)} %convolution_convert_fusion.4.k_ref, bf16[1024,1024]{1,0:T(8,128)(2,1)} %convolution_convert_fusion.3.v_ref, ...), custom_call_target="tpu_custom_call" | custom-call | flops 1024 | bytes 1024 | tf_op jit(solution)/shard_map/attention_forward/pallas_call | solution.py:187
  197.1 5.3 fusion.65
  206.4 20.6 %gelu_rows.1 = (bf16[1024,4096]{1,0:T(8,128)(2,1)}, f32[1024,4096]{1,0:T(8,128)}) custom-call(bf16[1024,1024]{1,0:T(8,128)(2,1)} %fusion.5.left_ref.refs_0_, bf16[16,520,1024]{2,1,0:T(8,128)(2,1)} %bitcast.85, f32[1,4096]{1,0:T(1,128)} %reshape.298.bias_ref), custom_call_target="tpu_custom_call" | custom-call | flops 1024 | bytes 1024 | tf_op jit(solution)/shard_map/gelu_rows/pallas_call | solution.py:255
  227.0 13.8 %down_rows.1 = f32[1024,1024]{1,0:T(8,128)S(1)} custom-call(bf16[1024,4096]{1,0:T(8,128)(2,1)} %get-tuple-element.172.left_ref, bf16[16,520,1024]{2,1,0:T(8,128)(2,1)} %bitcast.86), custom_call_target="tpu_custom_call" | custom-call | flops 1024 | bytes 1024 | tf_op jit(solution)/shard_map/down_rows/pallas_call | solution.py:283
  258.7 11.3 %convolution_convert_fusion = bf16[4096,1024]{1,0:T(8,128)(2,1)} fusion(bf16[1024,4096]{1,0:T(8,128)(2,1)S(1)} %bitcast.90, bf16[1024,1024]{1,0:T(8,128)(2,1)S(1)} %get-tuple-element.375), kind=kOutput, calls=%fused_computation | convolution fusion | flops 8594128896 | bytes 18874368 | tf_op jit(solution)/shard_map/tk,tn->kn/dot_general | solution.py:394
  270.1 17.6 %gelu_back_rows.1 = (bf16[1024,4096]{1,0:T(8,128)(2,1)}, f32[1,1,4096]{2,1,0:T(1,128)S(1)}) custom-call(bf16[1024,1024]{1,0:T(8,128)(2,1)S(1)} %get-tuple-element.375, bf16[16,520,1024]{2,1,0:T(8,128)(2,1)} %bitcast.87, f32[1024,4096]{1,0:T(8,128)} %get-tuple-element.179.slope_ref), custom_call_target="tpu_custom_call" | custom-call | flops 1024 | bytes 1024 | tf_op jit(solution)/shard_map/gelu_back_rows/pallas_call | solution.py:348
  287.7 12.9 %joined_grads.4 = (bf16[1024,2048]{1,0:T(8,128)(2,1)}, bf16[1024,2048]{1,0:T(8,128)(2,1)}) custom-call(bf16[1024,1024]{1,0:T(8,128)(2,1)S(1)} %copy-done.1, bf16[1024,4096]{1,0:T(8,128)(2,1)} %get-tuple-element.182.refs_1_.left_ref), custom_call_target="tpu_custom_call" | custom-call | flops 1024 | bytes 1024 | tf_op jit(solution)/shard_map/joined_grads/pallas_call | solution.py:1019
  300.7 14.2 %up_back_rows.1 = f32[1024,1024]{1,0:T(8,128)S(1)} custom-call(bf16[1024,4096]{1,0:T(8,128)(2,1)} %get-tuple-element.182.refs_1_.left_ref, bf16[16,520,1024]{2,1,0:T(8,128)(2,1)} %bitcast.88), custom_call_target="tpu_custom_call" | custom-call | flops 1024 | bytes 1024 | tf_op jit(solution)/shard_map/up_back_rows/pallas_call | solution.py:314
  323.5 3.9 add_convert_fusion
  330.2 3.1 maximum_bitcast_fusion.1.refs_0_
  334.4 5.9 convolution_convert_fusion.2.do_ref
  340.3 48.5 %attention_backward.3 = (bf16[1024,1024]{1,0:T(8,128)(2,1)S(1)}, bf16[1024,1024]{1,0:T(8,128)(2,1)S(1)}, bf16[1024,1024]{1,0:T(8,128)(2,1)}) custom-call(bf16[1024,1024]{1,0:T(8,128)(2,1)} %copy-done.8, bf16[1024,1024]{1,0:T(8,128)(2,1)} %convolution_convert_fusion.4.k_ref, bf16[1024,1024]{1,0:T(8,128)(2,1)} %convolution_convert_fusion.3.v_ref, ...), custom_call_target="tpu_custom_call" | custom-call | flops 1024 | bytes 1024 | tf_op jit(solution)/shard_map/attention_backward/pallas_call | solution.py:187
  388.9 3.6 collective-permute-done.6
  392.4 3.1 add_convert_fusion.3
  396.9 6.7 %multiply_reduce_fusion.1 = (bf16[1024]{0:T(1024)(128)(2,1)S(1)}, f32[1024]{0:T(1024)S(1)}, bf16[1024]{0:T(1024)(128)(2,1)S(1)}, f32[1024,1024]{1,0:T(8,128)}) fusion(f32[1024,1024]{1,0:T(8,128)S(1)} %copy-done.22, f32[1024]{0:T(1024)S(1)} %fusion.49, f32[1024]{0:T(1024)S(1)} %broadcast_multiply_fusion.2, f32[1024]{0:T(1024)S(1)} %get-tuple-element.365, ...), kind=kOutput, calls=%fused_computation.14 | convolution fusion | flops 2159014912 | bytes 16801792 | tf_op jit(solution)/shard_map/tn,kn->tk/dot_general | solution.py:398
  404.2 4.3 fusion.57
  413.0 16.4 %joined_grads.5 = bf16[1024,5248]{1,0:T(8,128)(2,1)} custom-call(bf16[1024,1024]{1,0:T(8,128)(2,1)S(1)} %copy-done.6, bf16[1024,1024]{1,0:T(8,128)(2,1)S(1)} %copy-done.5, bf16[1024,1024]{1,0:T(8,128)(2,1)} %copy-done.7, bf16[1024,1024]{1,0:T(8,128)(2,1)} %copy-done, bf16[1024,1024]{1,0:T(8,128)(2,1)} %copy-done.9, ...), custom_call_target="tpu_custom_call" | custom-call | flops 1024 | bytes 1024 | tf_op jit(solution)/shard_map/joined_grads/pallas_call | solution.py:1019
  429.4 4.1 add_convert_fusion.7
  435.1 4.1 fusion.22
  439.3 4.3 convolution_add_fusion
  443.6 7.2 %convolution_convert_fusion.1.do_ref = bf16[1024,1024]{1,0:T(8,128)(2,1)} fusion(bf16[1024,1024]{1,0:T(8,128)(2,1)S(1)} %copy-done.28, bf16[1024,8320]{1,0:T(8,128)(2,1)} %all-gather.4.cloned.1.call-done), kind=kOutput, calls=%fused_computation.60 | convolution fusion | flops 2148532224 | bytes 6291456 | tf_op jit(solution)/shard_map/tn,kn->tk/dot_general | solution.py:398
  462.3 17.8 %attention_backward.4 = (bf16[1024,512]{1,0:T(8,128)(2,1)S(1)}, bf16[1024,512]{1,0:T(8,128)(2,1)S(1)}, bf16[1024,512]{1,0:T(8,128)(2,1)S(1)}) custom-call(bf16[1024,1024]{1,0:T(8,128)(2,1)S(1)} %copy-done.3, bf16[1024,1024]{1,0:T(8,128)(2,1)} %convolution_convert_fusion.7.k_ref, bf16[1024,1024]{1,0:T(8,128)(2,1)} %convolution_convert_fusion.6.v_ref, ...), custom_call_target="tpu_custom_call" | custom-call | flops 1024 | bytes 1024 | tf_op jit(solution)/shard_map/attention_backward/pallas_call | solution.py:187
  480.2 3.2 collective-permute-done.9
  483.4 4.1 collective-permute-done.11
  489.4 6.7 %joined_grads.6 = (bf16[1024,768]{1,0:T(8,128)(2,1)}, bf16[1024,768]{1,0:T(8,128)(2,1)}) custom-call(bf16[1024,1024]{1,0:T(8,128)(2,1)} %maximum_bitcast_fusion.refs_0_, bf16[1024,512]{1,0:T(8,128)(2,1)S(1)} %get-tuple-element.226.refs_1_, bf16[1024,512]{1,0:T(8,128)(2,1)S(1)} %get-tuple-element.229.refs_2_, bf16[1024,512]{1,0:T(8,128)(2,1)S(1)} %get-tuple-element.230.refs_3_), custom_call_target="tpu_custom_call" | custom-call | flops 1024 | bytes 1024 | tf_op jit(solution)/shard_map/joined_grads/pallas_call | solution.py:1019
  501.7 18.2 %attention_backward.5 = (bf16[1024,512]{1,0:T(8,128)(2,1)S(1)}, bf16[1024,512]{1,0:T(8,128)(2,1)S(1)}, bf16[1024,512]{1,0:T(8,128)(2,1)S(1)}) custom-call(bf16[1024,1024]{1,0:T(8,128)(2,1)S(1)} %copy-done.3, bf16[1024,1024]{1,0:T(8,128)(2,1)} %convolution_convert_fusion.7.k_ref, bf16[1024,1024]{1,0:T(8,128)(2,1)} %convolution_convert_fusion.6.v_ref, ...), custom_call_target="tpu_custom_call" | custom-call | flops 1024 | bytes 1024 | tf_op jit(solution)/shard_map/attention_backward/pallas_call | solution.py:187
  523.0 4.0 fusion.10
  527.0 6.1 fusion.6
  533.1 5.0 add_add_fusion.3
  540.2 6.6 %joined_grads.7 = (bf16[1024,768]{1,0:T(8,128)(2,1)S(1)}, bf16[1024,768]{1,0:T(8,128)(2,1)}) custom-call(bf16[1024,1024]{1,0:T(8,128)(2,1)} %maximum_bitcast_fusion.refs_0_, bf16[1024,512]{1,0:T(8,128)(2,1)S(1)} %get-tuple-element.245, bf16[1024,512]{1,0:T(8,128)(2,1)S(1)} %get-tuple-element.246, bf16[1024,512]{1,0:T(8,128)(2,1)S(1)} %get-tuple-element.247), custom_call_target="tpu_custom_call" | custom-call | flops 1024 | bytes 1024 | tf_op jit(solution)/shard_map/joined_grads/pallas_call | solution.py:1019
  546.8 3.8 collective-permute-done.17
  556.4 11.1 %collective-permute-start.20 = (bf16[1,1,128,768]{3,2,1,0:T(8,128)(2,1)S(1)}, bf16[1,1,128,768]{3,2,1,0:T(8,128)(2,1)S(1)}, u32[]{:S(2)}, u32[]{:S(2)}) collective-permute-start(bf16[1,1,128,768]{3,2,1,0:T(8,128)(2,1)S(1)} %get-tuple-element.259), channel_id=1, source_target_pairs={{0,8},{2,10},{4,12},{6,14},{8,16},{10,18},{12,20},{14,22},{16,24},... | collective-permute-start | bytes 589832 | tf_op jit(solution)/shard_map/ppermute | solution.py:810
  570.0 8.9 %collective-permute-done.20 = bf16[1,1,128,768]{3,2,1,0:T(8,128)(2,1)S(1)} collective-permute-done((bf16[1,1,128,768]{3,2,1,0:T(8,128)(2,1)S(1)}, bf16[1,1,128,768]{3,2,1,0:T(8,128)(2,1)S(1)}, u32[]{:S(2)}, u32[]{:S(2)}) %collective-permute-start.20) | collective-permute-done | bytes 196640 | tf_op jit(solution)/shard_map/ppermute | solution.py:810
  578.9 8.2 %collective-permute-done.21 = bf16[1,1,128,768]{3,2,1,0:T(8,128)(2,1)S(1)} collective-permute-done((bf16[1,1,128,768]{3,2,1,0:T(8,128)(2,1)S(1)}, bf16[1,1,128,768]{3,2,1,0:T(8,128)(2,1)S(1)}, u32[]{:S(2)}, u32[]{:S(2)}) %collective-permute-start.21) | collective-permute-done | bytes 196640 | tf_op jit(solution)/shard_map/ppermute | solution.py:810
  590.7 4.8 collective-permute-start.24
  600.2 4.1 convert_select_fusion.1
  609.8 7.3 %collective-permute-done.28 = bf16[64,5248]{1,0:T(8,128)(2,1)S(1)} collective-permute-done((bf16[64,5248]{1,0:T(8,128)(2,1)}, bf16[64,5248]{1,0:T(8,128)(2,1)S(1)}, u32[]{:S(2)}, u32[]{:S(2)}) %collective-permute-start.28) | collective-permute-done | bytes 671776 | tf_op jit(solution)/shard_map/ppermute | solution.py:702
  (323 shorter events, 138.0 us)
Async XLA Ops:
  7.2 98.8 %all-gather.4.cloned.1.call-start = ((), (), s32[]{:S(2)}) async-start(), calls=%async_computation.2 | async-start | bytes 18104320 | tf_op jit(solution)/shard_map/all_gather | solution.py:743
  12.9 193.6 %all-gather.6.cloned.1.call-start = ((), (), s32[]{:S(2)}) async-start(), calls=%async_computation.5 | async-start | bytes 18104320 | tf_op jit(solution)/shard_map/all_gather | solution.py:1259
  20.6 431.4 %reduce-scatter.3.cloned.1.call-start = ((), (), s32[]{:S(2)}) async-start(), calls=%async_computation.3 | async-start | bytes 8912896 | tf_op jit(solution)/shard_map/reduce_scatter | solution.py:1078
  21.8 26.4 %collective-permute-start = (bf16[1,512,1024]{2,1,0:T(8,128)(2,1)}, bf16[1,512,1024]{2,1,0:T(8,128)(2,1)S(1)}, u32[]{:S(2)}, u32[]{:S(2)}) collective-permute-start(bf16[1,512,1024]{2,1,0:T(8,128)(2,1)} %constant_dynamic-slice_fusion.6), channel_id=1, source_target_pairs={{0,1},{1,0},{2,3},{3,2},{4,5},{5,4},{6,7},{7,6},{8,9},{9,8},{10,11... | collective-permute-start | bytes 3145736 | tf_op jit(solution)/shard_map/ppermute | solution.py:702
  24.7 23.5 %collective-permute-start.1 = (s32[1,512,2]{1,0,2:T(1,128)S(1)}, s32[1,512,2]{1,0,2:T(1,128)S(1)}, u32[]{:S(2)}, u32[]{:S(2)}) collective-permute-start(s32[1,512,2]{1,0,2:T(1,128)S(1)} %fusion.47), channel_id=1, source_target_pairs={{0,1},{1,0},{2,3},{3,2},{4,5},{5,4},{6,7},{7,6},{8,9},{9,8},{10,11... | collective-permute-start | bytes 12296 | tf_op jit(solution)/shard_map/ppermute | solution.py:702
  48.2 109.5 %collective-permute-start.2 = (bf16[1,512,1024]{2,1,0:T(8,128)(2,1)}, bf16[1,512,1024]{2,1,0:T(8,128)(2,1)}, u32[]{:S(2)}, u32[]{:S(2)}) collective-permute-start(bf16[1,512,1024]{2,1,0:T(8,128)(2,1)} %constant_dynamic-slice_fusion.3), channel_id=1, source_target_pairs={{0,1},{1,0},{2,3},{3,2},{4,5},{5,4},{6,7},{7,6},{8,9},{9,8},{10,11... | collective-permute-start | bytes 3145736 | tf_op jit(solution)/shard_map/ppermute | solution.py:702
  54.6 89.4 %copy-start.30 = (bf16[1,512,1024]{2,1,0:T(8,128)(2,1)}, bf16[1,512,1024]{2,1,0:T(8,128)(2,1)S(1)}, u32[]{:S(2)}) copy-start(bf16[1,512,1024]{2,1,0:T(8,128)(2,1)S(1)} %get-tuple-element.404) | copy-start | bytes 3145732
  54.6 89.4 %copy-start.31 = (bf16[1,512,1024]{2,1,0:T(8,128)(2,1)}, bf16[1,512,1024]{2,1,0:T(8,128)(2,1)S(1)}, u32[]{:S(2)}) copy-start(bf16[1,512,1024]{2,1,0:T(8,128)(2,1)S(1)} %get-tuple-element.405) | copy-start | bytes 3145732
  156.1 41.0 %collective-permute-start.3 = (bf16[1,512,1024]{2,1,0:T(8,128)(2,1)}, bf16[1,512,1024]{2,1,0:T(8,128)(2,1)}, u32[]{:S(2)}, u32[]{:S(2)}) collective-permute-start(bf16[1,512,1024]{2,1,0:T(8,128)(2,1)} %constant_dynamic-slice_fusion.2), channel_id=1, source_target_pairs={{0,1},{1,0},{2,3},{3,2},{4,5},{5,4},{6,7},{7,6},{8,9},{9,8},{10,11... | collective-permute-start | bytes 3145736 | tf_op jit(solution)/shard_map/ppermute | solution.py:702
  270.1 317.8 %reduce-scatter.5.cloned.1.call-start = ((), (), s32[]{:S(2)}) async-start(), calls=%async_computation.4 | async-start | bytes 11419648 | tf_op jit(solution)/shard_map/reduce_scatter | solution.py:1078
  270.1 17.6 %copy-start.1 = (bf16[1024,1024]{1,0:T(8,128)(2,1)S(1)}, bf16[1024,1024]{1,0:T(8,128)(2,1)}, u32[]{:S(2)}) copy-start(bf16[1024,1024]{1,0:T(8,128)(2,1)} %fusion.5.left_ref.refs_0_) | copy-start | bytes 6291460
  300.6 20.0 %collective-permute-start.4 = (bf16[1024,2048]{1,0:T(8,128)(2,1)}, bf16[1024,2048]{1,0:T(8,128)(2,1)}, u32[]{:S(2)}, u32[]{:S(2)}) collective-permute-start(bf16[1024,2048]{1,0:T(8,128)(2,1)} %get-tuple-element.183), channel_id=1, source_target_pairs={{0,2},{2,0},{4,6},{6,4},{8,10},{10,8},{12,14},{14,12},{16,18},{18,... | collective-permute-start | bytes 12582920 | tf_op jit(solution)/shard_map/ppermute | solution.py:802
  327.4 65.1 %collective-permute-start.6 = (bf16[4,1,128,2048]{3,2,1,0:T(8,128)(2,1)}, bf16[4,1,128,2048]{3,2,1,0:T(8,128)(2,1)}, u32[]{:S(2)}, u32[]{:S(2)}) collective-permute-start(bf16[4,1,128,2048]{3,2,1,0:T(8,128)(2,1)} %add_convert_fusion), channel_id=1, source_target_pairs={{0,4},{2,6},{4,0},{6,2},{8,12},{10,14},{12,8},{14,10},{16,20},{18,... | collective-permute-start | bytes 6291464 | tf_op jit(solution)/shard_map/ppermute | solution.py:806
  329.0 59.8 %collective-permute-start.5 = (bf16[1,512,1024]{2,1,0:T(8,128)(2,1)}, bf16[1,512,1024]{2,1,0:T(8,128)(2,1)}, u32[]{:S(2)}, u32[]{:S(2)}) collective-permute-start(bf16[1,512,1024]{2,1,0:T(8,128)(2,1)} %fusion.40), channel_id=1, source_target_pairs={{0,1},{1,0},{2,3},{3,2},{4,5},{5,4},{6,7},{7,6},{8,9},{9,8},{10,11... | collective-permute-start | bytes 3145736 | tf_op jit(solution)/shard_map/ppermute | solution.py:702
  340.3 56.6 %copy-start.26 = (f32[1024,1024]{1,0:T(8,128)S(1)}, f32[1024,1024]{1,0:T(8,128)}, u32[]{:S(2)}) copy-start(f32[1024,1024]{1,0:T(8,128)} %copy-done.25) | copy-start | bytes 12582916
  395.5 33.9 %collective-permute-start.7 = (bf16[4,1,128,1024]{3,2,1,0:T(8,128)(2,1)S(1)}, bf16[4,1,128,1024]{3,2,1,0:T(8,128)(2,1)S(1)}, u32[]{:S(2)}, u32[]{:S(2)}) collective-permute-start(bf16[4,1,128,1024]{3,2,1,0:T(8,128)(2,1)S(1)} %add_convert_fusion.3), channel_id=1, source_target_pairs={{0,1},{1,0},{2,3},{3,2},{4,5},{5,4},{6,7},{7,6},{8,9},{9,8},{10,11... | collective-permute-start | bytes 3145736 | tf_op jit(solution)/shard_map/ppermute | solution.py:702
  452.0 44.1 %collective-permute-start.12 = (bf16[1,512,1024]{2,1,0:T(8,128)(2,1)}, bf16[1,512,1024]{2,1,0:T(8,128)(2,1)}, u32[]{:S(2)}, u32[]{:S(2)}) collective-permute-start(bf16[1,512,1024]{2,1,0:T(8,128)(2,1)} %fusion.41), channel_id=1, source_target_pairs={{0,1},{1,0},{2,3},{3,2},{4,5},{5,4},{6,7},{7,6},{8,9},{9,8},{10,11... | collective-permute-start | bytes 3145736 | tf_op jit(solution)/shard_map/ppermute | solution.py:702
  452.5 35.0 %collective-permute-start.11 = (bf16[256,1024]{1,0:T(8,128)(2,1)}, bf16[256,1024]{1,0:T(8,128)(2,1)S(1)}, u32[]{:S(2)}, u32[]{:S(2)}) collective-permute-start(bf16[256,1024]{1,0:T(8,128)(2,1)} %reduce-scatter.3.cloned.1.call-done), channel_id=1, source_target_pairs={{0,1},{1,0},{2,3},{3,2},{4,5},{5,4},{6,7},{7,6},{8,9},{9,8},{10,11... | collective-permute-start | bytes 1572872 | tf_op jit(solution)/shard_map/ppermute | solution.py:702
  454.0 26.1 %collective-permute-start.8 = (bf16[1,1,128,1024]{3,2,1,0:T(8,128)(2,1)}, bf16[1,1,128,1024]{3,2,1,0:T(8,128)(2,1)}, u32[]{:S(2)}, u32[]{:S(2)}) collective-permute-start(bf16[1,1,128,1024]{3,2,1,0:T(8,128)(2,1)} %get-tuple-element.216), channel_id=1, source_target_pairs={{0,8},{2,10},{4,12},{6,14},{8,16},{10,18},{12,20},{14,22},{16,24},... | collective-permute-start | bytes 786440 | tf_op jit(solution)/shard_map/ppermute | solution.py:810
  455.4 27.9 %collective-permute-start.9 = (bf16[1,1,128,1024]{3,2,1,0:T(8,128)(2,1)}, bf16[1,1,128,1024]{3,2,1,0:T(8,128)(2,1)}, u32[]{:S(2)}, u32[]{:S(2)}) collective-permute-start(bf16[1,1,128,1024]{3,2,1,0:T(8,128)(2,1)} %get-tuple-element.217), channel_id=1, source_target_pairs={{0,16},{2,18},{4,20},{6,22},{8,24},{10,26},{12,28},{14,30},{16,0},... | collective-permute-start | bytes 786440 | tf_op jit(solution)/shard_map/ppermute | solution.py:810
  457.9 25.5 %collective-permute-start.10 = (bf16[1,1,128,1024]{3,2,1,0:T(8,128)(2,1)S(1)}, bf16[1,1,128,1024]{3,2,1,0:T(8,128)(2,1)}, u32[]{:S(2)}, u32[]{:S(2)}) collective-permute-start(bf16[1,1,128,1024]{3,2,1,0:T(8,128)(2,1)S(1)} %get-tuple-element.218), channel_id=1, source_target_pairs={{0,24},{2,26},{4,28},{6,30},{8,0},{10,2},{12,4},{14,6},{16,8},{18,... | collective-permute-start | bytes 786440 | tf_op jit(solution)/shard_map/ppermute | solution.py:810
  496.2 23.8 %collective-permute-start.13 = (bf16[1024,768]{1,0:T(8,128)(2,1)}, bf16[1024,768]{1,0:T(8,128)(2,1)}, u32[]{:S(2)}, u32[]{:S(2)}) collective-permute-start(bf16[1024,768]{1,0:T(8,128)(2,1)} %get-tuple-element.236), channel_id=1, source_target_pairs={{0,2},{2,0},{4,6},{6,4},{8,10},{10,8},{12,14},{14,12},{16,18},{18,... | collective-permute-start | bytes 4718600 | tf_op jit(solution)/shard_map/ppermute | solution.py:802
  498.0 21.9 %collective-permute-start.14 = (bf16[64,1024]{1,0:T(8,128)(2,1)S(1)}, bf16[64,1024]{1,0:T(8,128)(2,1)S(1)}, u32[]{:S(2)}, u32[]{:S(2)}) collective-permute-start(bf16[64,1024]{1,0:T(8,128)(2,1)S(1)} %get-tuple-element.237), channel_id=1, source_target_pairs={{0,1},{1,0},{2,3},{3,2},{4,5},{5,4},{6,7},{7,6},{8,9},{9,8},{10,11... | collective-permute-start | bytes 393224 | tf_op jit(solution)/shard_map/ppermute | solution.py:702
  499.1 20.9 %collective-permute-start.15 = (bf16[64,1024]{1,0:T(8,128)(2,1)S(1)}, bf16[64,1024]{1,0:T(8,128)(2,1)S(1)}, u32[]{:S(2)}, u32[]{:S(2)}) collective-permute-start(bf16[64,1024]{1,0:T(8,128)(2,1)S(1)} %get-tuple-element.239), channel_id=1, source_target_pairs={{0,2},{2,0},{4,6},{6,4},{8,10},{10,8},{12,14},{14,12},{16,18},{18,... | collective-permute-start | bytes 393224 | tf_op jit(solution)/shard_map/ppermute | solution.py:802
  499.3 20.7 %collective-permute-start.16 = (bf16[64,1024]{1,0:T(8,128)(2,1)S(1)}, bf16[64,1024]{1,0:T(8,128)(2,1)S(1)}, u32[]{:S(2)}, u32[]{:S(2)}) collective-permute-start(bf16[64,1024]{1,0:T(8,128)(2,1)S(1)} %get-tuple-element.239), channel_id=1, source_target_pairs={{0,3},{1,2},{2,1},{3,0},{4,7},{5,6},{6,5},{7,4},{8,11},{9,10},{10,... | collective-permute-start | bytes 393224 | tf_op jit(solution)/shard_map/ppermute | solution.py:815
  501.7 18.3 %copy-start.40 = (bf16[1024,768]{1,0:T(8,128)(2,1)S(1)}, bf16[1024,768]{1,0:T(8,128)(2,1)}, u32[]{:S(2)}) copy-start(bf16[1024,768]{1,0:T(8,128)(2,1)} %get-tuple-element.243) | copy-start | bytes 4718596
  501.7 21.3 %copy-start.17 = (bf16[1024,512]{1,0:T(8,128)(2,1)S(1)}, bf16[1024,512]{1,0:T(8,128)(2,1)}, u32[]{:S(2)}) copy-start(bf16[1024,512]{1,0:T(8,128)(2,1)} %copy-done.16) | copy-start | bytes 3145732
  521.4 29.2 %collective-permute-start.17 = (bf16[4,1,128,768]{3,2,1,0:T(8,128)(2,1)S(1)}, bf16[4,1,128,768]{3,2,1,0:T(8,128)(2,1)S(1)}, u32[]{:S(2)}, u32[]{:S(2)}) collective-permute-start(bf16[4,1,128,768]{3,2,1,0:T(8,128)(2,1)S(1)} %add_convert_fusion.5), channel_id=1, source_target_pairs={{0,4},{2,6},{4,0},{6,2},{8,12},{10,14},{12,8},{14,10},{16,20},{18,... | collective-permute-start | bytes 2359304 | tf_op jit(solution)/shard_map/ppermute | solution.py:806
  552.2 3.5 collective-permute-start.18
  553.4 33.8 %collective-permute-start.23 = (bf16[1,512,1024]{2,1,0:T(8,128)(2,1)S(1)}, bf16[1,512,1024]{2,1,0:T(8,128)(2,1)S(1)}, u32[]{:S(2)}, u32[]{:S(2)}) collective-permute-start(bf16[1,512,1024]{2,1,0:T(8,128)(2,1)S(1)} %fusion.42), channel_id=1, source_target_pairs={{0,1},{1,0},{2,3},{3,2},{4,5},{5,4},{6,7},{7,6},{8,9},{9,8},{10,11... | collective-permute-start | bytes 3145736 | tf_op jit(solution)/shard_map/ppermute | solution.py:702
  555.8 32.0 %collective-permute-start.19 = (bf16[4,1,128,768]{3,2,1,0:T(8,128)(2,1)S(1)}, bf16[4,1,128,768]{3,2,1,0:T(8,128)(2,1)}, u32[]{:S(2)}, u32[]{:S(2)}) collective-permute-start(bf16[4,1,128,768]{3,2,1,0:T(8,128)(2,1)S(1)} %add_convert_fusion.4), channel_id=1, source_target_pairs={{0,4},{2,6},{4,0},{6,2},{8,12},{10,14},{12,8},{14,10},{16,20},{18,... | collective-permute-start | bytes 2359304 | tf_op jit(solution)/shard_map/ppermute | solution.py:806
  556.4 22.5 %collective-permute-start.20 = (bf16[1,1,128,768]{3,2,1,0:T(8,128)(2,1)S(1)}, bf16[1,1,128,768]{3,2,1,0:T(8,128)(2,1)S(1)}, u32[]{:S(2)}, u32[]{:S(2)}) collective-permute-start(bf16[1,1,128,768]{3,2,1,0:T(8,128)(2,1)S(1)} %get-tuple-element.259), channel_id=1, source_target_pairs={{0,8},{2,10},{4,12},{6,14},{8,16},{10,18},{12,20},{14,22},{16,24},... | collective-permute-start | bytes 589832 | tf_op jit(solution)/shard_map/ppermute | solution.py:810
  567.5 19.6 %collective-permute-start.21 = (bf16[1,1,128,768]{3,2,1,0:T(8,128)(2,1)S(1)}, bf16[1,1,128,768]{3,2,1,0:T(8,128)(2,1)S(1)}, u32[]{:S(2)}, u32[]{:S(2)}) collective-permute-start(bf16[1,1,128,768]{3,2,1,0:T(8,128)(2,1)S(1)} %get-tuple-element.260), channel_id=1, source_target_pairs={{0,16},{2,18},{4,20},{6,22},{8,24},{10,26},{12,28},{14,30},{16,0},... | collective-permute-start | bytes 589832 | tf_op jit(solution)/shard_map/ppermute | solution.py:810
  569.5 17.6 %collective-permute-start.22 = (bf16[1,1,128,768]{3,2,1,0:T(8,128)(2,1)S(1)}, bf16[1,1,128,768]{3,2,1,0:T(8,128)(2,1)S(1)}, u32[]{:S(2)}, u32[]{:S(2)}) collective-permute-start(bf16[1,1,128,768]{3,2,1,0:T(8,128)(2,1)S(1)} %get-tuple-element.261), channel_id=1, source_target_pairs={{0,24},{2,26},{4,28},{6,30},{8,0},{10,2},{12,4},{14,6},{16,8},{18,... | collective-permute-start | bytes 589832 | tf_op jit(solution)/shard_map/ppermute | solution.py:810
  570.0 17.2 %copy-start.56 = (f32[64,4096]{1,0:T(8,128)}, f32[64,4096]{1,0:T(8,128)S(1)}, u32[]{:S(2)}) copy-start(f32[64,4096]{1,0:T(8,128)S(1)} %slice_dynamic-update-slice_fusion) | copy-start | bytes 3145732
  590.7 18.9 %collective-permute-start.24 = (bf16[1,1,128,768]{3,2,1,0:T(8,128)(2,1)S(1)}, bf16[1,1,128,768]{3,2,1,0:T(8,128)(2,1)S(1)}, u32[]{:S(2)}, u32[]{:S(2)}) collective-permute-start(bf16[1,1,128,768]{3,2,1,0:T(8,128)(2,1)S(1)} %get-tuple-element.271), channel_id=1, source_target_pairs={{0,8},{2,10},{4,12},{6,14},{8,16},{10,18},{12,20},{14,22},{16,24},... | collective-permute-start | bytes 589832 | tf_op jit(solution)/shard_map/ppermute | solution.py:810
  595.5 14.4 %collective-permute-start.25 = (bf16[1,1,128,768]{3,2,1,0:T(8,128)(2,1)S(1)}, bf16[1,1,128,768]{3,2,1,0:T(8,128)(2,1)S(1)}, u32[]{:S(2)}, u32[]{:S(2)}) collective-permute-start(bf16[1,1,128,768]{3,2,1,0:T(8,128)(2,1)S(1)} %get-tuple-element.272), channel_id=1, source_target_pairs={{0,16},{2,18},{4,20},{6,22},{8,24},{10,26},{12,28},{14,30},{16,0},... | collective-permute-start | bytes 589832 | tf_op jit(solution)/shard_map/ppermute | solution.py:810
  596.7 13.2 %collective-permute-start.26 = (bf16[1,1,128,768]{3,2,1,0:T(8,128)(2,1)S(1)}, bf16[1,1,128,768]{3,2,1,0:T(8,128)(2,1)S(1)}, u32[]{:S(2)}, u32[]{:S(2)}) collective-permute-start(bf16[1,1,128,768]{3,2,1,0:T(8,128)(2,1)S(1)} %get-tuple-element.273), channel_id=1, source_target_pairs={{0,24},{2,26},{4,28},{6,30},{8,0},{10,2},{12,4},{14,6},{16,8},{18,... | collective-permute-start | bytes 589832 | tf_op jit(solution)/shard_map/ppermute | solution.py:810
  598.1 11.4 %collective-permute-start.27 = (bf16[1,1,128,384]{3,2,1,0:T(8,128)(2,1)S(1)}, bf16[1,1,128,384]{3,2,1,0:T(8,128)(2,1)S(1)}, u32[]{:S(2)}, u32[]{:S(2)}) collective-permute-start(bf16[1,1,128,384]{3,2,1,0:T(8,128)(2,1)S(1)} %add_convert_fusion.19), channel_id=1, source_target_pairs={{0,1},{1,0},{2,3},{3,2},{4,5},{5,4},{6,7},{7,6},{8,9},{9,8},{10,11... | collective-permute-start | bytes 294920 | tf_op jit(solution)/shard_map/ppermute | solution.py:702
  599.7 17.5 %collective-permute-start.28 = (bf16[64,5248]{1,0:T(8,128)(2,1)}, bf16[64,5248]{1,0:T(8,128)(2,1)S(1)}, u32[]{:S(2)}, u32[]{:S(2)}) collective-permute-start(bf16[64,5248]{1,0:T(8,128)(2,1)} %reduce-scatter.5.cloned.1.call-done), channel_id=1, source_target_pairs={{0,1},{1,0},{2,3},{3,2},{4,5},{5,4},{6,7},{7,6},{8,9},{9,8},{10,11... | collective-permute-start | bytes 2015240 | tf_op jit(solution)/shard_map/ppermute | solution.py:702
  609.8 17.1 %copy-start.49 = (bf16[1,1,128,768]{3,2,1,0:T(8,128)(2,1)}, bf16[1,1,128,768]{3,2,1,0:T(8,128)(2,1)S(1)}, u32[]{:S(2)}) copy-start(bf16[1,1,128,768]{3,2,1,0:T(8,128)(2,1)S(1)} %collective-permute-done.26) | copy-start | bytes 589828
  619.5 7.3 %collective-permute-start.29 = (bf16[1,1,128,384]{3,2,1,0:T(8,128)(2,1)S(1)}, bf16[1,1,128,384]{3,2,1,0:T(8,128)(2,1)S(1)}, u32[]{:S(2)}, u32[]{:S(2)}) collective-permute-start(bf16[1,1,128,384]{3,2,1,0:T(8,128)(2,1)S(1)} %add_convert_fusion.17), channel_id=1, source_target_pairs={{0,1},{1,0},{2,3},{3,2},{4,5},{5,4},{6,7},{7,6},{8,9},{9,8},{10,11... | collective-permute-start | bytes 294920 | tf_op jit(solution)/shard_map/ppermute | solution.py:702
  620.7 6.1 collective-permute-start.30
  621.6 5.2 collective-permute-start.31
  621.6 5.2 collective-permute-start.32
  628.2 4.4 collective-permute-start.33
  629.1 3.4 collective-permute-start.34
  629.1 3.8 collective-permute-start.35
  (54 other events, 445.7 us)
Sparse Core Ops, SparseCore 0:
  13.0 93.0 all-gather.3
  107.6 90.2 all-gather.5
  270.2 119.7 reduce-scatter.2
  433.7 152.1 reduce-scatter.4

commit v4 on v3

--- a/solution.py
+++ b/solution.py
@@ -271,59 +271,126 @@
     )(left, ffn, bias.reshape(1, columns))
 
 
-def down_kernel(left_ref, right_ref, out_ref):
-    right = right_ref[...].reshape(-1, right_ref.shape[-1])
-    out_ref[...] = nn(left_ref[...], right)
-
-
-def down_rows(left, ffn):
-    rows, inner = left.shape
-    count, columns = ffn.shape[0], ffn.shape[2]
-    tall, wide = min(rows, 1024), 256
+def spread_rows(summed):
+    centred = summed - jnp.mean(summed, axis=1, keepdims=True)
+    scale = lax.rsqrt(jnp.mean(centred * centred, axis=1, keepdims=True) + EPSILON)
+    return centred * scale, scale
+
+
+def norm_back(unit, scale, gain, grad):
+    inner = grad * gain
+    lean = jnp.mean(inner, axis=1, keepdims=True)
+    tilt = jnp.mean(inner * unit, axis=1, keepdims=True)
+    return scale * (inner - lean - unit * tilt)
+
+
+def add_column_sums(ref, terms):
+    rows = [jnp.sum(t, axis=0, keepdims=True) for t in terms]
+    rows.append(jnp.zeros((ref.shape[0] - len(rows), ref.shape[1]), jnp.float32))
+    part = jnp.concatenate(rows, axis=0)
+
+    @pl.when(pl.program_id(0) == 0)
+    def _():
+        ref[...] = part
+
+    @pl.when(pl.program_id(0) > 0)
+    def _():
+        ref[...] += part
+
+
+def row_tiles(kernel, name, tiled, fixed, outs, sums=False):
+    rows = tiled[0].shape[0]
+    tall = min(rows, 256)
+    in_specs = [pl.BlockSpec((tall, a.shape[1]), lambda i: (i, 0)) for a in tiled]
+    for _, block, index in fixed:
+        in_specs.append(
+            pl.BlockSpec(block, lambda i, at=index: at, pipeline_mode=pl.Buffered(1))
+        )
+    out_specs = [pl.BlockSpec((tall, D), lambda i: (i, 0)) for _ in outs]
+    out_shape = [jax.ShapeDtypeStruct((rows, D), kind) for kind in outs]
+    if sums:
+        out_specs.append(pl.BlockSpec((8, D), lambda i: (0, 0)))
+        out_shape.append(jax.ShapeDtypeStruct((8, D), jnp.float32))
     return pl.pallas_call(
-        down_kernel,
-        grid=(rows // tall, columns // wide),
-        in_specs=[
-            pl.BlockSpec((tall, inner), lambda i, j: (i, 0)),
-            pl.BlockSpec((count, inner // count, wide), lambda i, j: (0, 1, j)),
-        ],
-        out_specs=pl.BlockSpec((tall, wide), lambda i, j: (i, j)),
-        out_shape=jax.ShapeDtypeStruct((rows, columns), jnp.float32),
-        compiler_params=pltpu.CompilerParams(vmem_limit_bytes=48 * 2**20),
+        kernel,
+        grid=(rows // tall,),
+        in_specs=in_specs,
+        out_specs=out_specs,
+        out_shape=out_shape,
+        compiler_params=pltpu.CompilerParams(vmem_limit_bytes=56 * 2**20),
         cost_estimate=SHORT,
-        name="down_rows",
-    )(left, ffn)
-
-
-def up_back_kernel(left_ref, right_ref, out_ref):
-    wide = right_ref.shape[2]
-    tall_shard = out_ref.shape[1] // right_ref.shape[0]
-    total = None
-    for n in range(right_ref.shape[1] // tall_shard):
-        right = right_ref[:, n * tall_shard : (n + 1) * tall_shard].reshape(-1, wide)
-        part = nt(left_ref[:, n * wide : (n + 1) * wide], right)
-        total = part if total is None else total + part
-    out_ref[...] = total
-
-
-def up_back_rows(left, ffn):
-    rows, inner = left.shape
-    count, wide = ffn.shape[0], ffn.shape[2]
-    tall_shard = D // count
-    tall, group = min(rows, 1024), 4
-    return pl.pallas_call(
-        up_back_kernel,
-        grid=(rows // tall, count // group),
-        in_specs=[
-            pl.BlockSpec((tall, inner), lambda i, j: (i, 0)),
-            pl.BlockSpec((group, inner // wide * tall_shard, wide), lambda i, j: (j, 0, 0)),
-        ],
-        out_specs=pl.BlockSpec((tall, group * tall_shard), lambda i, j: (i, j)),
-        out_shape=jax.ShapeDtypeStruct((rows, count * tall_shard), jnp.float32),
-        compiler_params=pltpu.CompilerParams(vmem_limit_bytes=48 * 2**20),
-        cost_estimate=SHORT,
-        name="up_back_rows",
-    )(left, ffn)
+        name=name,
+    )(*tiled, *[array for array, _, _ in fixed])
+
+
+def column_block(attn_full, block):
+    return (attn_full, (D, D), (0, block))
+
+
+def small_block(norms):
+    return (norms, norms.shape, (0, 0))
+
+
+def first_norm_kernel(mixed, x, out_w, cross_w, norms, sum_ref, normed_ref, low_ref, query_ref):
+    summed = ALPHA * x[...].astype(jnp.float32) + nn(mixed[...], out_w[...])
+    sum_ref[...] = summed
+    normed = spread_rows(summed)[0] * norms[0:1, :] + norms[3:4, :]
+    normed_ref[...] = normed
+    low = normed.astype(jnp.bfloat16)
+    low_ref[...] = low
+    query_ref[...] = nn(low, cross_w[...]).astype(jnp.bfloat16)
+
+
+def second_norm_kernel(mixed, first, out_w, norms, sum_ref, normed_ref, low_ref):
+    summed = ALPHA * first[...] + nn(mixed[...], out_w[...])
+    sum_ref[...] = summed
+    normed = spread_rows(summed)[0] * norms[1:2, :] + norms[4:5, :]
+    normed_ref[...] = normed
+    low_ref[...] = normed.astype(jnp.bfloat16)
+
+
+def third_norm_kernel(hidden, second, cot, down, norms, out_ref, grad_ref, low_ref, sums_ref):
+    right = down[...].reshape(-1, down.shape[-1])
+    summed = ALPHA * second[...] + nn(hidden[...], right) + norms[6:7, :]
+    unit, scale = spread_rows(summed)
+    out_ref[...] = (unit * norms[2:3, :] + norms[5:6, :]).astype(jnp.bfloat16)
+    cotangent = cot[...].astype(jnp.float32)
+    grad = norm_back(unit, scale, norms[2:3, :], cotangent)
+    grad_ref[...] = grad
+    low = grad.astype(jnp.bfloat16)
+    low_ref[...] = low
+    add_column_sums(sums_ref, [cotangent * unit, cotangent, low.astype(jnp.float32)])
+
+
+def second_back_kernel(
+    d_pre, d_third, summed, up, out_w, norms, grad_ref, low_ref, back_ref, sums_ref
+):
+    wide = up.shape[2]
+    tall_shard = D // up.shape[0]
+    grad = ALPHA * d_third[...]
+    for n in range(up.shape[1] // tall_shard):
+        right = up[:, n * tall_shard : (n + 1) * tall_shard].reshape(-1, wide)
+        grad += nt(d_pre[:, n * wide : (n + 1) * wide], right)
+    unit, scale = spread_rows(summed[...])
+    d_sum = norm_back(unit, scale, norms[1:2, :], grad)
+    grad_ref[...] = d_sum
+    low = d_sum.astype(jnp.bfloat16)
+    low_ref[...] = low
+    back_ref[...] = nt(low, out_w[...]).astype(jnp.bfloat16)
+    add_column_sums(sums_ref, [grad * unit, grad])
+
+
+def first_back_kernel(
+    d_query, d_second, summed, cross_w, out_w, norms, grad_ref, low_ref, back_ref, sums_ref
+):
+    grad = ALPHA * d_second[...] + nt(d_query[...], cross_w[...])
+    unit, scale = spread_rows(summed[...])
+    d_sum = norm_back(unit, scale, norms[0:1, :], grad)
+    grad_ref[...] = d_sum
+    low = d_sum.astype(jnp.bfloat16)
+    low_ref[...] = low
+    back_ref[...] = nt(low, out_w[...]).astype(jnp.bfloat16)
+    add_column_sums(sums_ref, [grad * unit, grad])
 
 
 def gelu_back_kernel(left_ref, right_ref, slope_ref, out_ref, sum_ref):
@@ -1250,11 +1317,13 @@
     for wide in [D] * 8 + [c.shape[1] for c in columns[5:8]]:
         fulls.append(attn_full[:, at : at + wide])
         at += wide
-    qkv_full, (out_full, cross_q_full, mk_full, mv_full, cross_out_full) = fulls[:3], fulls[3:8]
-    gain_full = fulls[8].T.astype(jnp.float32)
-    shift_full = fulls[9].T.astype(jnp.float32)
+    qkv_full, (mk_full, mv_full) = fulls[:3], fulls[5:7]
+    out_block, cross_q_block, cross_out_block = (column_block(attn_full, n) for n in (3, 4, 7))
+    norms = jnp.concatenate([fulls[8].T, fulls[9].T, jnp.zeros((1, D), low)], axis=0)
+    norms = norms.astype(jnp.float32)
     bias_full = fulls[10].reshape(-1).astype(jnp.float32)
     up_parts = [w_up[:, n : n + D] for n in range(0, w_up.shape[1], D)]
+    down_rows = w_down.shape[0]
     ffn_shard = jnp.concatenate(up_parts + [w_down, jnp.zeros((8, D), low)], axis=0)
     ffn_full = lax.all_gather(ffn_shard, "batch", axis=0)
     x_rows = Flight(rows_in_steps(inputs))
@@ -1265,11 +1334,12 @@
     cot_rows = Flight(rows_in_steps(cotangent))
     x_rows = x_rows.finish()
     rows, length = x_rows.shape[:2]
-    x_flat = x_rows.reshape(-1, D)
+    x_flat = lax.optimization_barrier(x_rows.reshape(-1, D))
     ids = ids.finish()
     target_flat = ids[:, :, 0].reshape(-1)
     memory_id_flat = ids[:, :, 1].reshape(-1)
-    memory_flat = memory_rows.finish().reshape(-1, D)
+    memory_flat = lax.optimization_barrier(memory_rows.finish().reshape(-1, D))
+    full = jnp.float32
 
     def self_forward(q, k, v, id_row, pairs):
         fq, fk = document_features(id_row, id_row)
@@ -1279,10 +1349,13 @@
     mixed_flat, self_lse = each_row(
         functools.partial(self_forward, pairs=(0, 2 * half)), rows, (*qkv, target_flat)
     )
-    first_sum = ALPHA * x_flat.astype(jnp.float32) + dot32(mixed_flat, out_full)
-    first = layer_norm(first_sum, gain_full[0], shift_full[0])
-    first_low = first.astype(low)
-    cross_queries = dot32(first_low, cross_q_full).astype(low)
+    first_sum, first, first_low, cross_queries = row_tiles(
+        first_norm_kernel,
+        "first_norm",
+        [mixed_flat, x_flat],
+        [out_block, cross_q_block, small_block(norms)],
+        [full, full, low, low],
+    )
     cross_queries = tick(cross_queries, cot_rows)
     memory_keys = dot32(memory_flat, mk_full).astype(low)
     memory_values = dot32(memory_flat, mv_full).astype(low)
@@ -1294,28 +1367,40 @@
     arrays = (cross_queries, memory_keys, memory_values, target_flat, memory_id_flat)
     mixed = each_row(functools.partial(cross_forward, pairs=(0, 2 * half)), rows, arrays)
     cross_flat, cross_lse = tick(mixed, cot_rows)
-    second_sum = ALPHA * first + dot32(cross_flat, cross_out_full)
-    second = layer_norm(second_sum, gain_full[1], shift_full[1])
-    second_low = second.astype(low)
+    second_sum, second, second_low = row_tiles(
+        second_norm_kernel,
+        "second_norm",
+        [cross_flat, first],
+        [cross_out_block, small_block(norms)],
+        [full, full, low],
+    )
     hidden_low, slope = gelu_rows(second_low, ffn_full, bias_full)
     cot_flat = cot_rows.finish().reshape(-1, D)
-    third_sum = ALPHA * second + down_rows(hidden_low, ffn_full) + shift_full[3]
-    result, third_back = jax.vjp(layer_norm, third_sum, gain_full[2], shift_full[2])
-
-    d_third, d_gain_three, d_shift_three = third_back(cot_flat.astype(jnp.float32))
-    d_branch_three = d_third.astype(low)
+    ffn_block = (ffn_full.shape[0], down_rows, D)
+    result, d_third, d_branch_three, third_sums = row_tiles(
+        third_norm_kernel,
+        "third_norm",
+        [hidden_low, second, cot_flat],
+        [(ffn_full, ffn_block, (0, 1, 0)), small_block(norms)],
+        [low, full, low],
+        True,
+    )
+
     output = Flight(rows_out_steps(result.reshape(rows, length, D), low))
     down_grad = Flight(whole_reduce([(hidden_low, [d_branch_three])]))
     d_branch_three, d_third = tick((d_branch_three, d_third), output, down_grad)
-    grad_bias_down = jnp.sum(d_branch_three.astype(jnp.float32), axis=0)
     d_pre, grad_bias_up = gelu_back_rows(d_branch_three, ffn_full, slope)
     up_grad = start_reduce([(second_low, [d_pre])], "xyz")
     d_pre = tick(d_pre, up_grad)
-    d_second = ALPHA * d_third + up_back_rows(d_pre, ffn_full)
-    second_back = jax.vjp(layer_norm, second_sum, gain_full[1], shift_full[1])[1]
-    d_second_sum, d_gain_two, d_shift_two = second_back(d_second)
-    d_branch_two = tick(d_second_sum.astype(low), up_grad)
-    d_cross = back_prod(d_branch_two, cross_out_full).astype(low)
+    d_second_sum, d_branch_two, d_cross, second_sums = row_tiles(
+        second_back_kernel,
+        "second_back",
+        [d_pre, d_third, second_sum],
+        [(ffn_full, ffn_block, (0, 0, 0)), cross_out_block, small_block(norms)],
+        [full, low, low],
+        True,
+    )
+    d_branch_two, d_cross = tick((d_branch_two, d_cross), up_grad)
 
     def cross_backward(id_row, memory_id_row, *arrays, pairs):
         fq, fk = document_features(id_row, memory_id_row)
@@ -1325,12 +1410,16 @@
     arrays += (cross_flat, cross_lse, d_cross)
     grads = each_row(functools.partial(cross_backward, pairs=(0, 2 * half)), rows, arrays)
     d_cross_low, d_memory_keys, d_memory_values = tick(grads, output, up_grad)
-    d_first = ALPHA * d_second_sum + back_prod(d_cross_low, cross_q_full)
-    first_back = jax.vjp(layer_norm, first_sum, gain_full[0], shift_full[0])[1]
-    d_first_sum, d_gain_one, d_shift_one = first_back(d_first)
-    d_branch_one = d_first_sum.astype(low)
-    grad_rows = [d_gain_one, d_gain_two, d_gain_three]
-    grad_rows += [d_shift_one, d_shift_two, d_shift_three, grad_bias_down]
+    d_first_sum, d_branch_one, d_self, first_sums = row_tiles(
+        first_back_kernel,
+        "first_back",
+        [d_cross_low, d_second_sum, first_sum],
+        [cross_q_block, out_block, small_block(norms)],
+        [full, low, low],
+        True,
+    )
+    every = [first_sums[0], second_sums[0], third_sums[0]]
+    grad_rows = every + [first_sums[1], second_sums[1], third_sums[1], third_sums[2]]
     cross_grad = Flight(
         whole_reduce(
             [
@@ -1342,8 +1431,7 @@
             (jnp.stack(grad_rows), grad_bias_up),
         )
     )
-    d_branch_one = tick(d_branch_one, cross_grad, up_grad)
-    d_self = back_prod(d_branch_one, out_full).astype(low)
+    d_self = tick(d_self, cross_grad, up_grad)
     d_memory = back_prod(d_memory_keys, mk_full) + back_prod(d_memory_values, mv_full)
     d_self, d_memory = lax.optimization_barrier((d_self, d_memory))
     d_memory = Flight(rows_out_steps(d_memory.reshape(rows, length, D), jnp.float32))

time: 649 us -> 636 us (0.980)
  Pallas kernels: 239 us -> 284 us
  matrix products: 95.4 us -> 62.5 us
  other arithmetic: 79.8 us -> 48.1 us
  waiting for transfers between devices: 117 us -> 135 us
  starting transfers between devices: 51.1 us -> 42.7 us
    pallas_call x2 -> x5, Pallas kernels: 28 us -> 72.4 us  [row_tiles(): pl.pallas_call(kernel, grid=(rows // tall,), in_specs=in_specs, out_specs...]
    ppermute x15, waiting for transfers between devices: 34.7 us -> 57.1 us  [swap_pair(): return lax.ppermute(array, 'blk', [(0, 1), (1, 0)])]
    dot_general x8 -> x5, matrix products: 43.5 us -> 21.3 us  [back_prod(): jnp.einsum('tn,kn->tk', grad_rows, matrix, preferred_element_type=jnp.flo...]
    reduce_sum x12 -> x0, other arithmetic: 19.7 us -> none  [the longest x3 8.9 us: layer_norm(): centred = summed - average]
    all_gather x1, waiting for transfers between devices: 51.4 us -> 33.3 us  [gathered(): return lax.all_gather(shard, 'batch', axis=axis, tiled=True)]
    dot_general x8 -> x5, matrix products: 40.6 us -> 26.2 us  [dot32(): return jnp.dot(left, right, preferred_element_type=jnp.float32)]
    ppermute x3, waiting for transfers between devices: 7.37 us -> 19.6 us  [to_x(): return lax.ppermute(array, 'batch', [(n, n ^ 2) for n in range(16)])]
    convert_element_type x6 -> x1, other arithmetic: 9.79 us -> 0.7 us  [whole_row_device(): norms = norms.astype(jnp.float32)]
  transfers between devices with their start and end apart: 40 -> 40, of which waited for: 13 -> 14; matrix products, arithmetic and copies ran while one was open for 26% -> 17% of each run, Pallas kernels for 32% -> 39%
where the time goes in v4:
time: 636 us; the launch traced here: 629 us
  Pallas kernels  284 us (45%)
  waiting for transfers between devices  135 us (21%)
  matrix products  62.5 us (10%)
  other arithmetic  48.1 us (8%)
  starting transfers between devices  42.7 us (7%)
  local copies, waits for them, and re-layouts  40.7 us (6%)
  between operations  15.2 us (2%)
    pallas_call x5, Pallas kernels, attention_call(): pl.pallas_call(functools.partial(kernel, causal), grid=(count,), in_specs...  130 us
    pallas_call x5, Pallas kernels, row_tiles(): pl.pallas_call(kernel, grid=(rows // tall,), in_specs=in_specs, out_specs...  72.4 us
    ppermute x15, waiting for transfers between devices, swap_pair(): return lax.ppermute(array, 'blk', [(0, 1), (1, 0)])  57.1 us
    pallas_call x4, Pallas kernels, joined_grads(): pl.pallas_call(functools.partial(grads_kernel, plan, halved), in_specs=[a...  43.6 us
    all_gather x1, waiting for transfers between devices, gathered(): return lax.all_gather(shard, 'batch', axis=axis, tiled=True)  33.3 us
    dot_general x5, matrix products, dot32(): return jnp.dot(left, right, preferred_element_type=jnp.float32)  26.2 us
    ppermute x9, waiting for transfers between devices, to_z(): lax.ppermute(array, 'batch', [(n, (n + 4 * step) % 16) for n in range(16)])  24 us
    unnamed x147, local copies, waits for them, and re-layouts  23.6 us
  transfers between devices with their start and end apart: 40, of which 14 were waited for; matrix products, arithmetic and copies ran while one was open for 17% of the time, Pallas kernels for 39%

profile of v4, /device:TPU:0, one launch (start us, length us, event | category | flops | bytes accessed | tf_op | source)
XLA Modules:
  0.0 628.8 jit_solution(7547426110534693379)
XLA Ops:
  9.6 3.1 concatenate.68
  19.8 3.0 collective-permute-start
  23.9 22.3 %collective-permute-done.1 = s32[1,512,2]{1,0,2:T(1,128)S(1)} collective-permute-done((s32[1,512,2]{1,0,2:T(1,128)S(1)}, s32[1,512,2]{1,0,2:T(1,128)S(1)}, u32[]{:S(2)}, u32[]{:S(2)}) %collective-permute-start.1) | collective-permute-done | bytes 4128 | tf_op jit(solution)/shard_map/ppermute | solution.py:769
  52.1 18.8 %collective-permute-done.2 = bf16[1,512,1024]{2,1,0:T(8,128)(2,1)S(1)} collective-permute-done((bf16[1,512,1024]{2,1,0:T(8,128)(2,1)}, bf16[1,512,1024]{2,1,0:T(8,128)(2,1)S(1)}, u32[]{:S(2)}, u32[]{:S(2)}) %collective-permute-start.2) | collective-permute-done | bytes 1048608 | tf_op jit(solution)/shard_map/ppermute | solution.py:769
  72.5 33.3 %all-gather.4.cloned.1.call-done.out_w.cross_w = bf16[1024,8320]{1,0:T(8,128)(2,1)} async-done(((bf16[64,8320]{1,0:T(8,128)(2,1)}), bf16[1024,8320]{1,0:T(8,128)(2,1)}) %all-gather.4.cloned.1.call-update) | async-done | bytes 17039376 | tf_op jit(solution)/shard_map/all_gather | solution.py:810
  105.8 5.4 convolution_convert_fusion.3.v_ref
  111.3 6.1 convolution_convert_fusion.4.k_ref
  117.3 3.9 convolution_convert_fusion.5.q_ref
  121.3 20.3 %attention_forward.2 = (bf16[1024,1024]{1,0:T(8,128)(2,1)S(1)}, f32[1024,1024]{1,0:T(8,128)}) custom-call(bf16[1024,1024]{1,0:T(8,128)(2,1)S(1)} %convolution_convert_fusion.5.q_ref, bf16[1024,1024]{1,0:T(8,128)(2,1)} %convolution_convert_fusion.4.k_ref, bf16[1024,1024]{1,0:T(8,128)(2,1)} %convolution_convert_fusion.3.v_ref, ...), custom_call_target="tpu_custom_call" | custom-call | flops 1024 | bytes 1024 | tf_op jit(solution)/shard_map/attention_forward/pallas_call | solution.py:187
  145.2 10.3 %first_norm.1 = (f32[1024,1024]{1,0:T(8,128)}, f32[1024,1024]{1,0:T(8,128)}, bf16[1024,1024]{1,0:T(8,128)(2,1)}, bf16[1024,1024]{1,0:T(8,128)(2,1)}) custom-call(bf16[1024,1024]{1,0:T(8,128)(2,1)} %copy-done, bf16[1024,1024]{1,0:T(8,128)(2,1)} %copy-done.18, bf16[1024,8320]{1,0:T(8,128)(2,1)} %all-gather.4.cloned.1.call-done.out_w.cross_w, ...), custom_call_target="tpu_custom_call" | custom-call | flops 1024 | bytes 1024 | tf_op jit(solution)/shard_map/first_norm/pallas_call | solution.py:314
  157.0 5.3 convolution_convert_fusion.1.v_ref
  162.2 5.5 convolution_convert_fusion.2.k_ref
  167.8 25.1 %attention_forward.3 = (bf16[1024,1024]{1,0:T(8,128)(2,1)S(1)}, f32[1024,1024]{1,0:T(8,128)}) custom-call(bf16[1024,1024]{1,0:T(8,128)(2,1)S(1)} %copy-done.6, bf16[1024,1024]{1,0:T(8,128)(2,1)} %convolution_convert_fusion.2.k_ref, bf16[1024,1024]{1,0:T(8,128)(2,1)} %convolution_convert_fusion.1.v_ref, bf16[1024,128]{1,0:T(8,128)(2,1)S(1)} %compare_convert_fusion.fq_ref, ...), custom_call_target="tpu_custom_call" | custom-call | flops 1024 | bytes 1024 | tf_op jit(solution)/shard_map/attention_forward/pallas_call | solution.py:187
  195.2 9.2 %second_norm.1 = (f32[1024,1024]{1,0:T(8,128)}, f32[1024,1024]{1,0:T(8,128)}, bf16[1024,1024]{1,0:T(8,128)(2,1)}) custom-call(bf16[1024,1024]{1,0:T(8,128)(2,1)} %copy-done.1, f32[1024,1024]{1,0:T(8,128)} %get-tuple-element.194.first, bf16[1024,8320]{1,0:T(8,128)(2,1)} %all-gather.4.cloned.1.call-done.out_w.cross_w, f32[8,1024]{1,0:T(8,128)} %maximum_convert_fusion.norms), custom_call_target="tpu_custom_call" | custom-call | flops 1024 | bytes 1024 | tf_op jit(solution)/shard_map/second_norm/pallas_call | solution.py:314
  207.2 20.7 %gelu_rows.1 = (bf16[1024,4096]{1,0:T(8,128)(2,1)}, f32[1024,4096]{1,0:T(8,128)}) custom-call(bf16[1024,1024]{1,0:T(8,128)(2,1)} %get-tuple-element.195.left_ref.refs_0_, bf16[16,520,1024]{2,1,0:T(8,128)(2,1)} %bitcast.65, f32[1,4096]{1,0:T(1,128)} %reshape.166.bias_ref), custom_call_target="tpu_custom_call" | custom-call | flops 1024 | bytes 1024 | tf_op jit(solution)/shard_map/gelu_rows/pallas_call | solution.py:255
  228.0 19.0 %third_norm.1 = (bf16[1024,1024]{1,0:T(8,128)(2,1)}, f32[1024,1024]{1,0:T(8,128)}, bf16[1024,1024]{1,0:T(8,128)(2,1)}, f32[8,1024]{1,0:T(8,128)}) custom-call(bf16[1024,4096]{1,0:T(8,128)(2,1)} %get-tuple-element.196.hidden, f32[1024,1024]{1,0:T(8,128)} %get-tuple-element.197.second, bf16[1024,1024]{1,0:T(8,128)(2,1)} %maximum_bitcast_fusion.2.cot, ...), custom_call_target="tpu_custom_call" | custom-call | flops 1024 | bytes 1024 | tf_op jit(solution)/shard_map/third_norm/pallas_call | solution.py:314
  247.0 15.0 %convolution_convert_fusion = bf16[4096,1024]{1,0:T(8,128)(2,1)} fusion(bf16[1024,4096]{1,0:T(8,128)(2,1)} %get-tuple-element.196.hidden, bf16[1024,1024]{1,0:T(8,128)(2,1)} %get-tuple-element.205.left_ref), kind=kOutput, calls=%fused_computation | convolution fusion | flops 8594128896 | bytes 18874368 | tf_op jit(solution)/shard_map/tk,tn->kn/dot_general | solution.py:461
  265.9 17.4 %gelu_back_rows.1 = (bf16[1024,4096]{1,0:T(8,128)(2,1)}, f32[1,1,4096]{2,1,0:T(1,128)S(1)}) custom-call(bf16[1024,1024]{1,0:T(8,128)(2,1)S(1)} %copy-done.12, bf16[16,520,1024]{2,1,0:T(8,128)(2,1)} %bitcast.67, f32[1024,4096]{1,0:T(8,128)} %get-tuple-element.206.slope_ref), custom_call_target="tpu_custom_call" | custom-call | flops 1024 | bytes 1024 | tf_op jit(solution)/shard_map/gelu_back_rows/pallas_call | solution.py:415
  283.3 12.8 %joined_grads.4 = (bf16[1024,2048]{1,0:T(8,128)(2,1)}, bf16[1024,2048]{1,0:T(8,128)(2,1)}) custom-call(bf16[1024,1024]{1,0:T(8,128)(2,1)S(1)} %copy-done.5, bf16[1024,4096]{1,0:T(8,128)(2,1)} %get-tuple-element.209.refs_1_.d_pre), custom_call_target="tpu_custom_call" | custom-call | flops 1024 | bytes 1024 | tf_op jit(solution)/shard_map/joined_grads/pallas_call | solution.py:1086
  296.3 21.0 %second_back.1 = (f32[1024,1024]{1,0:T(8,128)}, bf16[1024,1024]{1,0:T(8,128)(2,1)}, bf16[1024,1024]{1,0:T(8,128)(2,1)}, f32[8,1024]{1,0:T(8,128)}) custom-call(bf16[1024,4096]{1,0:T(8,128)(2,1)} %get-tuple-element.209.refs_1_.d_pre, f32[1024,1024]{1,0:T(8,128)} %get-tuple-element.210.d_third, f32[1024,1024]{1,0:T(8,128)} %get-tuple-element.211.summed, ...), custom_call_target="tpu_custom_call" | custom-call | flops 1024 | bytes 1024 | tf_op jit(solution)/shard_map/second_back/pallas_call | solution.py:314
  317.4 3.9 add_convert_fusion
  323.2 48.4 %attention_backward.3 = (bf16[1024,1024]{1,0:T(8,128)(2,1)S(1)}, bf16[1024,1024]{1,0:T(8,128)(2,1)S(1)}, bf16[1024,1024]{1,0:T(8,128)(2,1)}) custom-call(bf16[1024,1024]{1,0:T(8,128)(2,1)} %get-tuple-element.186.q_ref, bf16[1024,1024]{1,0:T(8,128)(2,1)} %convolution_convert_fusion.2.k_ref, bf16[1024,1024]{1,0:T(8,128)(2,1)} %convolution_convert_fusion.1.v_ref, ...), custom_call_target="tpu_custom_call" | custom-call | flops 1024 | bytes 1024 | tf_op jit(solution)/shard_map/attention_backward/pallas_call | solution.py:187
  371.7 14.7 %collective-permute-done.6 = bf16[4,1,128,2048]{3,2,1,0:T(8,128)(2,1)} collective-permute-done((bf16[4,1,128,2048]{3,2,1,0:T(8,128)(2,1)}, bf16[4,1,128,2048]{3,2,1,0:T(8,128)(2,1)}, u32[]{:S(2)}, u32[]{:S(2)}) %collective-permute-start.6) | collective-permute-done | bytes 2097184 | tf_op jit(solution)/shard_map/ppermute | solution.py:873
  386.4 3.1 add_convert_fusion.1
  391.4 12.9 %first_back.1 = (f32[1024,1024]{1,0:T(8,128)}, bf16[1024,1024]{1,0:T(8,128)(2,1)}, bf16[1024,1024]{1,0:T(8,128)(2,1)}, f32[8,1024]{1,0:T(8,128)}) custom-call(bf16[1024,1024]{1,0:T(8,128)(2,1)} %copy-done.2, f32[1024,1024]{1,0:T(8,128)} %get-tuple-element.231.d_second, f32[1024,1024]{1,0:T(8,128)} %get-tuple-element.232.summed, ...), custom_call_target="tpu_custom_call" | custom-call | flops 1024 | bytes 1024 | tf_op jit(solution)/shard_map/first_back/pallas_call | solution.py:314
  410.4 16.3 %joined_grads.5 = bf16[1024,5248]{1,0:T(8,128)(2,1)} custom-call(bf16[1024,1024]{1,0:T(8,128)(2,1)S(1)} %copy-done.4, bf16[1024,1024]{1,0:T(8,128)(2,1)S(1)} %copy-done.10, bf16[1024,1024]{1,0:T(8,128)(2,1)} %copy-done.1, bf16[1024,1024]{1,0:T(8,128)(2,1)} %copy-done, bf16[1024,1024]{1,0:T(8,128)(2,1)} %copy-done.11, ...), custom_call_target="tpu_custom_call" | custom-call | flops 1024 | bytes 1024 | tf_op jit(solution)/shard_map/joined_grads/pallas_call | solution.py:1086
  426.7 4.1 add_convert_fusion.5
  430.8 4.7 fusion.14
  435.5 4.2 convolution_add_fusion
  446.6 2.3 collective-permute-start.9
  451.7 18.0 %attention_backward.4 = (bf16[1024,512]{1,0:T(8,128)(2,1)S(1)}, bf16[1024,512]{1,0:T(8,128)(2,1)S(1)}, bf16[1024,512]{1,0:T(8,128)(2,1)S(1)}) custom-call(bf16[1024,1024]{1,0:T(8,128)(2,1)S(1)} %convolution_convert_fusion.5.q_ref, bf16[1024,1024]{1,0:T(8,128)(2,1)} %convolution_convert_fusion.4.k_ref, bf16[1024,1024]{1,0:T(8,128)(2,1)} %convolution_convert_fusion.3.v_ref, ...), custom_call_target="tpu_custom_call" | custom-call | flops 1024 | bytes 1024 | tf_op jit(solution)/shard_map/attention_backward/pallas_call | solution.py:187
  469.7 9.0 %collective-permute-done.11 = bf16[256,1024]{1,0:T(8,128)(2,1)} collective-permute-done((bf16[256,1024]{1,0:T(8,128)(2,1)}, bf16[256,1024]{1,0:T(8,128)(2,1)}, u32[]{:S(2)}, u32[]{:S(2)}) %collective-permute-start.11) | collective-permute-done | bytes 524320 | tf_op jit(solution)/shard_map/ppermute | solution.py:769
  481.4 6.6 %joined_grads.6 = (bf16[1024,768]{1,0:T(8,128)(2,1)}, bf16[1024,768]{1,0:T(8,128)(2,1)}) custom-call(bf16[1024,1024]{1,0:T(8,128)(2,1)} %copy-done.18, bf16[1024,512]{1,0:T(8,128)(2,1)S(1)} %get-tuple-element.268.refs_1_, bf16[1024,512]{1,0:T(8,128)(2,1)S(1)} %get-tuple-element.271.refs_2_, bf16[1024,512]{1,0:T(8,128)(2,1)S(1)} %get-tuple-element.272.refs_3_), custom_call_target="tpu_custom_call" | custom-call | flops 1024 | bytes 1024 | tf_op jit(solution)/shard_map/joined_grads/pallas_call | solution.py:1086
  493.5 18.4 %attention_backward.5 = (bf16[1024,512]{1,0:T(8,128)(2,1)S(1)}, bf16[1024,512]{1,0:T(8,128)(2,1)S(1)}, bf16[1024,512]{1,0:T(8,128)(2,1)S(1)}) custom-call(bf16[1024,1024]{1,0:T(8,128)(2,1)S(1)} %convolution_convert_fusion.5.q_ref, bf16[1024,1024]{1,0:T(8,128)(2,1)} %convolution_convert_fusion.4.k_ref, bf16[1024,1024]{1,0:T(8,128)(2,1)} %convolution_convert_fusion.3.v_ref, ...), custom_call_target="tpu_custom_call" | custom-call | flops 1024 | bytes 1024 | tf_op jit(solution)/shard_map/attention_backward/pallas_call | solution.py:187
  512.0 2.4 add_convert_fusion.3
  515.5 4.0 fusion
  519.5 4.1 fusion.4
  523.7 4.3 add_add_fusion
  528.2 7.9 %joined_grads.7 = (bf16[1024,768]{1,0:T(8,128)(2,1)S(1)}, bf16[1024,768]{1,0:T(8,128)(2,1)}) custom-call(bf16[1024,1024]{1,0:T(8,128)(2,1)} %copy-done.18, bf16[1024,512]{1,0:T(8,128)(2,1)S(1)} %get-tuple-element.287, bf16[1024,512]{1,0:T(8,128)(2,1)S(1)} %get-tuple-element.288, bf16[1024,512]{1,0:T(8,128)(2,1)S(1)} %get-tuple-element.289), custom_call_target="tpu_custom_call" | custom-call | flops 1024 | bytes 1024 | tf_op jit(solution)/shard_map/joined_grads/pallas_call | solution.py:1086
  536.1 4.9 collective-permute-done.17
  548.8 5.2 collective-permute-start.21
  554.1 9.4 %collective-permute-done.20 = bf16[1,1,128,768]{3,2,1,0:T(8,128)(2,1)S(1)} collective-permute-done((bf16[1,1,128,768]{3,2,1,0:T(8,128)(2,1)S(1)}, bf16[1,1,128,768]{3,2,1,0:T(8,128)(2,1)S(1)}, u32[]{:S(2)}, u32[]{:S(2)}) %collective-permute-start.20) | collective-permute-done | bytes 196640 | tf_op jit(solution)/shard_map/ppermute | solution.py:877
  563.5 12.8 %collective-permute-done.21 = bf16[1,1,128,768]{3,2,1,0:T(8,128)(2,1)S(1)} collective-permute-done((bf16[1,1,128,768]{3,2,1,0:T(8,128)(2,1)S(1)}, bf16[1,1,128,768]{3,2,1,0:T(8,128)(2,1)S(1)}, u32[]{:S(2)}, u32[]{:S(2)}) %collective-permute-start.21) | collective-permute-done | bytes 196640 | tf_op jit(solution)/shard_map/ppermute | solution.py:877
  582.2 4.4 collective-permute-start.24
  589.6 4.1 convert_select_fusion.1
  593.8 2.6 pad_maximum_fusion.1
  596.4 2.6 pad_maximum_fusion
  600.8 4.5 collective-permute-done.28
  (288 shorter events, 96.4 us)
Async XLA Ops:
  7.2 98.7 %all-gather.4.cloned.1.call-start = ((), (), s32[]{:S(2)}) async-start(), calls=%async_computation.2 | async-start | bytes 18104320 | tf_op jit(solution)/shard_map/all_gather | solution.py:810
  12.7 194.6 %all-gather.6.cloned.1.call-start = ((), (), s32[]{:S(2)}) async-start(), calls=%async_computation.5 | async-start | bytes 18104320 | tf_op jit(solution)/shard_map/all_gather | solution.py:1328
  18.6 424.2 %reduce-scatter.3.cloned.1.call-start = ((), (), s32[]{:S(2)}) async-start(), calls=%async_computation.3 | async-start | bytes 8912896 | tf_op jit(solution)/shard_map/reduce_scatter | solution.py:1145
  19.8 26.4 %collective-permute-start = (bf16[1,512,1024]{2,1,0:T(8,128)(2,1)}, bf16[1,512,1024]{2,1,0:T(8,128)(2,1)S(1)}, u32[]{:S(2)}, u32[]{:S(2)}) collective-permute-start(bf16[1,512,1024]{2,1,0:T(8,128)(2,1)} %constant_dynamic-slice_fusion.6), channel_id=1, source_target_pairs={{0,1},{1,0},{2,3},{3,2},{4,5},{5,4},{6,7},{7,6},{8,9},{9,8},{10,11... | collective-permute-start | bytes 3145736 | tf_op jit(solution)/shard_map/ppermute | solution.py:769
  22.8 23.5 %collective-permute-start.1 = (s32[1,512,2]{1,0,2:T(1,128)S(1)}, s32[1,512,2]{1,0,2:T(1,128)S(1)}, u32[]{:S(2)}, u32[]{:S(2)}) collective-permute-start(s32[1,512,2]{1,0,2:T(1,128)S(1)} %fusion.33), channel_id=1, source_target_pairs={{0,1},{1,0},{2,3},{3,2},{4,5},{5,4},{6,7},{7,6},{8,9},{9,8},{10,11... | collective-permute-start | bytes 12296 | tf_op jit(solution)/shard_map/ppermute | solution.py:769
  46.2 24.7 %collective-permute-start.2 = (bf16[1,512,1024]{2,1,0:T(8,128)(2,1)}, bf16[1,512,1024]{2,1,0:T(8,128)(2,1)S(1)}, u32[]{:S(2)}, u32[]{:S(2)}) collective-permute-start(bf16[1,512,1024]{2,1,0:T(8,128)(2,1)} %constant_dynamic-slice_fusion.3), channel_id=1, source_target_pairs={{0,1},{1,0},{2,3},{3,2},{4,5},{5,4},{6,7},{7,6},{8,9},{9,8},{10,11... | collective-permute-start | bytes 3145736 | tf_op jit(solution)/shard_map/ppermute | solution.py:769
  48.3 62.9 %copy-start.18 = (bf16[1024,1024]{1,0:T(8,128)(2,1)}, bf16[1024,1024]{1,0:T(8,128)(2,1)S(1)}, u32[]{:S(2)}) copy-start(bf16[1024,1024]{1,0:T(8,128)(2,1)S(1)} %maximum_bitcast_fusion.x.refs_0_) | copy-start | bytes 6291460
  48.4 22.5 %copy-start.26 = (bf16[2,512,1024]{2,1,0:T(8,128)(2,1)S(1)}, bf16[2,512,1024]{2,1,0:T(8,128)(2,1)}, u32[]{:S(2)}) copy-start(bf16[2,512,1024]{2,1,0:T(8,128)(2,1)} %param.16) | copy-start | bytes 6291460
  52.1 69.1 %copy-start.7 = (bf16[1024,128]{1,0:T(8,128)(2,1)}, bf16[1024,128]{1,0:T(8,128)(2,1)S(1)}, u32[]{:S(2)}) copy-start(bf16[1024,128]{1,0:T(8,128)(2,1)S(1)} %get-tuple-element.452.fk_ref) | copy-start | bytes 786436
  121.3 21.7 %slice-start = ((bf16[1024,8320]{1,0:T(8,128)(2,1)}), bf16[1024,3]{1,0:T(8,128)(2,1)S(1)}, s32[]{:S(2)}) async-start(bf16[1024,8320]{1,0:T(8,128)(2,1)} %all-gather.4.cloned.1.call-done.out_w.cross_w), calls=%async_computation.6 | async-start | bytes 524288 | tf_op jit(solution)/shard_map/slice | solution.py:1318
  155.5 39.7 %collective-permute-start.3 = (bf16[1,512,1024]{2,1,0:T(8,128)(2,1)}, bf16[1,512,1024]{2,1,0:T(8,128)(2,1)}, u32[]{:S(2)}, u32[]{:S(2)}) collective-permute-start(bf16[1,512,1024]{2,1,0:T(8,128)(2,1)} %constant_dynamic-slice_fusion.2), channel_id=1, source_target_pairs={{0,1},{1,0},{2,3},{3,2},{4,5},{5,4},{6,7},{7,6},{8,9},{9,8},{10,11... | collective-permute-start | bytes 3145736 | tf_op jit(solution)/shard_map/ppermute | solution.py:769
  264.3 313.6 %reduce-scatter.5.cloned.1.call-start = ((), (), s32[]{:S(2)}) async-start(), calls=%async_computation.4 | async-start | bytes 11419648 | tf_op jit(solution)/shard_map/reduce_scatter | solution.py:1145
  296.2 21.2 %collective-permute-start.4 = (bf16[1024,2048]{1,0:T(8,128)(2,1)}, bf16[1024,2048]{1,0:T(8,128)(2,1)}, u32[]{:S(2)}, u32[]{:S(2)}) collective-permute-start(bf16[1024,2048]{1,0:T(8,128)(2,1)} %get-tuple-element.214), channel_id=1, source_target_pairs={{0,2},{2,0},{4,6},{6,4},{8,10},{10,8},{12,14},{14,12},{16,18},{18,... | collective-permute-start | bytes 12582920 | tf_op jit(solution)/shard_map/ppermute | solution.py:869
  296.3 21.1 %copy-start.21 = (bf16[1024,2048]{1,0:T(8,128)(2,1)S(1)}, bf16[1024,2048]{1,0:T(8,128)(2,1)}, u32[]{:S(2)}) copy-start(bf16[1024,2048]{1,0:T(8,128)(2,1)} %get-tuple-element.217) | copy-start | bytes 12582916
  321.2 65.2 %collective-permute-start.6 = (bf16[4,1,128,2048]{3,2,1,0:T(8,128)(2,1)}, bf16[4,1,128,2048]{3,2,1,0:T(8,128)(2,1)}, u32[]{:S(2)}, u32[]{:S(2)}) collective-permute-start(bf16[4,1,128,2048]{3,2,1,0:T(8,128)(2,1)} %add_convert_fusion), channel_id=1, source_target_pairs={{0,4},{2,6},{4,0},{6,2},{8,12},{10,14},{12,8},{14,10},{16,20},{18,... | collective-permute-start | bytes 6291464 | tf_op jit(solution)/shard_map/ppermute | solution.py:873
  322.4 49.3 %collective-permute-start.5 = (bf16[1,512,1024]{2,1,0:T(8,128)(2,1)}, bf16[1,512,1024]{2,1,0:T(8,128)(2,1)}, u32[]{:S(2)}, u32[]{:S(2)}) collective-permute-start(bf16[1,512,1024]{2,1,0:T(8,128)(2,1)} %dynamic-slice_bitcast_fusion), channel_id=1, source_target_pairs={{0,1},{1,0},{2,3},{3,2},{4,5},{5,4},{6,7},{7,6},{8,9},{9,8},{10,11... | collective-permute-start | bytes 3145736 | tf_op jit(solution)/shard_map/ppermute | solution.py:769
  389.5 37.1 %collective-permute-start.7 = (bf16[4,1,128,1024]{3,2,1,0:T(8,128)(2,1)S(1)}, bf16[4,1,128,1024]{3,2,1,0:T(8,128)(2,1)}, u32[]{:S(2)}, u32[]{:S(2)}) collective-permute-start(bf16[4,1,128,1024]{3,2,1,0:T(8,128)(2,1)S(1)} %add_convert_fusion.1), channel_id=1, source_target_pairs={{0,1},{1,0},{2,3},{3,2},{4,5},{5,4},{6,7},{7,6},{8,9},{9,8},{10,11... | collective-permute-start | bytes 3145736 | tf_op jit(solution)/shard_map/ppermute | solution.py:769
  442.9 45.1 %collective-permute-start.12 = (bf16[1,512,1024]{2,1,0:T(8,128)(2,1)}, bf16[1,512,1024]{2,1,0:T(8,128)(2,1)}, u32[]{:S(2)}, u32[]{:S(2)}) collective-permute-start(bf16[1,512,1024]{2,1,0:T(8,128)(2,1)} %fusion.27), channel_id=1, source_target_pairs={{0,1},{1,0},{2,3},{3,2},{4,5},{5,4},{6,7},{7,6},{8,9},{9,8},{10,11... | collective-permute-start | bytes 3145736 | tf_op jit(solution)/shard_map/ppermute | solution.py:769
  444.6 34.1 %collective-permute-start.11 = (bf16[256,1024]{1,0:T(8,128)(2,1)}, bf16[256,1024]{1,0:T(8,128)(2,1)}, u32[]{:S(2)}, u32[]{:S(2)}) collective-permute-start(bf16[256,1024]{1,0:T(8,128)(2,1)} %reduce-scatter.3.cloned.1.call-done), channel_id=1, source_target_pairs={{0,1},{1,0},{2,3},{3,2},{4,5},{5,4},{6,7},{7,6},{8,9},{9,8},{10,11... | collective-permute-start | bytes 1572872 | tf_op jit(solution)/shard_map/ppermute | solution.py:769
  444.9 24.8 %collective-permute-start.8 = (bf16[1,1,128,1024]{3,2,1,0:T(8,128)(2,1)}, bf16[1,1,128,1024]{3,2,1,0:T(8,128)(2,1)}, u32[]{:S(2)}, u32[]{:S(2)}) collective-permute-start(bf16[1,1,128,1024]{3,2,1,0:T(8,128)(2,1)} %get-tuple-element.258), channel_id=1, source_target_pairs={{0,8},{2,10},{4,12},{6,14},{8,16},{10,18},{12,20},{14,22},{16,24},... | collective-permute-start | bytes 786440 | tf_op jit(solution)/shard_map/ppermute | solution.py:877
  446.6 23.1 %collective-permute-start.9 = (bf16[1,1,128,1024]{3,2,1,0:T(8,128)(2,1)}, bf16[1,1,128,1024]{3,2,1,0:T(8,128)(2,1)}, u32[]{:S(2)}, u32[]{:S(2)}) collective-permute-start(bf16[1,1,128,1024]{3,2,1,0:T(8,128)(2,1)} %get-tuple-element.259), channel_id=1, source_target_pairs={{0,16},{2,18},{4,20},{6,22},{8,24},{10,26},{12,28},{14,30},{16,0},... | collective-permute-start | bytes 786440 | tf_op jit(solution)/shard_map/ppermute | solution.py:877
  448.9 20.8 %collective-permute-start.10 = (bf16[1,1,128,1024]{3,2,1,0:T(8,128)(2,1)}, bf16[1,1,128,1024]{3,2,1,0:T(8,128)(2,1)}, u32[]{:S(2)}, u32[]{:S(2)}) collective-permute-start(bf16[1,1,128,1024]{3,2,1,0:T(8,128)(2,1)} %get-tuple-element.260), channel_id=1, source_target_pairs={{0,24},{2,26},{4,28},{6,30},{8,0},{10,2},{12,4},{14,6},{16,8},{18,... | collective-permute-start | bytes 786440 | tf_op jit(solution)/shard_map/ppermute | solution.py:877
  469.7 18.3 %copy-start.13 = (bf16[1024,512]{1,0:T(8,128)(2,1)}, bf16[1024,512]{1,0:T(8,128)(2,1)S(1)}, u32[]{:S(2)}) copy-start(bf16[1024,512]{1,0:T(8,128)(2,1)S(1)} %get-tuple-element.271.refs_2_) | copy-start | bytes 3145732
  488.0 24.0 %collective-permute-start.13 = (bf16[1024,768]{1,0:T(8,128)(2,1)}, bf16[1024,768]{1,0:T(8,128)(2,1)}, u32[]{:S(2)}, u32[]{:S(2)}) collective-permute-start(bf16[1024,768]{1,0:T(8,128)(2,1)} %get-tuple-element.278), channel_id=1, source_target_pairs={{0,2},{2,0},{4,6},{6,4},{8,10},{10,8},{12,14},{14,12},{16,18},{18,... | collective-permute-start | bytes 4718600 | tf_op jit(solution)/shard_map/ppermute | solution.py:869
  489.8 22.1 %collective-permute-start.14 = (bf16[64,1024]{1,0:T(8,128)(2,1)S(1)}, bf16[64,1024]{1,0:T(8,128)(2,1)S(1)}, u32[]{:S(2)}, u32[]{:S(2)}) collective-permute-start(bf16[64,1024]{1,0:T(8,128)(2,1)S(1)} %get-tuple-element.279), channel_id=1, source_target_pairs={{0,1},{1,0},{2,3},{3,2},{4,5},{5,4},{6,7},{7,6},{8,9},{9,8},{10,11... | collective-permute-start | bytes 393224 | tf_op jit(solution)/shard_map/ppermute | solution.py:769
  491.4 20.6 %collective-permute-start.15 = (bf16[64,1024]{1,0:T(8,128)(2,1)S(1)}, bf16[64,1024]{1,0:T(8,128)(2,1)S(1)}, u32[]{:S(2)}, u32[]{:S(2)}) collective-permute-start(bf16[64,1024]{1,0:T(8,128)(2,1)S(1)} %copy-done.46), channel_id=1, source_target_pairs={{0,2},{2,0},{4,6},{6,4},{8,10},{10,8},{12,14},{14,12},{16,18},{18,... | collective-permute-start | bytes 393224 | tf_op jit(solution)/shard_map/ppermute | solution.py:869
  491.6 20.4 %collective-permute-start.16 = (bf16[64,1024]{1,0:T(8,128)(2,1)S(1)}, bf16[64,1024]{1,0:T(8,128)(2,1)S(1)}, u32[]{:S(2)}, u32[]{:S(2)}) collective-permute-start(bf16[64,1024]{1,0:T(8,128)(2,1)S(1)} %copy-done.46), channel_id=1, source_target_pairs={{0,3},{1,2},{2,1},{3,0},{4,7},{5,6},{6,5},{7,4},{8,11},{9,10},{10,... | collective-permute-start | bytes 393224 | tf_op jit(solution)/shard_map/ppermute | solution.py:882
  493.5 18.5 %copy-start.29 = (bf16[1024,768]{1,0:T(8,128)(2,1)S(1)}, bf16[1024,768]{1,0:T(8,128)(2,1)}, u32[]{:S(2)}) copy-start(bf16[1024,768]{1,0:T(8,128)(2,1)} %get-tuple-element.285) | copy-start | bytes 4718596
  514.4 26.6 %collective-permute-start.17 = (bf16[4,1,128,768]{3,2,1,0:T(8,128)(2,1)}, bf16[4,1,128,768]{3,2,1,0:T(8,128)(2,1)}, u32[]{:S(2)}, u32[]{:S(2)}) collective-permute-start(bf16[4,1,128,768]{3,2,1,0:T(8,128)(2,1)} %add_convert_fusion.3), channel_id=1, source_target_pairs={{0,4},{2,6},{4,0},{6,2},{8,12},{10,14},{12,8},{14,10},{16,20},{18,... | collective-permute-start | bytes 2359304 | tf_op jit(solution)/shard_map/ppermute | solution.py:873
  542.6 4.2 collective-permute-start.18
  544.9 31.4 %collective-permute-start.23 = (bf16[1,512,1024]{2,1,0:T(8,128)(2,1)S(1)}, bf16[1,512,1024]{2,1,0:T(8,128)(2,1)S(1)}, u32[]{:S(2)}, u32[]{:S(2)}) collective-permute-start(bf16[1,512,1024]{2,1,0:T(8,128)(2,1)S(1)} %fusion.28), channel_id=1, source_target_pairs={{0,1},{1,0},{2,3},{3,2},{4,5},{5,4},{6,7},{7,6},{8,9},{9,8},{10,11... | collective-permute-start | bytes 3145736 | tf_op jit(solution)/shard_map/ppermute | solution.py:769
  547.0 30.0 %collective-permute-start.19 = (bf16[4,1,128,768]{3,2,1,0:T(8,128)(2,1)S(1)}, bf16[4,1,128,768]{3,2,1,0:T(8,128)(2,1)S(1)}, u32[]{:S(2)}, u32[]{:S(2)}) collective-permute-start(bf16[4,1,128,768]{3,2,1,0:T(8,128)(2,1)S(1)} %add_convert_fusion.2), channel_id=1, source_target_pairs={{0,4},{2,6},{4,0},{6,2},{8,12},{10,14},{12,8},{14,10},{16,20},{18,... | collective-permute-start | bytes 2359304 | tf_op jit(solution)/shard_map/ppermute | solution.py:873
  548.0 15.4 %collective-permute-start.20 = (bf16[1,1,128,768]{3,2,1,0:T(8,128)(2,1)S(1)}, bf16[1,1,128,768]{3,2,1,0:T(8,128)(2,1)S(1)}, u32[]{:S(2)}, u32[]{:S(2)}) collective-permute-start(bf16[1,1,128,768]{3,2,1,0:T(8,128)(2,1)S(1)} %get-tuple-element.301), channel_id=1, source_target_pairs={{0,8},{2,10},{4,12},{6,14},{8,16},{10,18},{12,20},{14,22},{16,24},... | collective-permute-start | bytes 589832 | tf_op jit(solution)/shard_map/ppermute | solution.py:877
  548.8 27.5 %collective-permute-start.21 = (bf16[1,1,128,768]{3,2,1,0:T(8,128)(2,1)S(1)}, bf16[1,1,128,768]{3,2,1,0:T(8,128)(2,1)S(1)}, u32[]{:S(2)}, u32[]{:S(2)}) collective-permute-start(bf16[1,1,128,768]{3,2,1,0:T(8,128)(2,1)S(1)} %get-tuple-element.302), channel_id=1, source_target_pairs={{0,16},{2,18},{4,20},{6,22},{8,24},{10,26},{12,28},{14,30},{16,0},... | collective-permute-start | bytes 589832 | tf_op jit(solution)/shard_map/ppermute | solution.py:877
  554.1 22.2 %collective-permute-start.22 = (bf16[1,1,128,768]{3,2,1,0:T(8,128)(2,1)S(1)}, bf16[1,1,128,768]{3,2,1,0:T(8,128)(2,1)S(1)}, u32[]{:S(2)}, u32[]{:S(2)}) collective-permute-start(bf16[1,1,128,768]{3,2,1,0:T(8,128)(2,1)S(1)} %get-tuple-element.303), channel_id=1, source_target_pairs={{0,24},{2,26},{4,28},{6,30},{8,0},{10,2},{12,4},{14,6},{16,8},{18,... | collective-permute-start | bytes 589832 | tf_op jit(solution)/shard_map/ppermute | solution.py:877
  554.1 22.2 %copy-start.55 = (f32[64,4096]{1,0:T(8,128)}, f32[64,4096]{1,0:T(8,128)S(1)}, u32[]{:S(2)}) copy-start(f32[64,4096]{1,0:T(8,128)S(1)} %slice_dynamic-update-slice_fusion) | copy-start | bytes 3145732
  580.6 18.3 %collective-permute-start.27 = (bf16[1,1,128,384]{3,2,1,0:T(8,128)(2,1)S(1)}, bf16[1,1,128,384]{3,2,1,0:T(8,128)(2,1)S(1)}, u32[]{:S(2)}, u32[]{:S(2)}) collective-permute-start(bf16[1,1,128,384]{3,2,1,0:T(8,128)(2,1)S(1)} %add_convert_fusion.17), channel_id=1, source_target_pairs={{0,1},{1,0},{2,3},{3,2},{4,5},{5,4},{6,7},{7,6},{8,9},{9,8},{10,11... | collective-permute-start | bytes 294920 | tf_op jit(solution)/shard_map/ppermute | solution.py:769
  582.2 16.8 %collective-permute-start.24 = (bf16[1,1,128,768]{3,2,1,0:T(8,128)(2,1)S(1)}, bf16[1,1,128,768]{3,2,1,0:T(8,128)(2,1)S(1)}, u32[]{:S(2)}, u32[]{:S(2)}) collective-permute-start(bf16[1,1,128,768]{3,2,1,0:T(8,128)(2,1)S(1)} %get-tuple-element.313), channel_id=1, source_target_pairs={{0,8},{2,10},{4,12},{6,14},{8,16},{10,18},{12,20},{14,22},{16,24},... | collective-permute-start | bytes 589832 | tf_op jit(solution)/shard_map/ppermute | solution.py:877
  586.6 14.2 %collective-permute-start.25 = (bf16[1,1,128,768]{3,2,1,0:T(8,128)(2,1)S(1)}, bf16[1,1,128,768]{3,2,1,0:T(8,128)(2,1)S(1)}, u32[]{:S(2)}, u32[]{:S(2)}) collective-permute-start(bf16[1,1,128,768]{3,2,1,0:T(8,128)(2,1)S(1)} %get-tuple-element.314), channel_id=1, source_target_pairs={{0,16},{2,18},{4,20},{6,22},{8,24},{10,26},{12,28},{14,30},{16,0},... | collective-permute-start | bytes 589832 | tf_op jit(solution)/shard_map/ppermute | solution.py:877
  588.1 12.8 %collective-permute-start.26 = (bf16[1,1,128,768]{3,2,1,0:T(8,128)(2,1)S(1)}, bf16[1,1,128,768]{3,2,1,0:T(8,128)(2,1)S(1)}, u32[]{:S(2)}, u32[]{:S(2)}) collective-permute-start(bf16[1,1,128,768]{3,2,1,0:T(8,128)(2,1)S(1)} %get-tuple-element.315), channel_id=1, source_target_pairs={{0,24},{2,26},{4,28},{6,30},{8,0},{10,2},{12,4},{14,6},{16,8},{18,... | collective-permute-start | bytes 589832 | tf_op jit(solution)/shard_map/ppermute | solution.py:877
  589.1 16.3 %collective-permute-start.28 = (bf16[64,5248]{1,0:T(8,128)(2,1)S(1)}, bf16[64,5248]{1,0:T(8,128)(2,1)S(1)}, u32[]{:S(2)}, u32[]{:S(2)}) collective-permute-start(bf16[64,5248]{1,0:T(8,128)(2,1)S(1)} %copy-done.34), channel_id=1, source_target_pairs={{0,1},{1,0},{2,3},{3,2},{4,5},{5,4},{6,7},{7,6},{8,9},{9,8},{10,11... | collective-permute-start | bytes 2015240 | tf_op jit(solution)/shard_map/ppermute | solution.py:769
  607.8 6.7 %collective-permute-start.30 = (bf16[64,384]{1,0:T(8,128)(2,1)S(1)}, bf16[64,384]{1,0:T(8,128)(2,1)S(1)}, u32[]{:S(2)}, u32[]{:S(2)}) collective-permute-start(bf16[64,384]{1,0:T(8,128)(2,1)S(1)} %get-tuple-element.323), channel_id=1, source_target_pairs={{0,1},{1,0},{2,3},{3,2},{4,5},{5,4},{6,7},{7,6},{8,9},{9,8},{10,11... | collective-permute-start | bytes 147464 | tf_op jit(solution)/shard_map/ppermute | solution.py:769
  608.3 6.2 collective-permute-start.31
  608.3 6.2 collective-permute-start.32
  610.0 5.0 collective-permute-start.29
  616.3 4.3 collective-permute-start.33
  617.4 3.2 collective-permute-start.34
  617.4 3.6 collective-permute-start.35
  (52 other events, 348.5 us)
Sparse Core Ops, SparseCore 0:
  12.8 93.0 all-gather.3
  107.4 90.2 all-gather.5
  264.4 119.7 reduce-scatter.2
  430.9 146.9 reduce-scatter.4

commit v5 on v4

--- a/solution.py
+++ b/solution.py
@@ -1409,7 +1409,7 @@
     arrays = (target_flat, memory_id_flat, cross_queries, memory_keys, memory_values)
     arrays += (cross_flat, cross_lse, d_cross)
     grads = each_row(functools.partial(cross_backward, pairs=(0, 2 * half)), rows, arrays)
-    d_cross_low, d_memory_keys, d_memory_values = tick(grads, output, up_grad)
+    d_cross_low, d_memory_keys, d_memory_values = tick(grads, output)
     d_first_sum, d_branch_one, d_self, first_sums = row_tiles(
         first_back_kernel,
         "first_back",
@@ -1418,6 +1418,7 @@
         [full, low, low],
         True,
     )
+    d_branch_one, d_self = tick((d_branch_one, d_self), up_grad)
     every = [first_sums[0], second_sums[0], third_sums[0]]
     grad_rows = every + [first_sums[1], second_sums[1], third_sums[1], third_sums[2]]
     cross_grad = Flight(
@@ -1431,11 +1432,11 @@
             (jnp.stack(grad_rows), grad_bias_up),
         )
     )
-    d_self = tick(d_self, cross_grad, up_grad)
+    d_self = tick(d_self, cross_grad)
     d_memory = back_prod(d_memory_keys, mk_full) + back_prod(d_memory_values, mv_full)
     d_self, d_memory = lax.optimization_barrier((d_self, d_memory))
     d_memory = Flight(rows_out_steps(d_memory.reshape(rows, length, D), jnp.float32))
-    d_self = tick(d_self, down_grad, d_memory)
+    d_self = tick(d_self, down_grad, d_memory, up_grad)
 
     def self_backward(id_row, *arrays, pairs):
         fq, fk = document_features(id_row, id_row)

time: 636 us -> 640 us (level)
  starting transfers between devices: 42.7 us -> 62.2 us
  waiting for transfers between devices: 135 us -> 122 us
    ppermute x9, starting transfers between devices: 18.7 us -> 38 us  [to_z(): lax.ppermute(array, 'batch', [(n, (n + 4 * step) % 16) for n in range(16)])]
    ppermute x3, waiting for transfers between devices: 19.6 us -> 4.62 us  [to_x(): return lax.ppermute(array, 'batch', [(n, n ^ 2) for n in range(16)])]
    unnamed x147 -> x145, local copies, waits for them, and re-layouts: 23.6 us -> 23.1 us
  transfers between devices with their start and end apart: 40 -> 40, of which waited for: 14 -> 14; matrix products, arithmetic and copies ran while one was open for 17% -> 16% of each run, Pallas kernels for 39% -> 39%
where the time goes in v5:
time: 640 us; the launch traced here: 633 us
  Pallas kernels  284 us (44%)
  waiting for transfers between devices  122 us (19%)
  starting transfers between devices  62.2 us (10%)
  matrix products  62.1 us (10%)
  other arithmetic  47.7 us (7%)
  local copies, waits for them, and re-layouts  38.8 us (6%)
  between operations  15.3 us (2%)
    pallas_call x5, Pallas kernels, attention_call(): pl.pallas_call(functools.partial(kernel, causal), grid=(count,), in_specs...  130 us
    pallas_call x5, Pallas kernels, row_tiles(): pl.pallas_call(kernel, grid=(rows // tall,), in_specs=in_specs, out_specs...  72.4 us
    ppermute x15, waiting for transfers between devices, swap_pair(): return lax.ppermute(array, 'blk', [(0, 1), (1, 0)])  59.5 us
    pallas_call x4, Pallas kernels, joined_grads(): pl.pallas_call(functools.partial(grads_kernel, plan, halved), in_specs=[a...  43.6 us
    ppermute x9, starting transfers between devices, to_z(): lax.ppermute(array, 'batch', [(n, (n + 4 * step) % 16) for n in range(16)])  38 us
    all_gather x1, waiting for transfers between devices, gathered(): return lax.all_gather(shard, 'batch', axis=axis, tiled=True)  33.3 us
    dot_general x5, matrix products, dot32(): return jnp.dot(left, right, preferred_element_type=jnp.float32)  26.2 us
    ppermute x9, waiting for transfers between devices, to_z(): lax.ppermute(array, 'batch', [(n, (n + 4 * step) % 16) for n in range(16)])  24.4 us
  transfers between devices with their start and end apart: 40, of which 14 were waited for; matrix products, arithmetic and copies ran while one was open for 16% of the time, Pallas kernels for 39%

profile of v5, /device:TPU:0, one launch (start us, length us, event | category | flops | bytes accessed | tf_op | source)
XLA Modules:
  0.0 632.8 jit_solution(16267273801569806522)
XLA Ops:
  9.6 3.1 concatenate.68
  19.8 3.0 collective-permute-start
  23.9 22.3 %collective-permute-done.1 = s32[1,512,2]{1,0,2:T(1,128)S(1)} collective-permute-done((s32[1,512,2]{1,0,2:T(1,128)S(1)}, s32[1,512,2]{1,0,2:T(1,128)S(1)}, u32[]{:S(2)}, u32[]{:S(2)}) %collective-permute-start.1) | collective-permute-done | bytes 4128 | tf_op jit(solution)/shard_map/ppermute | solution.py:769
  52.1 18.8 %collective-permute-done.2 = bf16[1,512,1024]{2,1,0:T(8,128)(2,1)S(1)} collective-permute-done((bf16[1,512,1024]{2,1,0:T(8,128)(2,1)}, bf16[1,512,1024]{2,1,0:T(8,128)(2,1)S(1)}, u32[]{:S(2)}, u32[]{:S(2)}) %collective-permute-start.2) | collective-permute-done | bytes 1048608 | tf_op jit(solution)/shard_map/ppermute | solution.py:769
  72.5 33.3 %all-gather.4.cloned.1.call-done.out_w.cross_w = bf16[1024,8320]{1,0:T(8,128)(2,1)} async-done(((bf16[64,8320]{1,0:T(8,128)(2,1)}), bf16[1024,8320]{1,0:T(8,128)(2,1)}) %all-gather.4.cloned.1.call-update) | async-done | bytes 17039376 | tf_op jit(solution)/shard_map/all_gather | solution.py:810
  105.8 5.4 convolution_convert_fusion.3.v_ref
  111.3 6.0 convolution_convert_fusion.4.k_ref
  117.3 3.9 convolution_convert_fusion.5.q_ref
  121.3 20.3 %attention_forward.2 = (bf16[1024,1024]{1,0:T(8,128)(2,1)S(1)}, f32[1024,1024]{1,0:T(8,128)}) custom-call(bf16[1024,1024]{1,0:T(8,128)(2,1)S(1)} %convolution_convert_fusion.5.q_ref, bf16[1024,1024]{1,0:T(8,128)(2,1)} %convolution_convert_fusion.4.k_ref, bf16[1024,1024]{1,0:T(8,128)(2,1)} %convolution_convert_fusion.3.v_ref, ...), custom_call_target="tpu_custom_call" | custom-call | flops 1024 | bytes 1024 | tf_op jit(solution)/shard_map/attention_forward/pallas_call | solution.py:187
  145.2 10.3 %first_norm.1 = (f32[1024,1024]{1,0:T(8,128)}, f32[1024,1024]{1,0:T(8,128)}, bf16[1024,1024]{1,0:T(8,128)(2,1)}, bf16[1024,1024]{1,0:T(8,128)(2,1)}) custom-call(bf16[1024,1024]{1,0:T(8,128)(2,1)} %copy-done, bf16[1024,1024]{1,0:T(8,128)(2,1)} %copy-done.18, bf16[1024,8320]{1,0:T(8,128)(2,1)} %all-gather.4.cloned.1.call-done.out_w.cross_w, ...), custom_call_target="tpu_custom_call" | custom-call | flops 1024 | bytes 1024 | tf_op jit(solution)/shard_map/first_norm/pallas_call | solution.py:314
  156.9 5.3 convolution_convert_fusion.1.v_ref
  162.2 5.5 convolution_convert_fusion.2.k_ref
  167.8 25.1 %attention_forward.3 = (bf16[1024,1024]{1,0:T(8,128)(2,1)S(1)}, f32[1024,1024]{1,0:T(8,128)}) custom-call(bf16[1024,1024]{1,0:T(8,128)(2,1)S(1)} %copy-done.6, bf16[1024,1024]{1,0:T(8,128)(2,1)} %convolution_convert_fusion.2.k_ref, bf16[1024,1024]{1,0:T(8,128)(2,1)} %convolution_convert_fusion.1.v_ref, bf16[1024,128]{1,0:T(8,128)(2,1)S(1)} %compare_convert_fusion.fq_ref, ...), custom_call_target="tpu_custom_call" | custom-call | flops 1024 | bytes 1024 | tf_op jit(solution)/shard_map/attention_forward/pallas_call | solution.py:187
  195.2 9.2 %second_norm.1 = (f32[1024,1024]{1,0:T(8,128)}, f32[1024,1024]{1,0:T(8,128)}, bf16[1024,1024]{1,0:T(8,128)(2,1)}) custom-call(bf16[1024,1024]{1,0:T(8,128)(2,1)} %copy-done.1, f32[1024,1024]{1,0:T(8,128)} %get-tuple-element.197.first, bf16[1024,8320]{1,0:T(8,128)(2,1)} %all-gather.4.cloned.1.call-done.out_w.cross_w, f32[8,1024]{1,0:T(8,128)} %maximum_convert_fusion.norms), custom_call_target="tpu_custom_call" | custom-call | flops 1024 | bytes 1024 | tf_op jit(solution)/shard_map/second_norm/pallas_call | solution.py:314
  207.3 20.8 %gelu_rows.1 = (bf16[1024,4096]{1,0:T(8,128)(2,1)}, f32[1024,4096]{1,0:T(8,128)}) custom-call(bf16[1024,1024]{1,0:T(8,128)(2,1)} %get-tuple-element.198.left_ref.refs_0_, bf16[16,520,1024]{2,1,0:T(8,128)(2,1)} %bitcast.65, f32[1,4096]{1,0:T(1,128)} %reshape.166.bias_ref), custom_call_target="tpu_custom_call" | custom-call | flops 1024 | bytes 1024 | tf_op jit(solution)/shard_map/gelu_rows/pallas_call | solution.py:255
  228.0 19.0 %third_norm.1 = (bf16[1024,1024]{1,0:T(8,128)(2,1)}, f32[1024,1024]{1,0:T(8,128)}, bf16[1024,1024]{1,0:T(8,128)(2,1)}, f32[8,1024]{1,0:T(8,128)}) custom-call(bf16[1024,4096]{1,0:T(8,128)(2,1)} %get-tuple-element.199.hidden, f32[1024,1024]{1,0:T(8,128)} %get-tuple-element.200.second, bf16[1024,1024]{1,0:T(8,128)(2,1)} %maximum_bitcast_fusion.2.cot, ...), custom_call_target="tpu_custom_call" | custom-call | flops 1024 | bytes 1024 | tf_op jit(solution)/shard_map/third_norm/pallas_call | solution.py:314
  247.0 15.0 %convolution_convert_fusion = bf16[4096,1024]{1,0:T(8,128)(2,1)} fusion(bf16[1024,4096]{1,0:T(8,128)(2,1)} %get-tuple-element.199.hidden, bf16[1024,1024]{1,0:T(8,128)(2,1)} %get-tuple-element.208.left_ref), kind=kOutput, calls=%fused_computation | convolution fusion | flops 8594128896 | bytes 18874368 | tf_op jit(solution)/shard_map/tk,tn->kn/dot_general | solution.py:461
  265.9 17.4 %gelu_back_rows.1 = (bf16[1024,4096]{1,0:T(8,128)(2,1)}, f32[1,1,4096]{2,1,0:T(1,128)S(1)}) custom-call(bf16[1024,1024]{1,0:T(8,128)(2,1)S(1)} %copy-done.12, bf16[16,520,1024]{2,1,0:T(8,128)(2,1)} %bitcast.67, f32[1024,4096]{1,0:T(8,128)} %get-tuple-element.209.slope_ref), custom_call_target="tpu_custom_call" | custom-call | flops 1024 | bytes 1024 | tf_op jit(solution)/shard_map/gelu_back_rows/pallas_call | solution.py:415
  283.3 12.9 %joined_grads.4 = (bf16[1024,2048]{1,0:T(8,128)(2,1)}, bf16[1024,2048]{1,0:T(8,128)(2,1)}) custom-call(bf16[1024,1024]{1,0:T(8,128)(2,1)S(1)} %copy-done.5, bf16[1024,4096]{1,0:T(8,128)(2,1)} %get-tuple-element.212.refs_1_.d_pre), custom_call_target="tpu_custom_call" | custom-call | flops 1024 | bytes 1024 | tf_op jit(solution)/shard_map/joined_grads/pallas_call | solution.py:1086
  296.3 21.1 %second_back.1 = (f32[1024,1024]{1,0:T(8,128)}, bf16[1024,1024]{1,0:T(8,128)(2,1)}, bf16[1024,1024]{1,0:T(8,128)(2,1)}, f32[8,1024]{1,0:T(8,128)}) custom-call(bf16[1024,4096]{1,0:T(8,128)(2,1)} %get-tuple-element.212.refs_1_.d_pre, f32[1024,1024]{1,0:T(8,128)} %get-tuple-element.213.d_third, f32[1024,1024]{1,0:T(8,128)} %get-tuple-element.214.summed, ...), custom_call_target="tpu_custom_call" | custom-call | flops 1024 | bytes 1024 | tf_op jit(solution)/shard_map/second_back/pallas_call | solution.py:314
  317.5 3.9 add_convert_fusion
  324.0 48.5 %attention_backward.3 = (bf16[1024,1024]{1,0:T(8,128)(2,1)S(1)}, bf16[1024,1024]{1,0:T(8,128)(2,1)S(1)}, bf16[1024,1024]{1,0:T(8,128)(2,1)}) custom-call(bf16[1024,1024]{1,0:T(8,128)(2,1)} %get-tuple-element.189.q_ref, bf16[1024,1024]{1,0:T(8,128)(2,1)} %convolution_convert_fusion.2.k_ref, bf16[1024,1024]{1,0:T(8,128)(2,1)} %convolution_convert_fusion.1.v_ref, ...), custom_call_target="tpu_custom_call" | custom-call | flops 1024 | bytes 1024 | tf_op jit(solution)/shard_map/attention_backward/pallas_call | solution.py:187
  375.1 13.0 %first_back.1 = (f32[1024,1024]{1,0:T(8,128)}, bf16[1024,1024]{1,0:T(8,128)(2,1)}, bf16[1024,1024]{1,0:T(8,128)(2,1)}, f32[8,1024]{1,0:T(8,128)}) custom-call(bf16[1024,1024]{1,0:T(8,128)(2,1)} %copy-done.2, f32[1024,1024]{1,0:T(8,128)} %get-tuple-element.232.d_second, f32[1024,1024]{1,0:T(8,128)} %get-tuple-element.233.summed, ...), custom_call_target="tpu_custom_call" | custom-call | flops 1024 | bytes 1024 | tf_op jit(solution)/shard_map/first_back/pallas_call | solution.py:314
  389.3 3.2 add_convert_fusion.1
  392.6 16.2 %joined_grads.5 = bf16[1024,5248]{1,0:T(8,128)(2,1)} custom-call(bf16[1024,1024]{1,0:T(8,128)(2,1)S(1)} %copy-done.4, bf16[1024,1024]{1,0:T(8,128)(2,1)S(1)} %copy-done.10, bf16[1024,1024]{1,0:T(8,128)(2,1)} %copy-done.1, bf16[1024,1024]{1,0:T(8,128)(2,1)} %copy-done, bf16[1024,1024]{1,0:T(8,128)(2,1)} %copy-done.11, ...), custom_call_target="tpu_custom_call" | custom-call | flops 1024 | bytes 1024 | tf_op jit(solution)/shard_map/joined_grads/pallas_call | solution.py:1086
  410.2 4.6 fusion.14
  414.8 4.0 convolution_add_fusion
  422.0 11.8 %collective-permute-done.7 = bf16[4,1,128,1024]{3,2,1,0:T(8,128)(2,1)} collective-permute-done((bf16[4,1,128,1024]{3,2,1,0:T(8,128)(2,1)S(1)}, bf16[4,1,128,1024]{3,2,1,0:T(8,128)(2,1)}, u32[]{:S(2)}, u32[]{:S(2)}) %collective-permute-start.7) | collective-permute-done | bytes 1048608 | tf_op jit(solution)/shard_map/ppermute | solution.py:769
  433.8 4.1 add_convert_fusion.5
  446.4 17.8 %attention_backward.4 = (bf16[1024,512]{1,0:T(8,128)(2,1)S(1)}, bf16[1024,512]{1,0:T(8,128)(2,1)S(1)}, bf16[1024,512]{1,0:T(8,128)(2,1)S(1)}) custom-call(bf16[1024,1024]{1,0:T(8,128)(2,1)S(1)} %convolution_convert_fusion.5.q_ref, bf16[1024,1024]{1,0:T(8,128)(2,1)} %convolution_convert_fusion.4.k_ref, bf16[1024,1024]{1,0:T(8,128)(2,1)} %convolution_convert_fusion.3.v_ref, ...), custom_call_target="tpu_custom_call" | custom-call | flops 1024 | bytes 1024 | tf_op jit(solution)/shard_map/attention_backward/pallas_call | solution.py:187
  464.3 8.7 %collective-permute-done.9 = bf16[1,1,128,1024]{3,2,1,0:T(8,128)(2,1)} collective-permute-done((bf16[1,1,128,1024]{3,2,1,0:T(8,128)(2,1)}, bf16[1,1,128,1024]{3,2,1,0:T(8,128)(2,1)}, u32[]{:S(2)}, u32[]{:S(2)}) %collective-permute-start.9) | collective-permute-done | bytes 262176 | tf_op jit(solution)/shard_map/ppermute | solution.py:877
  476.9 6.6 %joined_grads.6 = (bf16[1024,768]{1,0:T(8,128)(2,1)}, bf16[1024,768]{1,0:T(8,128)(2,1)}) custom-call(bf16[1024,1024]{1,0:T(8,128)(2,1)} %copy-done.18, bf16[1024,512]{1,0:T(8,128)(2,1)S(1)} %get-tuple-element.274.refs_1_, bf16[1024,512]{1,0:T(8,128)(2,1)S(1)} %get-tuple-element.277.refs_2_, bf16[1024,512]{1,0:T(8,128)(2,1)S(1)} %get-tuple-element.278.refs_3_), custom_call_target="tpu_custom_call" | custom-call | flops 1024 | bytes 1024 | tf_op jit(solution)/shard_map/joined_grads/pallas_call | solution.py:1086
  489.1 18.3 %attention_backward.5 = (bf16[1024,512]{1,0:T(8,128)(2,1)S(1)}, bf16[1024,512]{1,0:T(8,128)(2,1)S(1)}, bf16[1024,512]{1,0:T(8,128)(2,1)S(1)}) custom-call(bf16[1024,1024]{1,0:T(8,128)(2,1)S(1)} %convolution_convert_fusion.5.q_ref, bf16[1024,1024]{1,0:T(8,128)(2,1)} %convolution_convert_fusion.4.k_ref, bf16[1024,1024]{1,0:T(8,128)(2,1)} %convolution_convert_fusion.3.v_ref, ...), custom_call_target="tpu_custom_call" | custom-call | flops 1024 | bytes 1024 | tf_op jit(solution)/shard_map/attention_backward/pallas_call | solution.py:187
  507.6 2.5 add_convert_fusion.3
  510.5 4.0 fusion
  514.5 4.1 fusion.4
  518.7 4.3 add_add_fusion
  523.2 7.9 %joined_grads.7 = (bf16[1024,768]{1,0:T(8,128)(2,1)S(1)}, bf16[1024,768]{1,0:T(8,128)(2,1)}) custom-call(bf16[1024,1024]{1,0:T(8,128)(2,1)} %copy-done.18, bf16[1024,512]{1,0:T(8,128)(2,1)S(1)} %get-tuple-element.293, bf16[1024,512]{1,0:T(8,128)(2,1)S(1)} %get-tuple-element.294, bf16[1024,512]{1,0:T(8,128)(2,1)S(1)} %get-tuple-element.295), custom_call_target="tpu_custom_call" | custom-call | flops 1024 | bytes 1024 | tf_op jit(solution)/shard_map/joined_grads/pallas_call | solution.py:1086
  531.1 4.6 collective-permute-done.17
  537.4 2.3 convert_add_fusion.1
  543.2 20.4 %collective-permute-start.20 = (bf16[1,1,128,768]{3,2,1,0:T(8,128)(2,1)S(1)}, bf16[1,1,128,768]{3,2,1,0:T(8,128)(2,1)S(1)}, u32[]{:S(2)}, u32[]{:S(2)}) collective-permute-start(bf16[1,1,128,768]{3,2,1,0:T(8,128)(2,1)S(1)} %get-tuple-element.307), channel_id=1, source_target_pairs={{0,8},{2,10},{4,12},{6,14},{8,16},{10,18},{12,20},{14,22},{16,24},... | collective-permute-start | bytes 589832 | tf_op jit(solution)/shard_map/ppermute | solution.py:877
  566.1 4.7 collective-permute-done.20
  570.8 7.7 %collective-permute-done.21 = bf16[1,1,128,768]{3,2,1,0:T(8,128)(2,1)S(1)} collective-permute-done((bf16[1,1,128,768]{3,2,1,0:T(8,128)(2,1)S(1)}, bf16[1,1,128,768]{3,2,1,0:T(8,128)(2,1)S(1)}, u32[]{:S(2)}, u32[]{:S(2)}) %collective-permute-start.21) | collective-permute-done | bytes 196640 | tf_op jit(solution)/shard_map/ppermute | solution.py:877
  583.9 7.1 %collective-permute-start.24 = (bf16[1,1,128,768]{3,2,1,0:T(8,128)(2,1)S(1)}, bf16[1,1,128,768]{3,2,1,0:T(8,128)(2,1)S(1)}, u32[]{:S(2)}, u32[]{:S(2)}) collective-permute-start(bf16[1,1,128,768]{3,2,1,0:T(8,128)(2,1)S(1)} %get-tuple-element.319), channel_id=1, source_target_pairs={{0,8},{2,10},{4,12},{6,14},{8,16},{10,18},{12,20},{14,22},{16,24},... | collective-permute-start | bytes 589832 | tf_op jit(solution)/shard_map/ppermute | solution.py:877
  593.8 4.1 convert_select_fusion.1
  598.0 2.6 pad_maximum_fusion.1
  600.6 2.6 pad_maximum_fusion
  605.2 4.2 collective-permute-done.28
  (286 shorter events, 96.3 us)
Async XLA Ops:
  7.2 98.7 %all-gather.4.cloned.1.call-start = ((), (), s32[]{:S(2)}) async-start(), calls=%async_computation.2 | async-start | bytes 18104320 | tf_op jit(solution)/shard_map/all_gather | solution.py:810
  12.7 194.6 %all-gather.6.cloned.1.call-start = ((), (), s32[]{:S(2)}) async-start(), calls=%async_computation.5 | async-start | bytes 18104320 | tf_op jit(solution)/shard_map/all_gather | solution.py:1328
  18.7 415.2 %reduce-scatter.3.cloned.1.call-start = ((), (), s32[]{:S(2)}) async-start(), calls=%async_computation.3 | async-start | bytes 8912896 | tf_op jit(solution)/shard_map/reduce_scatter | solution.py:1145
  19.8 26.4 %collective-permute-start = (bf16[1,512,1024]{2,1,0:T(8,128)(2,1)}, bf16[1,512,1024]{2,1,0:T(8,128)(2,1)S(1)}, u32[]{:S(2)}, u32[]{:S(2)}) collective-permute-start(bf16[1,512,1024]{2,1,0:T(8,128)(2,1)} %constant_dynamic-slice_fusion.6), channel_id=1, source_target_pairs={{0,1},{1,0},{2,3},{3,2},{4,5},{5,4},{6,7},{7,6},{8,9},{9,8},{10,11... | collective-permute-start | bytes 3145736 | tf_op jit(solution)/shard_map/ppermute | solution.py:769
  22.8 23.5 %collective-permute-start.1 = (s32[1,512,2]{1,0,2:T(1,128)S(1)}, s32[1,512,2]{1,0,2:T(1,128)S(1)}, u32[]{:S(2)}, u32[]{:S(2)}) collective-permute-start(s32[1,512,2]{1,0,2:T(1,128)S(1)} %fusion.33), channel_id=1, source_target_pairs={{0,1},{1,0},{2,3},{3,2},{4,5},{5,4},{6,7},{7,6},{8,9},{9,8},{10,11... | collective-permute-start | bytes 12296 | tf_op jit(solution)/shard_map/ppermute | solution.py:769
  46.2 24.7 %collective-permute-start.2 = (bf16[1,512,1024]{2,1,0:T(8,128)(2,1)}, bf16[1,512,1024]{2,1,0:T(8,128)(2,1)S(1)}, u32[]{:S(2)}, u32[]{:S(2)}) collective-permute-start(bf16[1,512,1024]{2,1,0:T(8,128)(2,1)} %constant_dynamic-slice_fusion.3), channel_id=1, source_target_pairs={{0,1},{1,0},{2,3},{3,2},{4,5},{5,4},{6,7},{7,6},{8,9},{9,8},{10,11... | collective-permute-start | bytes 3145736 | tf_op jit(solution)/shard_map/ppermute | solution.py:769
  48.3 62.9 %copy-start.18 = (bf16[1024,1024]{1,0:T(8,128)(2,1)}, bf16[1024,1024]{1,0:T(8,128)(2,1)S(1)}, u32[]{:S(2)}) copy-start(bf16[1024,1024]{1,0:T(8,128)(2,1)S(1)} %maximum_bitcast_fusion.x.refs_0_) | copy-start | bytes 6291460
  48.4 22.5 %copy-start.26 = (bf16[2,512,1024]{2,1,0:T(8,128)(2,1)S(1)}, bf16[2,512,1024]{2,1,0:T(8,128)(2,1)}, u32[]{:S(2)}) copy-start(bf16[2,512,1024]{2,1,0:T(8,128)(2,1)} %param.16) | copy-start | bytes 6291460
  52.1 69.1 %copy-start.7 = (bf16[1024,128]{1,0:T(8,128)(2,1)}, bf16[1024,128]{1,0:T(8,128)(2,1)S(1)}, u32[]{:S(2)}) copy-start(bf16[1024,128]{1,0:T(8,128)(2,1)S(1)} %get-tuple-element.458.fk_ref) | copy-start | bytes 786436
  121.2 21.7 %slice-start = ((bf16[1024,8320]{1,0:T(8,128)(2,1)}), bf16[1024,3]{1,0:T(8,128)(2,1)S(1)}, s32[]{:S(2)}) async-start(bf16[1024,8320]{1,0:T(8,128)(2,1)} %all-gather.4.cloned.1.call-done.out_w.cross_w), calls=%async_computation.6 | async-start | bytes 524288 | tf_op jit(solution)/shard_map/slice | solution.py:1318
  155.5 39.7 %collective-permute-start.3 = (bf16[1,512,1024]{2,1,0:T(8,128)(2,1)}, bf16[1,512,1024]{2,1,0:T(8,128)(2,1)}, u32[]{:S(2)}, u32[]{:S(2)}) collective-permute-start(bf16[1,512,1024]{2,1,0:T(8,128)(2,1)} %constant_dynamic-slice_fusion.2), channel_id=1, source_target_pairs={{0,1},{1,0},{2,3},{3,2},{4,5},{5,4},{6,7},{7,6},{8,9},{9,8},{10,11... | collective-permute-start | bytes 3145736 | tf_op jit(solution)/shard_map/ppermute | solution.py:769
  264.3 315.0 %reduce-scatter.5.cloned.1.call-start = ((), (), s32[]{:S(2)}) async-start(), calls=%async_computation.4 | async-start | bytes 11419648 | tf_op jit(solution)/shard_map/reduce_scatter | solution.py:1145
  296.2 21.2 %collective-permute-start.4 = (bf16[1024,2048]{1,0:T(8,128)(2,1)}, bf16[1024,2048]{1,0:T(8,128)(2,1)}, u32[]{:S(2)}, u32[]{:S(2)}) collective-permute-start(bf16[1024,2048]{1,0:T(8,128)(2,1)} %get-tuple-element.217), channel_id=1, source_target_pairs={{0,2},{2,0},{4,6},{6,4},{8,10},{10,8},{12,14},{14,12},{16,18},{18,... | collective-permute-start | bytes 12582920 | tf_op jit(solution)/shard_map/ppermute | solution.py:869
  296.3 21.1 %copy-start.21 = (bf16[1024,2048]{1,0:T(8,128)(2,1)S(1)}, bf16[1024,2048]{1,0:T(8,128)(2,1)}, u32[]{:S(2)}) copy-start(bf16[1024,2048]{1,0:T(8,128)(2,1)} %get-tuple-element.220) | copy-start | bytes 12582916
  321.3 68.0 %collective-permute-start.6 = (bf16[4,1,128,2048]{3,2,1,0:T(8,128)(2,1)}, bf16[4,1,128,2048]{3,2,1,0:T(8,128)(2,1)}, u32[]{:S(2)}, u32[]{:S(2)}) collective-permute-start(bf16[4,1,128,2048]{3,2,1,0:T(8,128)(2,1)} %add_convert_fusion), channel_id=1, source_target_pairs={{0,4},{2,6},{4,0},{6,2},{8,12},{10,14},{12,8},{14,10},{16,20},{18,... | collective-permute-start | bytes 6291464 | tf_op jit(solution)/shard_map/ppermute | solution.py:873
  322.4 52.7 %collective-permute-start.5 = (bf16[1,512,1024]{2,1,0:T(8,128)(2,1)}, bf16[1,512,1024]{2,1,0:T(8,128)(2,1)}, u32[]{:S(2)}, u32[]{:S(2)}) collective-permute-start(bf16[1,512,1024]{2,1,0:T(8,128)(2,1)} %dynamic-slice_bitcast_fusion), channel_id=1, source_target_pairs={{0,1},{1,0},{2,3},{3,2},{4,5},{5,4},{6,7},{7,6},{8,9},{9,8},{10,11... | collective-permute-start | bytes 3145736 | tf_op jit(solution)/shard_map/ppermute | solution.py:769
  408.9 24.9 %collective-permute-start.7 = (bf16[4,1,128,1024]{3,2,1,0:T(8,128)(2,1)S(1)}, bf16[4,1,128,1024]{3,2,1,0:T(8,128)(2,1)}, u32[]{:S(2)}, u32[]{:S(2)}) collective-permute-start(bf16[4,1,128,1024]{3,2,1,0:T(8,128)(2,1)S(1)} %add_convert_fusion.1), channel_id=1, source_target_pairs={{0,1},{1,0},{2,3},{3,2},{4,5},{5,4},{6,7},{7,6},{8,9},{9,8},{10,11... | collective-permute-start | bytes 3145736 | tf_op jit(solution)/shard_map/ppermute | solution.py:769
  437.9 45.7 %collective-permute-start.12 = (bf16[1,512,1024]{2,1,0:T(8,128)(2,1)}, bf16[1,512,1024]{2,1,0:T(8,128)(2,1)}, u32[]{:S(2)}, u32[]{:S(2)}) collective-permute-start(bf16[1,512,1024]{2,1,0:T(8,128)(2,1)} %fusion.27), channel_id=1, source_target_pairs={{0,1},{1,0},{2,3},{3,2},{4,5},{5,4},{6,7},{7,6},{8,9},{9,8},{10,11... | collective-permute-start | bytes 3145736 | tf_op jit(solution)/shard_map/ppermute | solution.py:769
  439.3 35.0 %collective-permute-start.11 = (bf16[256,1024]{1,0:T(8,128)(2,1)}, bf16[256,1024]{1,0:T(8,128)(2,1)}, u32[]{:S(2)}, u32[]{:S(2)}) collective-permute-start(bf16[256,1024]{1,0:T(8,128)(2,1)} %reduce-scatter.3.cloned.1.call-done), channel_id=1, source_target_pairs={{0,1},{1,0},{2,3},{3,2},{4,5},{5,4},{6,7},{7,6},{8,9},{9,8},{10,11... | collective-permute-start | bytes 1572872 | tf_op jit(solution)/shard_map/ppermute | solution.py:769
  439.9 24.3 %collective-permute-start.8 = (bf16[1,1,128,1024]{3,2,1,0:T(8,128)(2,1)}, bf16[1,1,128,1024]{3,2,1,0:T(8,128)(2,1)}, u32[]{:S(2)}, u32[]{:S(2)}) collective-permute-start(bf16[1,1,128,1024]{3,2,1,0:T(8,128)(2,1)} %get-tuple-element.264), channel_id=1, source_target_pairs={{0,8},{2,10},{4,12},{6,14},{8,16},{10,18},{12,20},{14,22},{16,24},... | collective-permute-start | bytes 786440 | tf_op jit(solution)/shard_map/ppermute | solution.py:877
  441.6 31.4 %collective-permute-start.9 = (bf16[1,1,128,1024]{3,2,1,0:T(8,128)(2,1)}, bf16[1,1,128,1024]{3,2,1,0:T(8,128)(2,1)}, u32[]{:S(2)}, u32[]{:S(2)}) collective-permute-start(bf16[1,1,128,1024]{3,2,1,0:T(8,128)(2,1)} %get-tuple-element.265), channel_id=1, source_target_pairs={{0,16},{2,18},{4,20},{6,22},{8,24},{10,26},{12,28},{14,30},{16,0},... | collective-permute-start | bytes 786440 | tf_op jit(solution)/shard_map/ppermute | solution.py:877
  443.8 30.6 %collective-permute-start.10 = (bf16[1,1,128,1024]{3,2,1,0:T(8,128)(2,1)}, bf16[1,1,128,1024]{3,2,1,0:T(8,128)(2,1)}, u32[]{:S(2)}, u32[]{:S(2)}) collective-permute-start(bf16[1,1,128,1024]{3,2,1,0:T(8,128)(2,1)} %get-tuple-element.266), channel_id=1, source_target_pairs={{0,24},{2,26},{4,28},{6,30},{8,0},{10,2},{12,4},{14,6},{16,8},{18,... | collective-permute-start | bytes 786440 | tf_op jit(solution)/shard_map/ppermute | solution.py:877
  464.3 19.3 %copy-start.13 = (bf16[1024,512]{1,0:T(8,128)(2,1)}, bf16[1024,512]{1,0:T(8,128)(2,1)S(1)}, u32[]{:S(2)}) copy-start(bf16[1024,512]{1,0:T(8,128)(2,1)S(1)} %get-tuple-element.277.refs_2_) | copy-start | bytes 3145732
  464.3 19.3 %copy-start.15 = (bf16[1024,512]{1,0:T(8,128)(2,1)}, bf16[1024,512]{1,0:T(8,128)(2,1)S(1)}, u32[]{:S(2)}) copy-start(bf16[1024,512]{1,0:T(8,128)(2,1)S(1)} %get-tuple-element.274.refs_1_) | copy-start | bytes 3145732
  483.6 24.0 %collective-permute-start.13 = (bf16[1024,768]{1,0:T(8,128)(2,1)}, bf16[1024,768]{1,0:T(8,128)(2,1)}, u32[]{:S(2)}, u32[]{:S(2)}) collective-permute-start(bf16[1024,768]{1,0:T(8,128)(2,1)} %get-tuple-element.284), channel_id=1, source_target_pairs={{0,2},{2,0},{4,6},{6,4},{8,10},{10,8},{12,14},{14,12},{16,18},{18,... | collective-permute-start | bytes 4718600 | tf_op jit(solution)/shard_map/ppermute | solution.py:869
  485.4 22.1 %collective-permute-start.14 = (bf16[64,1024]{1,0:T(8,128)(2,1)S(1)}, bf16[64,1024]{1,0:T(8,128)(2,1)S(1)}, u32[]{:S(2)}, u32[]{:S(2)}) collective-permute-start(bf16[64,1024]{1,0:T(8,128)(2,1)S(1)} %get-tuple-element.285), channel_id=1, source_target_pairs={{0,1},{1,0},{2,3},{3,2},{4,5},{5,4},{6,7},{7,6},{8,9},{9,8},{10,11... | collective-permute-start | bytes 393224 | tf_op jit(solution)/shard_map/ppermute | solution.py:769
  486.9 20.6 %collective-permute-start.15 = (bf16[64,1024]{1,0:T(8,128)(2,1)S(1)}, bf16[64,1024]{1,0:T(8,128)(2,1)S(1)}, u32[]{:S(2)}, u32[]{:S(2)}) collective-permute-start(bf16[64,1024]{1,0:T(8,128)(2,1)S(1)} %copy-done.45), channel_id=1, source_target_pairs={{0,2},{2,0},{4,6},{6,4},{8,10},{10,8},{12,14},{14,12},{16,18},{18,... | collective-permute-start | bytes 393224 | tf_op jit(solution)/shard_map/ppermute | solution.py:869
  487.0 20.5 %collective-permute-start.16 = (bf16[64,1024]{1,0:T(8,128)(2,1)S(1)}, bf16[64,1024]{1,0:T(8,128)(2,1)S(1)}, u32[]{:S(2)}, u32[]{:S(2)}) collective-permute-start(bf16[64,1024]{1,0:T(8,128)(2,1)S(1)} %copy-done.45), channel_id=1, source_target_pairs={{0,3},{1,2},{2,1},{3,0},{4,7},{5,6},{6,5},{7,4},{8,11},{9,10},{10,... | collective-permute-start | bytes 393224 | tf_op jit(solution)/shard_map/ppermute | solution.py:882
  510.0 25.7 %collective-permute-start.17 = (bf16[4,1,128,768]{3,2,1,0:T(8,128)(2,1)}, bf16[4,1,128,768]{3,2,1,0:T(8,128)(2,1)}, u32[]{:S(2)}, u32[]{:S(2)}) collective-permute-start(bf16[4,1,128,768]{3,2,1,0:T(8,128)(2,1)} %add_convert_fusion.3), channel_id=1, source_target_pairs={{0,4},{2,6},{4,0},{6,2},{8,12},{10,14},{12,8},{14,10},{16,20},{18,... | collective-permute-start | bytes 2359304 | tf_op jit(solution)/shard_map/ppermute | solution.py:873
  537.3 4.4 collective-permute-start.18
  539.7 38.8 %collective-permute-start.23 = (bf16[1,512,1024]{2,1,0:T(8,128)(2,1)S(1)}, bf16[1,512,1024]{2,1,0:T(8,128)(2,1)S(1)}, u32[]{:S(2)}, u32[]{:S(2)}) collective-permute-start(bf16[1,512,1024]{2,1,0:T(8,128)(2,1)S(1)} %fusion.28), channel_id=1, source_target_pairs={{0,1},{1,0},{2,3},{3,2},{4,5},{5,4},{6,7},{7,6},{8,9},{9,8},{10,11... | collective-permute-start | bytes 3145736 | tf_op jit(solution)/shard_map/ppermute | solution.py:769
  541.7 24.4 %copy-start.31 = (bf16[1024,768]{1,0:T(8,128)(2,1)}, bf16[1024,768]{1,0:T(8,128)(2,1)S(1)}, u32[]{:S(2)}) copy-start(bf16[1024,768]{1,0:T(8,128)(2,1)S(1)} %collective-permute-done.18) | copy-start | bytes 4718596
  541.9 37.3 %collective-permute-start.19 = (bf16[4,1,128,768]{3,2,1,0:T(8,128)(2,1)S(1)}, bf16[4,1,128,768]{3,2,1,0:T(8,128)(2,1)S(1)}, u32[]{:S(2)}, u32[]{:S(2)}) collective-permute-start(bf16[4,1,128,768]{3,2,1,0:T(8,128)(2,1)S(1)} %add_convert_fusion.2), channel_id=1, source_target_pairs={{0,4},{2,6},{4,0},{6,2},{8,12},{10,14},{12,8},{14,10},{16,20},{18,... | collective-permute-start | bytes 2359304 | tf_op jit(solution)/shard_map/ppermute | solution.py:873
  543.2 27.5 %collective-permute-start.20 = (bf16[1,1,128,768]{3,2,1,0:T(8,128)(2,1)S(1)}, bf16[1,1,128,768]{3,2,1,0:T(8,128)(2,1)S(1)}, u32[]{:S(2)}, u32[]{:S(2)}) collective-permute-start(bf16[1,1,128,768]{3,2,1,0:T(8,128)(2,1)S(1)} %get-tuple-element.307), channel_id=1, source_target_pairs={{0,8},{2,10},{4,12},{6,14},{8,16},{10,18},{12,20},{14,22},{16,24},... | collective-permute-start | bytes 589832 | tf_op jit(solution)/shard_map/ppermute | solution.py:877
  563.6 14.9 %collective-permute-start.21 = (bf16[1,1,128,768]{3,2,1,0:T(8,128)(2,1)S(1)}, bf16[1,1,128,768]{3,2,1,0:T(8,128)(2,1)S(1)}, u32[]{:S(2)}, u32[]{:S(2)}) collective-permute-start(bf16[1,1,128,768]{3,2,1,0:T(8,128)(2,1)S(1)} %get-tuple-element.308), channel_id=1, source_target_pairs={{0,16},{2,18},{4,20},{6,22},{8,24},{10,26},{12,28},{14,30},{16,0},... | collective-permute-start | bytes 589832 | tf_op jit(solution)/shard_map/ppermute | solution.py:877
  565.5 13.0 %collective-permute-start.22 = (bf16[1,1,128,768]{3,2,1,0:T(8,128)(2,1)S(1)}, bf16[1,1,128,768]{3,2,1,0:T(8,128)(2,1)S(1)}, u32[]{:S(2)}, u32[]{:S(2)}) collective-permute-start(bf16[1,1,128,768]{3,2,1,0:T(8,128)(2,1)S(1)} %get-tuple-element.309), channel_id=1, source_target_pairs={{0,24},{2,26},{4,28},{6,30},{8,0},{10,2},{12,4},{14,6},{16,8},{18,... | collective-permute-start | bytes 589832 | tf_op jit(solution)/shard_map/ppermute | solution.py:877
  582.4 20.8 %collective-permute-start.27 = (bf16[1,1,128,384]{3,2,1,0:T(8,128)(2,1)S(1)}, bf16[1,1,128,384]{3,2,1,0:T(8,128)(2,1)S(1)}, u32[]{:S(2)}, u32[]{:S(2)}) collective-permute-start(bf16[1,1,128,384]{3,2,1,0:T(8,128)(2,1)S(1)} %add_convert_fusion.17), channel_id=1, source_target_pairs={{0,1},{1,0},{2,3},{3,2},{4,5},{5,4},{6,7},{7,6},{8,9},{9,8},{10,11... | collective-permute-start | bytes 294920 | tf_op jit(solution)/shard_map/ppermute | solution.py:769
  583.9 19.3 %collective-permute-start.24 = (bf16[1,1,128,768]{3,2,1,0:T(8,128)(2,1)S(1)}, bf16[1,1,128,768]{3,2,1,0:T(8,128)(2,1)S(1)}, u32[]{:S(2)}, u32[]{:S(2)}) collective-permute-start(bf16[1,1,128,768]{3,2,1,0:T(8,128)(2,1)S(1)} %get-tuple-element.319), channel_id=1, source_target_pairs={{0,8},{2,10},{4,12},{6,14},{8,16},{10,18},{12,20},{14,22},{16,24},... | collective-permute-start | bytes 589832 | tf_op jit(solution)/shard_map/ppermute | solution.py:877
  591.0 14.2 %collective-permute-start.25 = (bf16[1,1,128,768]{3,2,1,0:T(8,128)(2,1)S(1)}, bf16[1,1,128,768]{3,2,1,0:T(8,128)(2,1)S(1)}, u32[]{:S(2)}, u32[]{:S(2)}) collective-permute-start(bf16[1,1,128,768]{3,2,1,0:T(8,128)(2,1)S(1)} %get-tuple-element.320), channel_id=1, source_target_pairs={{0,16},{2,18},{4,20},{6,22},{8,24},{10,26},{12,28},{14,30},{16,0},... | collective-permute-start | bytes 589832 | tf_op jit(solution)/shard_map/ppermute | solution.py:877
  592.8 12.4 %collective-permute-start.26 = (bf16[1,1,128,768]{3,2,1,0:T(8,128)(2,1)S(1)}, bf16[1,1,128,768]{3,2,1,0:T(8,128)(2,1)S(1)}, u32[]{:S(2)}, u32[]{:S(2)}) collective-permute-start(bf16[1,1,128,768]{3,2,1,0:T(8,128)(2,1)S(1)} %get-tuple-element.321), channel_id=1, source_target_pairs={{0,24},{2,26},{4,28},{6,30},{8,0},{10,2},{12,4},{14,6},{16,8},{18,... | collective-permute-start | bytes 589832 | tf_op jit(solution)/shard_map/ppermute | solution.py:877
  593.5 15.9 %collective-permute-start.28 = (bf16[64,5248]{1,0:T(8,128)(2,1)S(1)}, bf16[64,5248]{1,0:T(8,128)(2,1)S(1)}, u32[]{:S(2)}, u32[]{:S(2)}) collective-permute-start(bf16[64,5248]{1,0:T(8,128)(2,1)S(1)} %copy-done.34), channel_id=1, source_target_pairs={{0,1},{1,0},{2,3},{3,2},{4,5},{5,4},{6,7},{7,6},{8,9},{9,8},{10,11... | collective-permute-start | bytes 2015240 | tf_op jit(solution)/shard_map/ppermute | solution.py:769
  611.8 6.6 %collective-permute-start.30 = (bf16[64,384]{1,0:T(8,128)(2,1)S(1)}, bf16[64,384]{1,0:T(8,128)(2,1)S(1)}, u32[]{:S(2)}, u32[]{:S(2)}) collective-permute-start(bf16[64,384]{1,0:T(8,128)(2,1)S(1)} %get-tuple-element.329), channel_id=1, source_target_pairs={{0,1},{1,0},{2,3},{3,2},{4,5},{5,4},{6,7},{7,6},{8,9},{9,8},{10,11... | collective-permute-start | bytes 147464 | tf_op jit(solution)/shard_map/ppermute | solution.py:769
  612.3 6.2 collective-permute-start.31
  612.3 6.2 collective-permute-start.32
  614.0 5.0 collective-permute-start.29
  620.3 4.2 collective-permute-start.33
  621.4 3.1 collective-permute-start.34
  621.4 3.5 collective-permute-start.35
  (51 other events, 316.7 us)
Sparse Core Ops, SparseCore 0:
  12.8 93.0 all-gather.3
  107.4 90.2 all-gather.5
  264.4 119.7 reduce-scatter.2
  409.0 155.1 reduce-scatter.4
